TPU v7x, 512 devices: a whole 4x4x16 slice. The times are simulated.
512 devices in a mesh: section: 16 (over z_hi, y, core), tensor: 32 (over z_lo, x).
Axes of the slice: x: 4, y: 4, z: 16 (z_hi: 2, z_lo: 8; z = z_hi * 8 + z_lo), core: 2. Of those that a mesh axis runs over, the one named last changes fastest.
Arguments:
- encoded: bfloat16 [16, 256, 8192], P(None, 'section', 'tensor'), may hold values from -6 to 6
- w_key: bfloat16 [16, 8192, 4096], P('section', None, 'tensor'), may hold values from -0.125 to 0.125
- w_value: bfloat16 [16, 8192, 4096], P('section', None, 'tensor'), may hold values from -0.0625 to 0.0625
- queries: bfloat16 [16, 64, 4096], P('section', None, 'tensor'), may hold values from -6 to 6
- cotangent: bfloat16 [16, 64, 4096], P('section', None, 'tensor'), may hold values from -96 to 96
- counts: int32 [16, 1], P('section'), may hold values from 0 to 2
Outputs:
- grad_query: bfloat16 [16, 64, 4096], P('section', None, 'tensor')
- grad_encoded: float32 [16, 256, 8192], P(None, 'section', 'tensor')
All inputs are finite; a program needn't handle non-finite values.
Results may differ from a plain program's by a relative error of at most 0.03.
Values may be sent and summed in bfloat16 or wider, within the bound.
No kernel may reach another device: no remote copies, remote signals or barrier semaphores. Data moves between devices by JAX's collectives and lax.ppermute only.
A program may use at most 64 MiB of HBM per device.

v0:
```python
import math

import jax
import jax.numpy as jnp
from jax import lax
from jax.sharding import PartitionSpec as P

GROUP = 64
NBR_LEN = 128
NBRS = 2


def attention_backward(query_block, grad_block, key_rows, value_rows, live_mask, no_neighbours):
    group_count = query_block.shape[0]
    width_head = query_block.shape[2]
    inverse_root = 1.0 / math.sqrt(width_head)
    key_blocks = key_rows.reshape(group_count, -1, width_head)
    value_blocks = value_rows.reshape(group_count, -1, width_head)
    scores = (
        jnp.einsum("cqd,ckd->cqk", query_block, key_blocks, preferred_element_type=jnp.float32)
        * inverse_root
    )
    weighted = jnp.where(live_mask[:, None, :] > 0.5, jnp.exp(scores), 0.0)
    totals = jnp.sum(weighted, axis=2, keepdims=True) + no_neighbours[:, None, None]
    probs = weighted / totals
    probs_low = probs.astype(jnp.bfloat16)
    grad_values = jnp.einsum(
        "cqk,cqd->ckd", probs_low, grad_block, preferred_element_type=jnp.float32
    ).astype(jnp.bfloat16)
    grad_probs = jnp.einsum(
        "cqd,ckd->cqk", grad_block, value_blocks, preferred_element_type=jnp.float32
    )
    centre = jnp.sum(probs * grad_probs, axis=2, keepdims=True)
    grad_scores = (probs * (grad_probs - centre)).astype(jnp.bfloat16)
    grad_queries = (
        jnp.einsum("cqk,ckd->cqd", grad_scores, key_blocks, preferred_element_type=jnp.float32)
        * inverse_root
    ).astype(jnp.bfloat16)
    grad_keys = (
        jnp.einsum("cqk,cqd->ckd", grad_scores, query_block, preferred_element_type=jnp.float32)
        * inverse_root
    ).astype(jnp.bfloat16)
    return (grad_queries, grad_keys, grad_values)


def local(encoded, w_key, w_value, queries, cotangent, counts):
    key_weight = w_key[0]
    value_weight = w_value[0]
    width_head = key_weight.shape[1]
    group_count = counts.shape[1]
    whole_rows = lax.all_gather(encoded, "tensor", axis=2, tiled=True)
    own_rows = lax.all_to_all(whole_rows, "section", split_axis=0, concat_axis=1, tiled=True)[0]
    key_total = jnp.dot(own_rows, key_weight, preferred_element_type=jnp.float32)
    value_total = jnp.dot(own_rows, value_weight, preferred_element_type=jnp.float32)
    key_rows = key_total.astype(jnp.bfloat16)
    value_rows = value_total.astype(jnp.bfloat16)
    slot_index = jnp.arange(NBRS * NBR_LEN, dtype=jnp.int32) // NBR_LEN
    own_counts = counts[0]
    live_mask = (slot_index[None, :] < own_counts[:, None]).astype(jnp.float32)
    no_neighbours = (own_counts == 0).astype(jnp.float32)
    query_block = queries[0].reshape(group_count, GROUP, width_head)
    grad_block = cotangent[0].reshape(group_count, GROUP, width_head)
    grad_queries, grad_keys, grad_values = attention_backward(
        query_block, grad_block, key_rows, value_rows, live_mask, no_neighbours
    )
    key_grads = grad_keys.reshape(-1, width_head)
    value_grads = grad_values.reshape(-1, width_head)
    head_term = jnp.dot(key_grads, key_weight.T, preferred_element_type=jnp.float32)
    head_term = head_term + jnp.dot(value_grads, value_weight.T, preferred_element_type=jnp.float32)
    summed = lax.psum_scatter(
        head_term.astype(jnp.bfloat16), "tensor", scatter_dimension=1, tiled=True
    ).astype(jnp.float32)
    returned = lax.all_to_all(
        summed[None].astype(jnp.bfloat16), "section", split_axis=1, concat_axis=0, tiled=True
    ).astype(jnp.float32)
    return (grad_queries, returned)


def solution(mesh):
    return jax.shard_map(
        local,
        mesh=mesh,
        in_specs=(
            P(None, "section", "tensor"),
            P("section", None, "tensor"),
            P("section", None, "tensor"),
            P("section", None, "tensor"),
            P("section", None, "tensor"),
            P("section", None),
        ),
        out_specs=(P("section", None, "tensor"), P(None, "section", "tensor")),
        check_vma=False,
    )
```

profile of v0, /device:TPU:1, one launch (start us, length us, event | category | flops | bytes accessed | tf_op | source)
XLA Modules:
  0.0 713.1 jit_solution(10552674481134932043)
XLA Ops:
  7.2 0.0 copy-start
  7.2 0.0 all-gather.2.cloned.1.call-start
  7.2 0.7 all-gather.2.cloned.1.call-update
  7.9 183.1 %all-gather.2.cloned.1.call-done = bf16[16,16,8192]{2,1,0:T(8,128)(2,1)} async-done(((bf16[16,16,256]{2,1,0:T(8,128)(2,1)}), bf16[16,16,8192]{2,1,0:T(8,128)(2,1)}) %all-gather.2.cloned.1.call-update) | async-done | bytes 4194320 | tf_op jit(solution)/shard_map/all_gather | solution.py:51
  191.0 23.2 %all-to-all-start = ((bf16[16,16,8192]{2,1,0:T(8,128)(2,1)}), bf16[16,16,8192]{2,1,0:T(8,128)(2,1)}, u32[]{:S(2)}, u32[]{:S(2)}) async-start(bf16[16,16,8192]{2,1,0:T(8,128)(2,1)} %all-gather.2.cloned.1.call-done), calls=%async_computation | async-start | bytes 8388608 | tf_op jit(solution)/shard_map/all_to_all | solution.py:52
  214.2 0.0 copy-start.2
  214.2 0.0 copy-start.1
  214.2 0.0 reduce-scatter.2.cloned.1.call-start
  214.9 151.7 %all-to-all-done = bf16[16,16,8192]{2,1,0:T(8,128)(2,1)} async-done(((bf16[16,16,8192]{2,1,0:T(8,128)(2,1)}), bf16[16,16,8192]{2,1,0:T(8,128)(2,1)}, u32[]{:S(2)}, u32[]{:S(2)}) %all-to-all-start) | async-done | bytes 4194336 | tf_op jit(solution)/shard_map/all_to_all | solution.py:52
  366.6 0.0 copy-done
  366.6 3.4 fusion.8
  370.1 0.0 copy-done.2
  370.1 0.3 fusion.32
  370.3 0.0 copy-done.1
  370.4 4.3 fusion.21
  374.7 0.1 fusion.22
  374.8 4.6 fusion.4
  379.4 7.4 %fusion = bf16[256,8192]{1,0:T(8,128)(2,1)} fusion(f32[256,8192]{1,0:T(8,128)} %fusion.4, bf16[1,8192,128]{2,1,0:T(8,128)(2,1)} %param.8, bf16[1,64,128]{2,1,0:T(8,128)(2,1)S(1)} %copy-done.1, f32[256,64]{0,1:T(8,128)S(1)} %get-tuple-element.3, f32[64]{0:T(128)S(1)} %broadcast_add_fusion), kind=kOutput, calls=%fused_computation.1 | convolution fusion | flops 545325056 | bytes 14762240 | tf_op jit(solution)/shard_map/dot_general | solution.py:69
  386.9 0.0 reduce-scatter.2.cloned.1.call-update
  386.9 264.2 %reduce-scatter.2.cloned.1.call-done = bf16[256,256]{1,0:T(8,128)(2,1)} async-done(((bf16[256,8192]{1,0:T(8,128)(2,1)}), bf16[256,256]{1,0:T(8,128)(2,1)}) %reduce-scatter.2.cloned.1.call-update) | async-done | bytes 131088 | tf_op jit(solution)/shard_map/reduce_scatter | solution.py:70
  651.1 1.1 copy.11
  652.2 0.5 broadcast.79
  652.7 1.4 reduce.5
  654.1 0.7 reshape.110
  654.8 35.8 %all-to-all-start.1 = ((bf16[16,2,2048]{2,1,0:T(2,128)(2,1)}), bf16[16,2,2048]{2,1,0:T(2,128)(2,1)S(1)}, u32[]{:S(2)}, u32[]{:S(2)}) async-start(bf16[16,2,2048]{2,1,0:T(2,128)(2,1)} %reshape.110), calls=%async_computation.2 | async-start | bytes 262144 | tf_op jit(solution)/shard_map/all_to_all | solution.py:73
  690.5 0.7 fusion.20
  691.3 14.1 %all-to-all-done.1 = bf16[16,2,2048]{2,1,0:T(2,128)(2,1)S(1)} async-done(((bf16[16,2,2048]{2,1,0:T(2,128)(2,1)}), bf16[16,2,2048]{2,1,0:T(2,128)(2,1)S(1)}, u32[]{:S(2)}, u32[]{:S(2)}) %all-to-all-start.1) | async-done | bytes 131104 | tf_op jit(solution)/shard_map/all_to_all | solution.py:73
  705.4 0.1 reshape.111
  705.5 0.7 copy.9
  (2 shorter events, 0.0 us)
Async XLA Ops:
  7.2 359.5 %copy-start = (bf16[1,8192,128]{2,1,0:T(8,128)(2,1)S(1)}, bf16[1,8192,128]{2,1,0:T(8,128)(2,1)}, u32[]{:S(2)}) copy-start(bf16[1,8192,128]{2,1,0:T(8,128)(2,1)} %param.7) | copy-start | bytes 6291460
  7.2 183.9 %all-gather.2.cloned.1.call-start = ((), (), s32[]{:S(2)}) async-start(), calls=%async_computation.3 | async-start | bytes 4325376 | tf_op jit(solution)/shard_map/all_gather | solution.py:51
  191.0 175.6 %all-to-all-start = ((bf16[16,16,8192]{2,1,0:T(8,128)(2,1)}), bf16[16,16,8192]{2,1,0:T(8,128)(2,1)}, u32[]{:S(2)}, u32[]{:S(2)}) async-start(bf16[16,16,8192]{2,1,0:T(8,128)(2,1)} %all-gather.2.cloned.1.call-done), calls=%async_computation | async-start | bytes 8388608 | tf_op jit(solution)/shard_map/all_to_all | solution.py:52
  214.2 155.9 %copy-start.2 = (bf16[1,64,128]{2,1,0:T(8,128)(2,1)S(1)}, bf16[1,64,128]{2,1,0:T(8,128)(2,1)}, u32[]{:S(2)}) copy-start(bf16[1,64,128]{2,1,0:T(8,128)(2,1)} %param.9) | copy-start | bytes 49156
  214.2 156.2 %copy-start.1 = (bf16[1,64,128]{2,1,0:T(8,128)(2,1)S(1)}, bf16[1,64,128]{2,1,0:T(8,128)(2,1)}, u32[]{:S(2)}) copy-start(bf16[1,64,128]{2,1,0:T(8,128)(2,1)} %param.10) | copy-start | bytes 49156
  214.2 436.8 %reduce-scatter.2.cloned.1.call-start = ((), (), s32[]{:S(2)}) async-start(), calls=%async_computation.4 | async-start | bytes 4325376 | tf_op jit(solution)/shard_map/reduce_scatter | solution.py:70
  654.8 50.6 %all-to-all-start.1 = ((bf16[16,2,2048]{2,1,0:T(2,128)(2,1)}), bf16[16,2,2048]{2,1,0:T(2,128)(2,1)S(1)}, u32[]{:S(2)}, u32[]{:S(2)}) async-start(bf16[16,2,2048]{2,1,0:T(2,128)(2,1)} %reshape.110), calls=%async_computation.2 | async-start | bytes 262144 | tf_op jit(solution)/shard_map/all_to_all | solution.py:73
Sparse Core Ops, SparseCore 0:
  10.0 180.9 all-gather.1
  387.0 263.9 reduce-scatter.1
where the time goes:
time: 713 us
  waiting for transfers between devices  614 us (86%)
  starting transfers between devices  59 us (8%)
  matrix products  20.8 us (3%)
  between operations  14.8 us (2%)
    reduce_scatter x1, waiting for transfers between devices, local(): lax.psum_scatter(head_term.astype(jnp.bfloat16), 'tensor', scatter_dimens...  264 us
    all_gather x1, waiting for transfers between devices, local(): whole_rows = lax.all_gather(encoded, 'tensor', axis=2, tiled=True)  183 us
    all_to_all x1, waiting for transfers between devices, local(): lax.all_to_all(whole_rows, 'section', split_axis=0, concat_axis=1, tiled=...  152 us
    all_to_all x1, starting transfers between devices, local(): lax.all_to_all(summed[None].astype(jnp.bfloat16), 'section', split_axis=1...  35.8 us
    all_to_all x1, starting transfers between devices, local(): lax.all_to_all(whole_rows, 'section', split_axis=0, concat_axis=1, tiled=...  23.2 us
  transfers between devices with their start and end apart: 4, of which 4 were waited for; matrix products, arithmetic and copies ran while one was open for 0% of the time, Pallas kernels for 0%

commit v1 on v0

v1 whole, which is shorter than its diff:
```python
import math

import jax
import jax.numpy as jnp
from jax import lax
from jax.experimental import pallas as pl
from jax.experimental.pallas import tpu as pltpu
from jax.sharding import Mesh, PartitionSpec as P

NBR_LEN = 128
HEAD = 128
GROUP = 64
BLOCK = 256
INV = 1.0 / math.sqrt(HEAD)
F32 = jnp.float32
BF16 = jnp.bfloat16

SECTION = ("zh", "y", "c")
TENSOR = ("z4", "z2", "x")
TEAM = ("z2", "x")
SPREAD = ("zh", "y", "c", "z4")


def nt(a, b):
    return lax.dot_general(a, b, (((1,), (1,)), ((), ())), preferred_element_type=F32)


def project_kernel(q_ref, ct_ref, wk_ref, wv_ref, out_ref):
    for d in range(out_ref.shape[0]):
        for a in range(wk_ref.shape[0]):
            cols = pl.ds(a * BLOCK, BLOCK)
            out_ref[d, 0:GROUP, cols] = nt(q_ref[...], wk_ref[a, d]).astype(BF16)
            out_ref[d, GROUP : 2 * GROUP, cols] = nt(ct_ref[...], wv_ref[a, d]).astype(BF16)


def project(q, ct, wk, wv):
    per = 2
    w_spec = pl.BlockSpec((4, per, BLOCK, HEAD), lambda i: (0, i, 0, 0))
    small = pl.BlockSpec((GROUP, HEAD), lambda i: (0, 0))
    return pl.pallas_call(
        project_kernel,
        grid=(8 // per,),
        in_specs=[small, small, w_spec, w_spec],
        out_specs=pl.BlockSpec((per, 2 * GROUP, 4 * BLOCK), lambda i: (i, 0, 0)),
        out_shape=jax.ShapeDtypeStruct((8, 2 * GROUP, 4 * BLOCK), BF16),
        cost_estimate=pl.CostEstimate(
            flops=2 * 128 * 8192 * 128, bytes_accessed=6 << 20, transcendentals=0
        ),
    )(q, ct, wk.reshape(4, 8, BLOCK, HEAD), wv.reshape(4, 8, BLOCK, HEAD))


def score_kernel(a_ref, e_ref, out_ref):
    total = None
    rows = a_ref.shape[0] * a_ref.shape[1]
    for b in range(4):
        part = nt(
            a_ref[:, :, b * BLOCK : (b + 1) * BLOCK].reshape(rows, BLOCK),
            e_ref[:, b].reshape(256, BLOCK),
        )
        total = part if total is None else total + part
    out_ref[...] = total.astype(BF16).reshape(out_ref.shape)


def score(a, e):
    per = 2
    return pl.pallas_call(
        score_kernel,
        grid=(8 // per,),
        in_specs=[
            pl.BlockSpec((per, 2 * GROUP, 4 * BLOCK), lambda i: (i, 0, 0)),
            pl.BlockSpec((16, 4, 16, BLOCK), lambda i: (0, 0, 0, 0)),
        ],
        out_specs=pl.BlockSpec((per, 2 * GROUP, 256), lambda i: (i, 0, 0)),
        out_shape=jax.ShapeDtypeStruct((8, 2 * GROUP, 256), BF16),
        cost_estimate=pl.CostEstimate(
            flops=2 * 1024 * 1024 * 256, bytes_accessed=3 << 20, transcendentals=0
        ),
    )(a, e)


def attend_kernel(count_ref, s_ref, out_ref):
    total = s_ref[0].astype(F32)
    for k in range(1, 8):
        total = total + s_ref[k].astype(F32)
    scores = total[0:GROUP] * INV
    grad_probs = total[GROUP : 2 * GROUP]
    count = count_ref[0]
    row = lax.broadcasted_iota(jnp.int32, scores.shape, 1)
    weighted = jnp.where(row < count * NBR_LEN, jnp.exp(scores), 0.0)
    empty = jnp.where(count == 0, 1.0, 0.0)
    probs = weighted / (jnp.sum(weighted, axis=1, keepdims=True) + empty)
    centre = jnp.sum(probs * grad_probs, axis=1, keepdims=True)
    grad_scores = (probs * (grad_probs - centre) * INV).astype(BF16)
    probs_low = probs.astype(BF16)
    for k in range(8):
        out_ref[k, 0:GROUP] = grad_scores
        out_ref[k, GROUP : 2 * GROUP] = probs_low


def attend(counts, s):
    return pl.pallas_call(
        attend_kernel,
        in_specs=[
            pl.BlockSpec(memory_space=pltpu.SMEM),
            pl.BlockSpec(memory_space=pltpu.VMEM),
        ],
        out_specs=pl.BlockSpec(memory_space=pltpu.VMEM),
        out_shape=jax.ShapeDtypeStruct((8, 2 * GROUP, 256), BF16),
    )(counts, s)


def term_kernel(g_ref, a_ref, out_ref, gt_ref):
    @pl.when(pl.program_id(0) == 0)
    def _():
        for h in range(8):
            gt_ref[:, h * 128 : (h + 1) * 128] = g_ref[h].astype(F32).T.astype(BF16)

    part = jnp.dot(
        gt_ref[...], a_ref[...].reshape(1024, BLOCK), preferred_element_type=F32
    )
    out_ref[:, 0] = part.astype(BF16).reshape(16, 16, BLOCK)


def term(g, a):
    return pl.pallas_call(
        term_kernel,
        grid=(4,),
        in_specs=[
            pl.BlockSpec((8, 2 * GROUP, 256), lambda i: (0, 0, 0)),
            pl.BlockSpec((8, 2 * GROUP, BLOCK), lambda i: (0, 0, i)),
        ],
        out_specs=pl.BlockSpec((16, 1, 16, BLOCK), lambda i: (0, i, 0, 0)),
        out_shape=jax.ShapeDtypeStruct((16, 4, 16, BLOCK), BF16),
        scratch_shapes=[pltpu.VMEM((256, 1024), BF16)],
        cost_estimate=pl.CostEstimate(
            flops=2 * 1024 * 1024 * 256, bytes_accessed=3 << 20, transcendentals=0
        ),
    )(g, a)


def mix_kernel(g_ref, e_ref, out_ref):
    gs = g_ref[:, 0:GROUP].reshape(8 * GROUP, 256)
    for b in range(4):
        part = jnp.dot(gs, e_ref[:, b].reshape(256, BLOCK), preferred_element_type=F32)
        out_ref[:, :, b * BLOCK : (b + 1) * BLOCK] = part.astype(BF16).reshape(8, GROUP, BLOCK)


def mix(g, e):
    vmem = pl.BlockSpec(memory_space=pltpu.VMEM)
    return pl.pallas_call(
        mix_kernel,
        in_specs=[vmem, vmem],
        out_specs=vmem,
        out_shape=jax.ShapeDtypeStruct((8, GROUP, 4 * BLOCK), BF16),
        cost_estimate=pl.CostEstimate(
            flops=2 * 512 * 256 * 1024, bytes_accessed=2 << 20, transcendentals=0
        ),
    )(g, e)


def query_kernel(x_ref, w_ref, out_ref, acc_ref):
    @pl.when(pl.program_id(0) == 0)
    def _():
        acc_ref[...] = jnp.zeros_like(acc_ref)

    total = acc_ref[...]
    for d in range(x_ref.shape[0]):
        for b in range(4):
            total = total + jnp.dot(
                x_ref[d, :, b * BLOCK : (b + 1) * BLOCK], w_ref[b, d], preferred_element_type=F32
            )
    acc_ref[...] = total
    out_ref[...] = total.astype(BF16)


def query(x, wk):
    per = 4
    return pl.pallas_call(
        query_kernel,
        grid=(8 // per,),
        in_specs=[
            pl.BlockSpec((per, GROUP, 4 * BLOCK), lambda i: (i, 0, 0)),
            pl.BlockSpec((4, per, BLOCK, HEAD), lambda i: (0, i, 0, 0)),
        ],
        out_specs=pl.BlockSpec((GROUP, HEAD), lambda i: (0, 0)),
        out_shape=jax.ShapeDtypeStruct((GROUP, HEAD), BF16),
        scratch_shapes=[pltpu.VMEM((GROUP, HEAD), F32)],
        cost_estimate=pl.CostEstimate(
            flops=2 * 64 * 8192 * 128, bytes_accessed=3 << 20, transcendentals=0
        ),
    )(x, wk.reshape(4, 8, BLOCK, HEAD))


def local(encoded, w_key, w_value, queries, cotangent, counts):
    key_weight, value_weight = w_key[0], w_value[0]
    out_rows = jnp.broadcast_to(encoded[:, None], (16, 4, 16, BLOCK)).reshape(64, 16, BLOCK)
    rows = lax.all_to_all(out_rows, SPREAD, 0, 0, tiled=True).reshape(16, 4, 16, BLOCK)
    projected = project(queries[0], cotangent[0], key_weight, value_weight)
    shared = lax.all_to_all(projected, TEAM, 0, 0, tiled=True)
    parts = lax.all_to_all(score(shared, rows), TEAM, 0, 0, tiled=True)
    grads = lax.all_to_all(attend(counts.reshape(1), parts), TEAM, 0, 0, tiled=True)
    sent = term(grads, shared).reshape(64, 16, BLOCK)
    terms = lax.all_to_all(sent, SPREAD, 0, 0, tiled=True).reshape(16, 4, 16, BLOCK)
    mixed = lax.all_to_all(mix(grads, rows), TEAM, 0, 0, tiled=True)
    grad_queries = query(mixed, key_weight)
    grad_encoded = jnp.sum(terms.astype(F32), axis=1)
    return grad_queries[None], grad_encoded


def solution(mesh):
    fine = Mesh(mesh.devices.reshape(2, 4, 2, 4, 2, 4), ("zh", "y", "c", "z4", "z2", "x"))
    by_head = P(SECTION, None, TENSOR)
    return jax.shard_map(
        local,
        mesh=fine,
        in_specs=(P(None, SECTION, TENSOR), by_head, by_head, by_head, by_head, P(SECTION, None)),
        out_specs=(by_head, P(None, SECTION, TENSOR)),
        check_vma=False,
    )
```

time: 713 us -> 186 us (0.26)
  waiting for transfers between devices: 614 us -> 71.2 us
  blocking collectives: 0 us -> 44.2 us
  Pallas kernels: 0 us -> 21.2 us
  matrix products: 20.8 us -> 0 us
  starting transfers between devices: 59 us -> 40.7 us
  between operations: 14.8 us -> 1.31 us
    reduce_scatter x1 -> x0, waiting for transfers between devices: 264 us -> none  [local(): lax.psum_scatter(head_term.astype(jnp.bfloat16), 'tensor', scatter_dimens...]
    all_gather x1 -> x0, waiting for transfers between devices: 183 us -> none  [local(): whole_rows = lax.all_gather(encoded, 'tensor', axis=2, tiled=True)]
    all_to_all x2 -> x4, waiting for transfers between devices: 166 us -> 71.2 us  [the longest x1 28.6 us: local(): lax.all_to_all(sent, SPREAD, 0, 0, tiled=True).reshape(16, 4, 16, BLOCK)]
    all_to_all x0 -> x2, blocking collectives: none -> 44.2 us  [the longest x1 32.6 us: local(): shared = lax.all_to_all(projected, TEAM, 0, 0, tiled=True)]
    pallas_call x0 -> x6, Pallas kernels: none -> 21.2 us  [the longest x1 5.08 us: project(): pl.pallas_call(project_kernel, grid=(8 // per,), in_specs=[small, small,...]
    dot_general x6 -> x0, matrix products: 20.8 us -> none  [the longest x1 7.44 us: local(): jnp.dot(value_grads, value_weight.T, preferred_element_type=jnp.float32)]
    all_to_all x2 -> x4, starting transfers between devices: 58.9 us -> 40.7 us  [the longest x1 19.8 us: local(): lax.all_to_all(out_rows, SPREAD, 0, 0, tiled=True).reshape(16, 4, 16, BLOCK)]
  transfers between devices with their start and end apart: 4 -> 4, of which waited for: 4 -> 4; matrix products, arithmetic and copies ran while one was open for 0% -> 0% of each run, Pallas kernels for 0% -> 4%
where the time goes in v1:
time: 186 us; the launch traced here: 183 us
  waiting for transfers between devices  71.2 us (38%)
  blocking collectives  44.2 us (24%)
  starting transfers between devices  40.7 us (22%)
  Pallas kernels  21.2 us (11%)
  local copies, waits for them, and re-layouts  3.53 us (2%)
    all_to_all x1, blocking collectives, local(): shared = lax.all_to_all(projected, TEAM, 0, 0, tiled=True)  32.6 us
    all_to_all x1, waiting for transfers between devices, local(): lax.all_to_all(sent, SPREAD, 0, 0, tiled=True).reshape(16, 4, 16, BLOCK)  28.6 us
    all_to_all x1, waiting for transfers between devices, local(): lax.all_to_all(out_rows, SPREAD, 0, 0, tiled=True).reshape(16, 4, 16, BLOCK)  24.2 us
    all_to_all x1, starting transfers between devices, local(): lax.all_to_all(out_rows, SPREAD, 0, 0, tiled=True).reshape(16, 4, 16, BLOCK)  19.8 us
    all_to_all x1, starting transfers between devices, local(): lax.all_to_all(sent, SPREAD, 0, 0, tiled=True).reshape(16, 4, 16, BLOCK)  13.6 us
    all_to_all x1, waiting for transfers between devices, local(): mixed = lax.all_to_all(mix(grads, rows), TEAM, 0, 0, tiled=True)  12 us
    all_to_all x1, blocking collectives, local(): lax.all_to_all(attend(counts.reshape(1), parts), TEAM, 0, 0, tiled=True)  11.6 us
    all_to_all x1, waiting for transfers between devices, local(): parts = lax.all_to_all(score(shared, rows), TEAM, 0, 0, tiled=True)  6.42 us
  transfers between devices with their start and end apart: 4, of which 4 were waited for; matrix products, arithmetic and copies ran while one was open for 0% of the time, Pallas kernels for 4%

profile of v1, /device:TPU:1, one launch (start us, length us, event | category | flops | bytes accessed | tf_op | source)
XLA Modules:
  0.0 183.0 jit_solution(205502152383814136)
XLA Ops:
  0.6 1.7 broadcast_in_dim.4
  2.4 19.8 %all-to-all-start.1 = ((bf16[64,16,256]{2,1,0:T(8,128)(2,1)}), bf16[64,16,256]{2,1,0:T(8,128)(2,1)S(1)}, u32[]{:S(2)}, u32[]{:S(2)}) async-start(bf16[64,16,256]{2,1,0:T(8,128)(2,1)} %bitcast.5), calls=%async_computation.1 | async-start | bytes 1048576 | tf_op jit(solution)/shard_map/all_to_all | solution.py:197
  22.2 5.1 %shard_map.77 = bf16[8,128,1024]{2,1,0:T(8,128)(2,1)} custom-call(bf16[64,128]{1,0:T(8,128)(2,1)} %bitcast.19, bf16[64,128]{1,0:T(8,128)(2,1)} %bitcast.20, bf16[4,8,256,128]{3,2,1,0:T(8,128)(2,1)} %bitcast.13, bf16[4,8,256,128]{3,2,1,0:T(8,128)(2,1)} %bitcast.17), custom_call_target="tpu_custom_call" | custom-call | flops 268435456 | bytes 6291456 | tf_op jit(solution)/shard_map/pallas_call | solution.py:40
  27.2 24.2 %all-to-all-done.1 = bf16[64,16,256]{2,1,0:T(8,128)(2,1)S(1)} async-done(((bf16[64,16,256]{2,1,0:T(8,128)(2,1)}), bf16[64,16,256]{2,1,0:T(8,128)(2,1)S(1)}, u32[]{:S(2)}, u32[]{:S(2)}) %all-to-all-start.1) | async-done | bytes 524320 | tf_op jit(solution)/shard_map/all_to_all | solution.py:197
  51.4 0.0 copy-start
  51.4 32.6 %all_to_all.30.a_ref = bf16[8,128,1024]{2,1,0:T(8,128)(2,1)} all-to-all(bf16[8,128,1024]{2,1,0:T(8,128)(2,1)} %shard_map.77), channel_id=1, replica_groups=mesh['zh'=2,'y'=4,'c'=2,'z4'=4,'z2'=2,'x'=4] {'z2','x'}, dimensions={0} | all-to-all | bytes 4194304 | tf_op jit(solution)/shard_map/all_to_all | solution.py:199
  84.0 0.0 copy-done
  84.0 4.3 %shard_map.78 = bf16[8,128,256]{2,1,0:T(8,128)(2,1)} custom-call(bf16[8,128,1024]{2,1,0:T(8,128)(2,1)} %all_to_all.30.a_ref, bf16[16,4,16,256]{3,2,1,0:T(8,128)(2,1)} %bitcast.15), custom_call_target="tpu_custom_call" | custom-call | flops 536870912 | bytes 3145728 | tf_op jit(solution)/shard_map/pallas_call | solution.py:66
  88.3 3.5 %all-to-all-start.2 = ((bf16[8,128,256]{2,1,0:T(8,128)(2,1)}), bf16[8,128,256]{2,1,0:T(8,128)(2,1)S(1)}, u32[]{:S(2)}, u32[]{:S(2)}) async-start(bf16[8,128,256]{2,1,0:T(8,128)(2,1)} %shard_map.78), calls=%async_computation.2 | async-start | bytes 1048576 | tf_op jit(solution)/shard_map/all_to_all | solution.py:200
  92.4 6.4 %all-to-all-done.2.s_ref = bf16[8,128,256]{2,1,0:T(8,128)(2,1)S(1)} async-done(((bf16[8,128,256]{2,1,0:T(8,128)(2,1)}), bf16[8,128,256]{2,1,0:T(8,128)(2,1)S(1)}, u32[]{:S(2)}, u32[]{:S(2)}) %all-to-all-start.2) | async-done | bytes 524320 | tf_op jit(solution)/shard_map/all_to_all | solution.py:200
  98.9 0.0 copy-start.2
  98.9 0.8 copy-done.2
  99.7 2.1 %shard_map.79 = bf16[8,128,256]{2,1,0:T(8,128)(2,1)} custom-call(s32[1]{0:T(128)} %bitcast.12.count_ref, bf16[8,128,256]{2,1,0:T(8,128)(2,1)} %copy-done.2), custom_call_target="tpu_custom_call" | custom-call | tf_op jit(solution)/shard_map/pallas_call | solution.py:101
  101.7 11.6 %all_to_all.31.g_ref = bf16[8,128,256]{2,1,0:T(8,128)(2,1)} all-to-all(bf16[8,128,256]{2,1,0:T(8,128)(2,1)} %shard_map.79), channel_id=1, replica_groups=mesh['zh'=2,'y'=4,'c'=2,'z4'=4,'z2'=2,'x'=4] {'z2','x'}, dimensions={0} | all-to-all | bytes 1048576 | tf_op jit(solution)/shard_map/all_to_all | solution.py:201
  113.3 4.4 %shard_map.82 = bf16[16,4,16,256]{3,2,1,0:T(8,128)(2,1)} custom-call(bf16[8,128,256]{2,1,0:T(8,128)(2,1)} %all_to_all.31.g_ref, bf16[8,128,1024]{2,1,0:T(8,128)(2,1)} %all_to_all.30.a_ref), custom_call_target="tpu_custom_call" | custom-call | flops 536870912 | bytes 3145728 | tf_op jit(solution)/shard_map/pallas_call | solution.py:125
  117.8 13.6 %all-to-all-start.5 = ((bf16[64,16,256]{2,1,0:T(8,128)(2,1)}), bf16[64,16,256]{2,1,0:T(8,128)(2,1)S(1)}, u32[]{:S(2)}, u32[]{:S(2)}) async-start(bf16[64,16,256]{2,1,0:T(8,128)(2,1)} %bitcast.18), calls=%async_computation.5 | async-start | bytes 1048576 | tf_op jit(solution)/shard_map/all_to_all | solution.py:203
  131.4 2.6 %shard_map.80 = bf16[8,64,1024]{2,1,0:T(8,128)(2,1)} custom-call(bf16[8,128,256]{2,1,0:T(8,128)(2,1)} %all_to_all.31.g_ref, bf16[16,4,16,256]{3,2,1,0:T(8,128)(2,1)} %bitcast.16), custom_call_target="tpu_custom_call" | custom-call | flops 268435456 | bytes 2097152 | tf_op jit(solution)/shard_map/pallas_call | solution.py:150
  134.0 28.6 %all-to-all-done.5 = bf16[64,16,256]{2,1,0:T(8,128)(2,1)S(1)} async-done(((bf16[64,16,256]{2,1,0:T(8,128)(2,1)}), bf16[64,16,256]{2,1,0:T(8,128)(2,1)S(1)}, u32[]{:S(2)}, u32[]{:S(2)}) %all-to-all-start.5) | async-done | bytes 524320 | tf_op jit(solution)/shard_map/all_to_all | solution.py:203
  162.6 3.8 %all-to-all-start.4 = ((bf16[8,64,1024]{2,1,0:T(8,128)(2,1)}), bf16[8,64,1024]{2,1,0:T(8,128)(2,1)S(1)}, u32[]{:S(2)}, u32[]{:S(2)}) async-start(bf16[8,64,1024]{2,1,0:T(8,128)(2,1)} %shard_map.80), calls=%async_computation.4 | async-start | bytes 2097152 | tf_op jit(solution)/shard_map/all_to_all | solution.py:204
  166.4 0.8 convert_reduce_fusion
  167.2 12.0 %all-to-all-done.4.x_ref = bf16[8,64,1024]{2,1,0:T(8,128)(2,1)S(1)} async-done(((bf16[8,64,1024]{2,1,0:T(8,128)(2,1)}), bf16[8,64,1024]{2,1,0:T(8,128)(2,1)S(1)}, u32[]{:S(2)}, u32[]{:S(2)}) %all-to-all-start.4) | async-done | bytes 1048608 | tf_op jit(solution)/shard_map/all_to_all | solution.py:204
  179.2 0.0 copy-start.1
  179.2 1.0 copy-done.1
  180.2 2.8 %shard_map.81 = bf16[64,128]{1,0:T(8,128)(2,1)} custom-call(bf16[8,64,1024]{2,1,0:T(8,128)(2,1)} %copy-done.1, bf16[4,8,256,128]{3,2,1,0:T(8,128)(2,1)} %bitcast.14), custom_call_target="tpu_custom_call" | custom-call | flops 134217728 | bytes 3145728 | tf_op jit(solution)/shard_map/pallas_call | solution.py:178
Async XLA Ops:
  2.4 49.1 %all-to-all-start.1 = ((bf16[64,16,256]{2,1,0:T(8,128)(2,1)}), bf16[64,16,256]{2,1,0:T(8,128)(2,1)S(1)}, u32[]{:S(2)}, u32[]{:S(2)}) async-start(bf16[64,16,256]{2,1,0:T(8,128)(2,1)} %bitcast.5), calls=%async_computation.1 | async-start | bytes 1048576 | tf_op jit(solution)/shard_map/all_to_all | solution.py:197
  51.4 32.6 %copy-start = (bf16[64,16,256]{2,1,0:T(8,128)(2,1)}, bf16[64,16,256]{2,1,0:T(8,128)(2,1)S(1)}, u32[]{:S(2)}) copy-start(bf16[64,16,256]{2,1,0:T(8,128)(2,1)S(1)} %all-to-all-done.1) | copy-start | bytes 1572868
  88.3 10.6 %all-to-all-start.2 = ((bf16[8,128,256]{2,1,0:T(8,128)(2,1)}), bf16[8,128,256]{2,1,0:T(8,128)(2,1)S(1)}, u32[]{:S(2)}, u32[]{:S(2)}) async-start(bf16[8,128,256]{2,1,0:T(8,128)(2,1)} %shard_map.78), calls=%async_computation.2 | async-start | bytes 1048576 | tf_op jit(solution)/shard_map/all_to_all | solution.py:200
  98.9 0.8 copy-start.2
  117.8 44.8 %all-to-all-start.5 = ((bf16[64,16,256]{2,1,0:T(8,128)(2,1)}), bf16[64,16,256]{2,1,0:T(8,128)(2,1)S(1)}, u32[]{:S(2)}, u32[]{:S(2)}) async-start(bf16[64,16,256]{2,1,0:T(8,128)(2,1)} %bitcast.18), calls=%async_computation.5 | async-start | bytes 1048576 | tf_op jit(solution)/shard_map/all_to_all | solution.py:203
  162.6 16.6 %all-to-all-start.4 = ((bf16[8,64,1024]{2,1,0:T(8,128)(2,1)}), bf16[8,64,1024]{2,1,0:T(8,128)(2,1)S(1)}, u32[]{:S(2)}, u32[]{:S(2)}) async-start(bf16[8,64,1024]{2,1,0:T(8,128)(2,1)} %shard_map.80), calls=%async_computation.4 | async-start | bytes 2097152 | tf_op jit(solution)/shard_map/all_to_all | solution.py:204
  179.2 1.0 copy-start.1

commit v2 on v0

v2 whole, which is shorter than its diff:
```python
import math

import jax
import jax.numpy as jnp
from jax import lax
from jax.experimental import pallas as pl
from jax.experimental.pallas import tpu as pltpu
from jax.sharding import Mesh, PartitionSpec as P

NBR_LEN = 128
HEAD = 128
GROUP = 64
PAIR = 2 * GROUP
ROWS = 256
BLOCK = 256
HALF = 4 * BLOCK
INV = 1.0 / math.sqrt(HEAD)
F32 = jnp.float32
BF16 = jnp.bfloat16

SECTION = ("zh", "y", "c")
TENSOR = ("z4", "z2", "x")
SPREAD = ("zh", "y", "c", "z4")
FLIP = [(0, 1), (1, 0)]


def across(k):
    return [(i, i ^ k) for i in range(4)]


def nt(a, b):
    return lax.dot_general(a, b, (((1,), (1,)), ((), ())), preferred_element_type=F32)


def nn(a, b):
    return jnp.dot(a, b, preferred_element_type=F32)


def cost(flops, nbytes):
    return pl.CostEstimate(flops=flops, bytes_accessed=nbytes, transcendentals=0)


def full(shape):
    return pl.BlockSpec(shape, lambda i, s: (0,) * len(shape))


def call(kernel, scalars, grid, in_specs, out_specs, out_shape, args, estimate, scratch=()):
    return pl.pallas_call(
        kernel,
        grid_spec=pltpu.PrefetchScalarGridSpec(
            num_scalar_prefetch=1,
            grid=(grid,),
            in_specs=in_specs,
            out_specs=out_specs,
            scratch_shapes=scratch,
        ),
        out_shape=out_shape,
        cost_estimate=estimate,
    )(scalars, *args)


def project_kernel(s_ref, q_ref, ct_ref, wk_ref, wv_ref, out_ref):
    for b in range(4):
        cols = pl.ds(b * BLOCK, BLOCK)
        out_ref[0:GROUP, cols] = nt(q_ref[...], wk_ref[b, 0, 0]).astype(BF16)
        out_ref[GROUP:PAIR, cols] = nt(ct_ref[...], wv_ref[b, 0, 0]).astype(BF16)


def project(scalars, q, ct, wk, wv, k):
    w_spec = pl.BlockSpec((4, 1, 1, BLOCK, HEAD), lambda i, s: (0, i, s[1] ^ k, 0, 0))
    small = full((GROUP, HEAD))
    return call(
        project_kernel,
        scalars,
        2,
        [small, small, w_spec, w_spec],
        pl.BlockSpec((PAIR, HALF), lambda i, s: (0, i)),
        jax.ShapeDtypeStruct((PAIR, 2 * HALF), BF16),
        (q, ct, wk, wv),
        cost(2 * 128 * 2048 * 128, 3 << 19),
    )


def partial_scores(a_refs, e_ref):
    total = None
    for b in range(4):
        a = jnp.concatenate([r[:, b * BLOCK : (b + 1) * BLOCK] for r in a_refs], axis=0)
        part = nt(a, e_ref[:, b].reshape(ROWS, BLOCK))
        total = part if total is None else total + part
    return total


def first_scores_kernel(s_ref, a0, a1, a2, a3, e_ref, out_ref):
    out_ref[...] = partial_scores((a0, a1, a2, a3), e_ref)


def last_scores_kernel(s_ref, a0, a1, a2, a3, e_ref, first_ref, out_ref):
    total = first_ref[...] + partial_scores((a0, a1, a2, a3), e_ref)
    for k in range(4):
        out_ref[s_ref[1] ^ k] = total[k * PAIR : (k + 1) * PAIR].astype(BF16)


A_OWN = pl.BlockSpec((PAIR, HALF), lambda i, s: (0, s[0]))
A_OTHER = pl.BlockSpec((PAIR, HALF), lambda i, s: (0, 1 - s[0]))
E_SPEC = full((16, 4, 16, BLOCK))
SCORE_COST = cost(2 * 512 * 1024 * 256, 2 << 20)


def first_scores(scalars, a, e):
    return call(
        first_scores_kernel,
        scalars,
        1,
        [A_OWN] * 4 + [E_SPEC],
        full((4 * PAIR, ROWS)),
        jax.ShapeDtypeStruct((4 * PAIR, ROWS), F32),
        (*a, e),
        SCORE_COST,
    )


def last_scores(scalars, a, e, first):
    return call(
        last_scores_kernel,
        scalars,
        1,
        [A_OTHER] * 4 + [E_SPEC, full((4 * PAIR, ROWS))],
        full((4, PAIR, ROWS)),
        jax.ShapeDtypeStruct((4, PAIR, ROWS), BF16),
        (*a, e, first),
        SCORE_COST,
    )


def attend_kernel(count_ref, s_ref, out_ref):
    total = s_ref[0].astype(F32)
    for k in range(1, 4):
        total = total + s_ref[k].astype(F32)
    scores = total[0:GROUP] * INV
    grad_probs = total[GROUP:PAIR]
    count = count_ref[0]
    row = lax.broadcasted_iota(jnp.int32, scores.shape, 1)
    weighted = jnp.where(row < count * NBR_LEN, jnp.exp(scores), 0.0)
    empty = jnp.where(count == 0, 1.0, 0.0)
    probs = weighted / (jnp.sum(weighted, axis=1, keepdims=True) + empty)
    centre = jnp.sum(probs * grad_probs, axis=1, keepdims=True)
    grad_scores = probs * (grad_probs - centre) * INV
    both = jnp.concatenate([grad_scores, probs], axis=0).T.astype(BF16)
    for k in range(4):
        out_ref[k] = both


def attend(counts, s):
    return pl.pallas_call(
        attend_kernel,
        in_specs=[
            pl.BlockSpec(memory_space=pltpu.SMEM),
            pl.BlockSpec(memory_space=pltpu.VMEM),
        ],
        out_specs=pl.BlockSpec(memory_space=pltpu.VMEM),
        out_shape=jax.ShapeDtypeStruct((4, ROWS, PAIR), BF16),
    )(counts, s)


def term_kernel(s_ref, g_ref, a0, a1, a2, a3, out_ref):
    g = jnp.concatenate([g_ref[s_ref[1] ^ k] for k in range(4)], axis=1)
    for b in range(4):
        a = jnp.concatenate([r[:, b * BLOCK : (b + 1) * BLOCK] for r in (a0, a1, a2, a3)], axis=0)
        out_ref[:, b] = nn(g, a).astype(out_ref.dtype).reshape(16, 16, BLOCK)


def term(scalars, g, a, a_spec, kind):
    return call(
        term_kernel,
        scalars,
        1,
        [full((4, ROWS, PAIR))] + [a_spec] * 4,
        E_SPEC,
        jax.ShapeDtypeStruct((16, 4, 16, BLOCK), kind),
        (g, *a),
        cost(2 * 512 * 1024 * 256, 2 << 20),
    )


def mix_kernel(s_ref, g_ref, own_ref, other_ref, *out_refs):
    gs = jnp.concatenate([g_ref[s_ref[1] ^ k, :, 0:GROUP] for k in range(4)], axis=1)
    gs = gs.astype(F32).T.astype(BF16)
    for p, e_ref in enumerate((own_ref, other_ref)):
        for b in range(4):
            part = nn(gs, e_ref[:, b].reshape(ROWS, BLOCK)).astype(BF16)
            for k in range(4):
                at = p * HALF + b * BLOCK
                out_refs[k][:, at : at + BLOCK] = part[k * GROUP : (k + 1) * GROUP]


def mix(scalars, g, own, other):
    return call(
        mix_kernel,
        scalars,
        1,
        [full((4, ROWS, PAIR)), E_SPEC, E_SPEC],
        [full((GROUP, 2 * HALF))] * 4,
        [jax.ShapeDtypeStruct((GROUP, 2 * HALF), BF16)] * 4,
        (g, own, other),
        cost(2 * 256 * 256 * 2048, 2 << 20),
    )


def query_kernel(s_ref, x0, x1, x2, x3, w_ref, out_ref, acc_ref):
    total = None
    for k, x_ref in enumerate((x0, x1, x2, x3)):
        for b in range(4):
            part = nn(x_ref[:, b * BLOCK : (b + 1) * BLOCK], w_ref[b, 0, s_ref[1] ^ k])
            total = part if total is None else total + part

    @pl.when(pl.program_id(0) == 0)
    def _():
        acc_ref[...] = total

    @pl.when(pl.program_id(0) == 1)
    def _():
        out_ref[...] = (acc_ref[...] + total).astype(BF16)


def query(scalars, x, wk):
    return call(
        query_kernel,
        scalars,
        2,
        [pl.BlockSpec((GROUP, HALF), lambda i, s: (0, i))] * 4
        + [pl.BlockSpec((4, 1, 4, BLOCK, HEAD), lambda i, s: (0, s[0] ^ i, 0, 0, 0))],
        full((GROUP, HEAD)),
        jax.ShapeDtypeStruct((GROUP, HEAD), BF16),
        (*x, wk),
        cost(2 * 64 * 8192 * 128, 3 << 20),
        [pltpu.VMEM((GROUP, HEAD), F32)],
    )


def to_members(parts):
    return [parts[0]] + [lax.ppermute(parts[k], "x", across(k)) for k in range(1, 4)]


def local(encoded, w_key, w_value, queries, cotangent, counts):
    scalars = jnp.stack([lax.axis_index("z2"), lax.axis_index("x")]).astype(jnp.int32)
    wk = w_key.reshape(4, 2, 4, BLOCK, HEAD)
    wv = w_value.reshape(4, 2, 4, BLOCK, HEAD)
    out_rows = jnp.broadcast_to(encoded[:, None], (16, 4, 16, BLOCK)).reshape(64, 16, BLOCK)
    own = lax.all_to_all(out_rows, SPREAD, 0, 0, tiled=True).reshape(16, 4, 16, BLOCK)
    shared = to_members(
        [project(scalars, queries[0], cotangent[0], wk, wv, k) for k in range(4)]
    )
    other = lax.ppermute(own, "z2", FLIP)
    first = first_scores(scalars, shared, own)
    sums = last_scores(scalars, shared, other, first)
    parts = lax.all_to_all(sums, "x", 0, 0, tiled=True)
    grads = lax.all_to_all(attend(counts.reshape(1), parts), "x", 0, 0, tiled=True)
    passed = lax.ppermute(term(scalars, grads, shared, A_OTHER, BF16), "z2", FLIP)
    kept = term(scalars, grads, shared, A_OWN, F32)
    sent = (kept + passed.astype(F32)).astype(BF16).reshape(64, 16, BLOCK)
    terms = lax.all_to_all(sent, SPREAD, 0, 0, tiled=True).reshape(16, 4, 16, BLOCK)
    mixed = to_members(mix(scalars, grads, own, other))
    grad_queries = query(scalars, mixed, wk)
    grad_encoded = jnp.sum(terms.astype(F32), axis=1)
    return grad_queries[None], grad_encoded


def solution(mesh):
    fine = Mesh(mesh.devices.reshape(2, 4, 2, 4, 2, 4), ("zh", "y", "c", "z4", "z2", "x"))
    by_head = P(SECTION, None, TENSOR)
    return jax.shard_map(
        local,
        mesh=fine,
        in_specs=(P(None, SECTION, TENSOR), by_head, by_head, by_head, by_head, P(SECTION, None)),
        out_specs=(by_head, P(None, SECTION, TENSOR)),
        check_vma=False,
    )
```

time: 713 us -> 167 us (0.23)
  waiting for transfers between devices: 614 us -> 41.2 us
  Pallas kernels: 0 us -> 34.4 us
  matrix products: 20.8 us -> 0 us
  between operations: 14.8 us -> 1.43 us
  blocking collectives: 0 us -> 9.62 us
  starting transfers between devices: 59 us -> 68.6 us
    reduce_scatter x1 -> x0, waiting for transfers between devices: 264 us -> none  [local(): lax.psum_scatter(head_term.astype(jnp.bfloat16), 'tensor', scatter_dimens...]
    all_gather x1 -> x0, waiting for transfers between devices: 183 us -> none  [local(): whole_rows = lax.all_gather(encoded, 'tensor', axis=2, tiled=True)]
    all_to_all x2 -> x3, waiting for transfers between devices: 166 us -> 15.2 us  [the longest x1 9.89 us: local(): lax.all_to_all(out_rows, SPREAD, 0, 0, tiled=True).reshape(16, 4, 16, BLOCK)]
    pallas_call x0 -> x11, Pallas kernels: none -> 34.4 us  [the longest x10 32.5 us: call(): pl.pallas_call(kernel, grid_spec=pltpu.PrefetchScalarGridSpec(num_scalar_...]
    ppermute x0 -> x8, starting transfers between devices: none -> 26.9 us  [the longest x6 19.1 us: to_members(): lax.ppermute(parts[k], 'x', across(k))]
    ppermute x0 -> x8, waiting for transfers between devices: none -> 26 us  [the longest x6 18.8 us: to_members(): lax.ppermute(parts[k], 'x', across(k))]
    dot_general x6 -> x0, matrix products: 20.8 us -> none  [the longest x1 7.44 us: local(): jnp.dot(value_grads, value_weight.T, preferred_element_type=jnp.float32)]
    all_to_all x2 -> x3, starting transfers between devices: 58.9 us -> 41.7 us  [the longest x1 19.8 us: local(): lax.all_to_all(out_rows, SPREAD, 0, 0, tiled=True).reshape(16, 4, 16, BLOCK)]
  transfers between devices with their start and end apart: 4 -> 11, of which waited for: 4 -> 6; matrix products, arithmetic and copies ran while one was open for 0% -> 0% of each run, Pallas kernels for 0% -> 16%
where the time goes in v2:
time: 167 us; the launch traced here: 164 us
  starting transfers between devices  68.6 us (41%)
  waiting for transfers between devices  41.2 us (25%)
  Pallas kernels  34.4 us (21%)
  blocking collectives  9.62 us (6%)
  local copies, waits for them, and re-layouts  4.76 us (3%)
  other arithmetic  3.55 us (2%)
    pallas_call x10, Pallas kernels, call(): pl.pallas_call(kernel, grid_spec=pltpu.PrefetchScalarGridSpec(num_scalar_...  32.5 us
    all_to_all x1, starting transfers between devices, local(): lax.all_to_all(out_rows, SPREAD, 0, 0, tiled=True).reshape(16, 4, 16, BLOCK)  19.8 us
    ppermute x6, starting transfers between devices, to_members(): lax.ppermute(parts[k], 'x', across(k))  19.1 us
    ppermute x6, waiting for transfers between devices, to_members(): lax.ppermute(parts[k], 'x', across(k))  18.8 us
    all_to_all x1, starting transfers between devices, local(): lax.all_to_all(sent, SPREAD, 0, 0, tiled=True).reshape(16, 4, 16, BLOCK)  18.5 us
    all_to_all x1, waiting for transfers between devices, local(): lax.all_to_all(out_rows, SPREAD, 0, 0, tiled=True).reshape(16, 4, 16, BLOCK)  9.89 us
    all_to_all x1, blocking collectives, local(): lax.all_to_all(attend(counts.reshape(1), parts), 'x', 0, 0, tiled=True)  9.62 us
    ppermute x1, waiting for transfers between devices, local(): lax.ppermute(term(scalars, grads, shared, A_OTHER, BF16), 'z2', FLIP)  7.18 us
  transfers between devices with their start and end apart: 11, of which 6 were waited for; matrix products, arithmetic and copies ran while one was open for 0% of the time, Pallas kernels for 16%

profile of v2, /device:TPU:1, one launch (start us, length us, event | category | flops | bytes accessed | tf_op | source)
XLA Modules:
  0.0 163.6 jit_solution(13470121825238307064)
XLA Ops:
  0.6 1.7 %broadcast_in_dim.4 = bf16[16,4,16,256]{3,2,1,0:T(8,128)(2,1)} broadcast(bf16[16,16,256]{2,1,0:T(8,128)(2,1)} %param.6), dimensions={0,2,3} | broadcast | bytes 655360 | tf_op jit(solution)/shard_map/broadcast_in_dim | solution.py:248
  2.4 19.8 %all-to-all-start = ((bf16[64,16,256]{2,1,0:T(8,128)(2,1)}), bf16[64,16,256]{2,1,0:T(8,128)(2,1)S(1)}, u32[]{:S(2)}, u32[]{:S(2)}) async-start(bf16[64,16,256]{2,1,0:T(8,128)(2,1)} %bitcast.7), calls=%async_computation | async-start | bytes 1048576 | tf_op jit(solution)/shard_map/all_to_all | solution.py:249
  22.2 0.6 pad_add_fusion.s_ref
  22.8 3.0 %shard_map.78 = bf16[128,2048]{1,0:T(8,128)(2,1)} custom-call(s32[2]{0:T(128)} %pad_add_fusion.s_ref, bf16[64,128]{1,0:T(8,128)(2,1)} %bitcast.27, bf16[64,128]{1,0:T(8,128)(2,1)} %bitcast.31, bf16[4,2,4,256,128]{4,3,2,1,0:T(8,128)(2,1)} %bitcast.15, bf16[4,2,4,256,128]{4,3,2,1,0:T(8,128)(2,1)} %bitcast.20), custom_call_target="tpu_custom_call" | custom-call | flops 67108864 | bytes 1572864 | tf_op jit(solution)/shard_map/pallas_call | solution.py:48
  25.8 3.1 %collective-permute-start = (bf16[128,2048]{1,0:T(8,128)(2,1)}, bf16[128,2048]{1,0:T(8,128)(2,1)S(1)}, u32[]{:S(2)}, u32[]{:S(2)}) collective-permute-start(bf16[128,2048]{1,0:T(8,128)(2,1)} %shard_map.78), channel_id=1, source_target_pairs={{0,1},{1,0},{2,3},{3,2},{4,5},{5,4},{6,7},{7,6},{8,9},{9,8},{10,11... | collective-permute-start | bytes 1572872 | tf_op jit(solution)/shard_map/ppermute | solution.py:241
  28.9 3.1 %shard_map.79 = bf16[128,2048]{1,0:T(8,128)(2,1)} custom-call(s32[2]{0:T(128)} %pad_add_fusion.s_ref, bf16[64,128]{1,0:T(8,128)(2,1)} %bitcast.28, bf16[64,128]{1,0:T(8,128)(2,1)} %bitcast.32, bf16[4,2,4,256,128]{4,3,2,1,0:T(8,128)(2,1)} %bitcast.16, bf16[4,2,4,256,128]{4,3,2,1,0:T(8,128)(2,1)} %bitcast.21), custom_call_target="tpu_custom_call" | custom-call | flops 67108864 | bytes 1572864 | tf_op jit(solution)/shard_map/pallas_call | solution.py:48
  32.0 4.3 %collective-permute-start.1 = (bf16[128,2048]{1,0:T(8,128)(2,1)}, bf16[128,2048]{1,0:T(8,128)(2,1)S(1)}, u32[]{:S(2)}, u32[]{:S(2)}) collective-permute-start(bf16[128,2048]{1,0:T(8,128)(2,1)} %shard_map.79), channel_id=1, source_target_pairs={{0,2},{1,3},{2,0},{3,1},{4,6},{5,7},{6,4},{7,5},{8,10},{9,11},{10,... | collective-permute-start | bytes 1572872 | tf_op jit(solution)/shard_map/ppermute | solution.py:241
  36.4 3.1 %shard_map.80 = bf16[128,2048]{1,0:T(8,128)(2,1)} custom-call(s32[2]{0:T(128)} %pad_add_fusion.s_ref, bf16[64,128]{1,0:T(8,128)(2,1)} %bitcast.29, bf16[64,128]{1,0:T(8,128)(2,1)} %bitcast.33, bf16[4,2,4,256,128]{4,3,2,1,0:T(8,128)(2,1)} %bitcast.17, bf16[4,2,4,256,128]{4,3,2,1,0:T(8,128)(2,1)} %bitcast.22), custom_call_target="tpu_custom_call" | custom-call | flops 67108864 | bytes 1572864 | tf_op jit(solution)/shard_map/pallas_call | solution.py:48
  39.4 2.1 %collective-permute-start.2 = (bf16[128,2048]{1,0:T(8,128)(2,1)}, bf16[128,2048]{1,0:T(8,128)(2,1)S(1)}, u32[]{:S(2)}, u32[]{:S(2)}) collective-permute-start(bf16[128,2048]{1,0:T(8,128)(2,1)} %shard_map.80), channel_id=1, source_target_pairs={{0,3},{1,2},{2,1},{3,0},{4,7},{5,6},{6,5},{7,4},{8,11},{9,10},{10,... | collective-permute-start | bytes 1572872 | tf_op jit(solution)/shard_map/ppermute | solution.py:241
  41.5 9.9 %all-to-all-done = bf16[64,16,256]{2,1,0:T(8,128)(2,1)S(1)} async-done(((bf16[64,16,256]{2,1,0:T(8,128)(2,1)}), bf16[64,16,256]{2,1,0:T(8,128)(2,1)S(1)}, u32[]{:S(2)}, u32[]{:S(2)}) %all-to-all-start) | async-done | bytes 524320 | tf_op jit(solution)/shard_map/all_to_all | solution.py:249
  51.4 0.0 copy-start.3
  51.4 5.6 %collective-permute-start.3 = (bf16[16,4,16,256]{3,2,1,0:T(8,128)(2,1)S(1)}, bf16[16,4,16,256]{3,2,1,0:T(8,128)(2,1)S(1)}, u32[]{:S(2)}, u32[]{:S(2)}) collective-permute-start(bf16[16,4,16,256]{3,2,1,0:T(8,128)(2,1)S(1)} %bitcast.24), channel_id=1, source_target_pairs={{0,4},{4,0},{1,5},{5,1},{2,6},{6,2},{3,7},{7,3},{8,12},{12,8},{9,1... | collective-permute-start | bytes 1572872 | tf_op jit(solution)/shard_map/ppermute | solution.py:253
  57.1 3.1 %shard_map.77.a0 = bf16[128,2048]{1,0:T(8,128)(2,1)} custom-call(s32[2]{0:T(128)} %pad_add_fusion.s_ref, bf16[64,128]{1,0:T(8,128)(2,1)} %bitcast.30, bf16[64,128]{1,0:T(8,128)(2,1)} %bitcast.34, bf16[4,2,4,256,128]{4,3,2,1,0:T(8,128)(2,1)} %bitcast.18, bf16[4,2,4,256,128]{4,3,2,1,0:T(8,128)(2,1)} %bitcast.23), custom_call_target="tpu_custom_call" | custom-call | flops 67108864 | bytes 1572864 | tf_op jit(solution)/shard_map/pallas_call | solution.py:48
  60.1 0.0 copy-done.3
  60.2 0.0 collective-permute-done.a1
  60.2 0.0 copy-start
  60.2 0.0 collective-permute-done.1.a2
  60.2 0.0 copy-start.1
  60.2 6.2 %collective-permute-done.2.a3 = bf16[128,2048]{1,0:T(8,128)(2,1)S(1)} collective-permute-done((bf16[128,2048]{1,0:T(8,128)(2,1)}, bf16[128,2048]{1,0:T(8,128)(2,1)S(1)}, u32[]{:S(2)}, u32[]{:S(2)}) %collective-permute-start.2) | collective-permute-done | bytes 524320 | tf_op jit(solution)/shard_map/ppermute | solution.py:241
  66.4 0.0 copy-done
  66.4 0.0 copy-done.1
  66.4 0.0 copy-start.2
  66.4 0.8 copy-done.2
  67.2 3.3 %shard_map.81.first_ref = f32[512,256]{1,0:T(8,128)} custom-call(s32[2]{0:T(128)} %pad_add_fusion.s_ref, bf16[128,2048]{1,0:T(8,128)(2,1)} %shard_map.77.a0, bf16[128,2048]{1,0:T(8,128)(2,1)} %copy-done, bf16[128,2048]{1,0:T(8,128)(2,1)} %copy-done.1, bf16[128,2048]{1,0:T(8,128)(2,1)} %copy-done.2, bf16[16,4,16,256]{3,2,1,0:T(8,128)(2,1)} %bitcast.25), custom_call_target="tpu_custom_call" | custom-call | flops 268435456 | bytes 2097152 | tf_op jit(solution)/shard_map/pallas_call | solution.py:48
  70.5 0.0 collective-permute-done.3.e_ref.other_ref
  70.5 0.0 copy-start.4
  70.5 0.8 copy-done.4
  71.3 3.4 %shard_map.82 = bf16[4,128,256]{2,1,0:T(8,128)(2,1)} custom-call(s32[2]{0:T(128)} %pad_add_fusion.s_ref, bf16[128,2048]{1,0:T(8,128)(2,1)} %shard_map.77.a0, bf16[128,2048]{1,0:T(8,128)(2,1)} %copy-done, bf16[128,2048]{1,0:T(8,128)(2,1)} %copy-done.1, bf16[128,2048]{1,0:T(8,128)(2,1)} %copy-done.2, bf16[16,4,16,256]{3,2,1,0:T(8,128)(2,1)} %copy-done.4, ...), custom_call_target="tpu_custom_call" | custom-call | flops 268435456 | bytes 2097152 | tf_op jit(solution)/shard_map/pallas_call | solution.py:48
  74.7 3.4 %all-to-all-start.1 = ((bf16[4,128,256]{2,1,0:T(8,128)(2,1)}), bf16[4,128,256]{2,1,0:T(8,128)(2,1)S(1)}, u32[]{:S(2)}, u32[]{:S(2)}) async-start(bf16[4,128,256]{2,1,0:T(8,128)(2,1)} %shard_map.82), calls=%async_computation.1 | async-start | bytes 524288 | tf_op jit(solution)/shard_map/all_to_all | solution.py:256
  78.8 5.3 %all-to-all-done.1.s_ref = bf16[4,128,256]{2,1,0:T(8,128)(2,1)S(1)} async-done(((bf16[4,128,256]{2,1,0:T(8,128)(2,1)}), bf16[4,128,256]{2,1,0:T(8,128)(2,1)S(1)}, u32[]{:S(2)}, u32[]{:S(2)}) %all-to-all-start.1) | async-done | bytes 262176 | tf_op jit(solution)/shard_map/all_to_all | solution.py:256
  84.1 0.0 copy-start.5
  84.1 0.7 copy-done.5
  84.8 2.0 %shard_map.83 = bf16[4,256,128]{2,1,0:T(8,128)(2,1)} custom-call(s32[1]{0:T(128)} %bitcast.14.count_ref, bf16[4,128,256]{2,1,0:T(8,128)(2,1)} %copy-done.5), custom_call_target="tpu_custom_call" | custom-call | tf_op jit(solution)/shard_map/pallas_call | solution.py:154
  86.7 9.6 %all_to_all.20.g_ref = bf16[4,256,128]{2,1,0:T(8,128)(2,1)} all-to-all(bf16[4,256,128]{2,1,0:T(8,128)(2,1)} %shard_map.83), channel_id=1, replica_groups=mesh['zh'=2,'y'=4,'c'=2,'z4'=4,'z2'=2,'x'=4] {'x'}, dimensions={0} | all-to-all | bytes 524288 | tf_op jit(solution)/shard_map/all_to_all | solution.py:257
  96.4 3.2 %shard_map.87 = bf16[16,4,16,256]{3,2,1,0:T(8,128)(2,1)} custom-call(s32[2]{0:T(128)} %pad_add_fusion.s_ref, bf16[4,256,128]{2,1,0:T(8,128)(2,1)} %all_to_all.20.g_ref, bf16[128,2048]{1,0:T(8,128)(2,1)} %shard_map.77.a0, bf16[128,2048]{1,0:T(8,128)(2,1)} %copy-done, bf16[128,2048]{1,0:T(8,128)(2,1)} %copy-done.1, bf16[128,2048]{1,0:T(8,128)(2,1)} %copy-done.2), custom_call_target="tpu_custom_call" | custom-call | flops 268435456 | bytes 2097152 | tf_op jit(solution)/shard_map/pallas_call | solution.py:48
  99.5 2.2 %collective-permute-start.7 = (bf16[16,4,16,256]{3,2,1,0:T(8,128)(2,1)}, bf16[16,4,16,256]{3,2,1,0:T(8,128)(2,1)S(1)}, u32[]{:S(2)}, u32[]{:S(2)}) collective-permute-start(bf16[16,4,16,256]{3,2,1,0:T(8,128)(2,1)} %shard_map.87), channel_id=1, source_target_pairs={{0,4},{4,0},{1,5},{5,1},{2,6},{6,2},{3,7},{7,3},{8,12},{12,8},{9,1... | collective-permute-start | bytes 1572872 | tf_op jit(solution)/shard_map/ppermute | solution.py:258
  101.7 3.4 %shard_map.86 = f32[16,4,16,256]{3,2,1,0:T(8,128)} custom-call(s32[2]{0:T(128)} %pad_add_fusion.s_ref, bf16[4,256,128]{2,1,0:T(8,128)(2,1)} %all_to_all.20.g_ref, bf16[128,2048]{1,0:T(8,128)(2,1)} %shard_map.77.a0, bf16[128,2048]{1,0:T(8,128)(2,1)} %copy-done, bf16[128,2048]{1,0:T(8,128)(2,1)} %copy-done.1, bf16[128,2048]{1,0:T(8,128)(2,1)} %copy-done.2), custom_call_target="tpu_custom_call" | custom-call | flops 268435456 | bytes 2097152 | tf_op jit(solution)/shard_map/pallas_call | solution.py:48
  105.1 7.2 %collective-permute-done.7 = bf16[16,4,16,256]{3,2,1,0:T(8,128)(2,1)S(1)} collective-permute-done((bf16[16,4,16,256]{3,2,1,0:T(8,128)(2,1)}, bf16[16,4,16,256]{3,2,1,0:T(8,128)(2,1)S(1)}, u32[]{:S(2)}, u32[]{:S(2)}) %collective-permute-start.7) | collective-permute-done | bytes 524320 | tf_op jit(solution)/shard_map/ppermute | solution.py:258
  112.3 2.2 %add_convert_fusion = bf16[16,4,16,256]{3,2,1,0:T(8,128)(2,1)} fusion(f32[16,4,16,256]{3,2,1,0:T(8,128)} %shard_map.86, bf16[16,4,16,256]{3,2,1,0:T(8,128)(2,1)S(1)} %collective-permute-done.7), kind=kLoop, calls=%fused_computation.1 | loop fusion | flops 786432 | bytes 2097152 | tf_op jit(solution)/shard_map/convert_element_type | solution.py:260
  114.5 18.5 %all-to-all-start.3 = ((bf16[64,16,256]{2,1,0:T(8,128)(2,1)}), bf16[64,16,256]{2,1,0:T(8,128)(2,1)S(1)}, u32[]{:S(2)}, u32[]{:S(2)}) async-start(bf16[64,16,256]{2,1,0:T(8,128)(2,1)} %bitcast.10), calls=%async_computation.3 | async-start | bytes 1048576 | tf_op jit(solution)/shard_map/all_to_all | solution.py:261
  133.0 3.4 %shard_map.84 = (bf16[64,2048]{1,0:T(8,128)(2,1)}, bf16[64,2048]{1,0:T(8,128)(2,1)}, bf16[64,2048]{1,0:T(8,128)(2,1)}, bf16[64,2048]{1,0:T(8,128)(2,1)}) custom-call(s32[2]{0:T(128)} %pad_add_fusion.s_ref, bf16[4,256,128]{2,1,0:T(8,128)(2,1)} %all_to_all.20.g_ref, bf16[16,4,16,256]{3,2,1,0:T(8,128)(2,1)} %bitcast.26, bf16[16,4,16,256]{3,2,1,0:T(8,128)(2,1)} %copy-done.4), custom_call_target="tpu_custom_call" | custom-call | flops 268435456 | bytes 2097152 | tf_op jit(solution)/shard_map/pallas_call | solution.py:48
  136.4 2.2 %collective-permute-start.4 = (bf16[64,2048]{1,0:T(8,128)(2,1)}, bf16[64,2048]{1,0:T(8,128)(2,1)S(1)}, u32[]{:S(2)}, u32[]{:S(2)}) collective-permute-start(bf16[64,2048]{1,0:T(8,128)(2,1)} %get-tuple-element.7), channel_id=1, source_target_pairs={{0,1},{1,0},{2,3},{3,2},{4,5},{5,4},{6,7},{7,6},{8,9},{9,8},{10,11... | collective-permute-start | bytes 786440 | tf_op jit(solution)/shard_map/ppermute | solution.py:241
  138.5 3.7 %collective-permute-start.5 = (bf16[64,2048]{1,0:T(8,128)(2,1)}, bf16[64,2048]{1,0:T(8,128)(2,1)S(1)}, u32[]{:S(2)}, u32[]{:S(2)}) collective-permute-start(bf16[64,2048]{1,0:T(8,128)(2,1)} %get-tuple-element.8), channel_id=1, source_target_pairs={{0,2},{1,3},{2,0},{3,1},{4,6},{5,7},{6,4},{7,5},{8,10},{9,11},{10,... | collective-permute-start | bytes 786440 | tf_op jit(solution)/shard_map/ppermute | solution.py:241
  142.3 3.7 %collective-permute-start.6 = (bf16[64,2048]{1,0:T(8,128)(2,1)}, bf16[64,2048]{1,0:T(8,128)(2,1)S(1)}, u32[]{:S(2)}, u32[]{:S(2)}) collective-permute-start(bf16[64,2048]{1,0:T(8,128)(2,1)} %get-tuple-element.9), channel_id=1, source_target_pairs={{0,3},{1,2},{2,1},{3,0},{4,7},{5,6},{6,5},{7,4},{8,11},{9,10},{10,... | collective-permute-start | bytes 786440 | tf_op jit(solution)/shard_map/ppermute | solution.py:241
  145.9 0.0 collective-permute-done.4.x1
  146.0 0.0 copy-start.6
  146.0 6.2 %collective-permute-done.5.x2 = bf16[64,2048]{1,0:T(8,128)(2,1)S(1)} collective-permute-done((bf16[64,2048]{1,0:T(8,128)(2,1)}, bf16[64,2048]{1,0:T(8,128)(2,1)S(1)}, u32[]{:S(2)}, u32[]{:S(2)}) %collective-permute-start.5) | collective-permute-done | bytes 262176 | tf_op jit(solution)/shard_map/ppermute | solution.py:241
  152.2 0.0 copy-start.7
  152.2 6.4 %collective-permute-done.6.x3 = bf16[64,2048]{1,0:T(8,128)(2,1)S(1)} collective-permute-done((bf16[64,2048]{1,0:T(8,128)(2,1)}, bf16[64,2048]{1,0:T(8,128)(2,1)S(1)}, u32[]{:S(2)}, u32[]{:S(2)}) %collective-permute-start.6) | collective-permute-done | bytes 262176 | tf_op jit(solution)/shard_map/ppermute | solution.py:241
  158.5 0.0 copy-start.8
  158.5 0.0 copy-done.6
  158.5 0.0 copy-done.7
  158.5 0.7 copy-done.8
  159.2 3.6 %shard_map.85 = bf16[64,128]{1,0:T(8,128)(2,1)} custom-call(s32[2]{0:T(128)} %pad_add_fusion.s_ref, bf16[64,2048]{1,0:T(8,128)(2,1)} %get-tuple-element.6.x0, bf16[64,2048]{1,0:T(8,128)(2,1)} %copy-done.6, bf16[64,2048]{1,0:T(8,128)(2,1)} %copy-done.7, bf16[64,2048]{1,0:T(8,128)(2,1)} %copy-done.8, bf16[4,2,4,256,128]{4,3,2,1,0:T(8,128)(2,1)} %bitcast.19), custom_call_target="tpu_custom_call" | custom-call | flops 134217728 | bytes 3145728 | tf_op jit(solution)/shard_map/pallas_call | solution.py:48
  162.8 0.0 all-to-all-done.3
  162.8 0.8 convert_reduce_fusion
Async XLA Ops:
  2.4 49.1 %all-to-all-start = ((bf16[64,16,256]{2,1,0:T(8,128)(2,1)}), bf16[64,16,256]{2,1,0:T(8,128)(2,1)S(1)}, u32[]{:S(2)}, u32[]{:S(2)}) async-start(bf16[64,16,256]{2,1,0:T(8,128)(2,1)} %bitcast.7), calls=%async_computation | async-start | bytes 1048576 | tf_op jit(solution)/shard_map/all_to_all | solution.py:249
  25.8 34.3 %collective-permute-start = (bf16[128,2048]{1,0:T(8,128)(2,1)}, bf16[128,2048]{1,0:T(8,128)(2,1)S(1)}, u32[]{:S(2)}, u32[]{:S(2)}) collective-permute-start(bf16[128,2048]{1,0:T(8,128)(2,1)} %shard_map.78), channel_id=1, source_target_pairs={{0,1},{1,0},{2,3},{3,2},{4,5},{5,4},{6,7},{7,6},{8,9},{9,8},{10,11... | collective-permute-start | bytes 1572872 | tf_op jit(solution)/shard_map/ppermute | solution.py:241
  32.0 28.2 %collective-permute-start.1 = (bf16[128,2048]{1,0:T(8,128)(2,1)}, bf16[128,2048]{1,0:T(8,128)(2,1)S(1)}, u32[]{:S(2)}, u32[]{:S(2)}) collective-permute-start(bf16[128,2048]{1,0:T(8,128)(2,1)} %shard_map.79), channel_id=1, source_target_pairs={{0,2},{1,3},{2,0},{3,1},{4,6},{5,7},{6,4},{7,5},{8,10},{9,11},{10,... | collective-permute-start | bytes 1572872 | tf_op jit(solution)/shard_map/ppermute | solution.py:241
  39.4 27.0 %collective-permute-start.2 = (bf16[128,2048]{1,0:T(8,128)(2,1)}, bf16[128,2048]{1,0:T(8,128)(2,1)S(1)}, u32[]{:S(2)}, u32[]{:S(2)}) collective-permute-start(bf16[128,2048]{1,0:T(8,128)(2,1)} %shard_map.80), channel_id=1, source_target_pairs={{0,3},{1,2},{2,1},{3,0},{4,7},{5,6},{6,5},{7,4},{8,11},{9,10},{10,... | collective-permute-start | bytes 1572872 | tf_op jit(solution)/shard_map/ppermute | solution.py:241
  51.4 8.7 %copy-start.3 = (bf16[64,16,256]{2,1,0:T(8,128)(2,1)}, bf16[64,16,256]{2,1,0:T(8,128)(2,1)S(1)}, u32[]{:S(2)}) copy-start(bf16[64,16,256]{2,1,0:T(8,128)(2,1)S(1)} %all-to-all-done) | copy-start | bytes 1572868
  51.4 19.1 %collective-permute-start.3 = (bf16[16,4,16,256]{3,2,1,0:T(8,128)(2,1)S(1)}, bf16[16,4,16,256]{3,2,1,0:T(8,128)(2,1)S(1)}, u32[]{:S(2)}, u32[]{:S(2)}) collective-permute-start(bf16[16,4,16,256]{3,2,1,0:T(8,128)(2,1)S(1)} %bitcast.24), channel_id=1, source_target_pairs={{0,4},{4,0},{1,5},{5,1},{2,6},{6,2},{3,7},{7,3},{8,12},{12,8},{9,1... | collective-permute-start | bytes 1572872 | tf_op jit(solution)/shard_map/ppermute | solution.py:253
  60.2 6.3 %copy-start = (bf16[128,2048]{1,0:T(8,128)(2,1)}, bf16[128,2048]{1,0:T(8,128)(2,1)S(1)}, u32[]{:S(2)}) copy-start(bf16[128,2048]{1,0:T(8,128)(2,1)S(1)} %collective-permute-done.a1) | copy-start | bytes 1572868
  60.2 6.2 %copy-start.1 = (bf16[128,2048]{1,0:T(8,128)(2,1)}, bf16[128,2048]{1,0:T(8,128)(2,1)S(1)}, u32[]{:S(2)}) copy-start(bf16[128,2048]{1,0:T(8,128)(2,1)S(1)} %collective-permute-done.1.a2) | copy-start | bytes 1572868
  66.4 0.8 copy-start.2
  70.5 0.8 copy-start.4
  74.7 9.4 %all-to-all-start.1 = ((bf16[4,128,256]{2,1,0:T(8,128)(2,1)}), bf16[4,128,256]{2,1,0:T(8,128)(2,1)S(1)}, u32[]{:S(2)}, u32[]{:S(2)}) async-start(bf16[4,128,256]{2,1,0:T(8,128)(2,1)} %shard_map.82), calls=%async_computation.1 | async-start | bytes 524288 | tf_op jit(solution)/shard_map/all_to_all | solution.py:256
  84.1 0.7 copy-start.5
  99.5 12.7 %collective-permute-start.7 = (bf16[16,4,16,256]{3,2,1,0:T(8,128)(2,1)}, bf16[16,4,16,256]{3,2,1,0:T(8,128)(2,1)S(1)}, u32[]{:S(2)}, u32[]{:S(2)}) collective-permute-start(bf16[16,4,16,256]{3,2,1,0:T(8,128)(2,1)} %shard_map.87), channel_id=1, source_target_pairs={{0,4},{4,0},{1,5},{5,1},{2,6},{6,2},{3,7},{7,3},{8,12},{12,8},{9,1... | collective-permute-start | bytes 1572872 | tf_op jit(solution)/shard_map/ppermute | solution.py:258
  114.5 48.4 %all-to-all-start.3 = ((bf16[64,16,256]{2,1,0:T(8,128)(2,1)}), bf16[64,16,256]{2,1,0:T(8,128)(2,1)S(1)}, u32[]{:S(2)}, u32[]{:S(2)}) async-start(bf16[64,16,256]{2,1,0:T(8,128)(2,1)} %bitcast.10), calls=%async_computation.3 | async-start | bytes 1048576 | tf_op jit(solution)/shard_map/all_to_all | solution.py:261
  136.4 9.6 %collective-permute-start.4 = (bf16[64,2048]{1,0:T(8,128)(2,1)}, bf16[64,2048]{1,0:T(8,128)(2,1)S(1)}, u32[]{:S(2)}, u32[]{:S(2)}) collective-permute-start(bf16[64,2048]{1,0:T(8,128)(2,1)} %get-tuple-element.7), channel_id=1, source_target_pairs={{0,1},{1,0},{2,3},{3,2},{4,5},{5,4},{6,7},{7,6},{8,9},{9,8},{10,11... | collective-permute-start | bytes 786440 | tf_op jit(solution)/shard_map/ppermute | solution.py:241
  138.5 13.6 %collective-permute-start.5 = (bf16[64,2048]{1,0:T(8,128)(2,1)}, bf16[64,2048]{1,0:T(8,128)(2,1)S(1)}, u32[]{:S(2)}, u32[]{:S(2)}) collective-permute-start(bf16[64,2048]{1,0:T(8,128)(2,1)} %get-tuple-element.8), channel_id=1, source_target_pairs={{0,2},{1,3},{2,0},{3,1},{4,6},{5,7},{6,4},{7,5},{8,10},{9,11},{10,... | collective-permute-start | bytes 786440 | tf_op jit(solution)/shard_map/ppermute | solution.py:241
  142.3 16.3 %collective-permute-start.6 = (bf16[64,2048]{1,0:T(8,128)(2,1)}, bf16[64,2048]{1,0:T(8,128)(2,1)S(1)}, u32[]{:S(2)}, u32[]{:S(2)}) collective-permute-start(bf16[64,2048]{1,0:T(8,128)(2,1)} %get-tuple-element.9), channel_id=1, source_target_pairs={{0,3},{1,2},{2,1},{3,0},{4,7},{5,6},{6,5},{7,4},{8,11},{9,10},{10,... | collective-permute-start | bytes 786440 | tf_op jit(solution)/shard_map/ppermute | solution.py:241
  146.0 12.6 %copy-start.6 = (bf16[64,2048]{1,0:T(8,128)(2,1)}, bf16[64,2048]{1,0:T(8,128)(2,1)S(1)}, u32[]{:S(2)}) copy-start(bf16[64,2048]{1,0:T(8,128)(2,1)S(1)} %collective-permute-done.4.x1) | copy-start | bytes 786436
  152.2 6.4 %copy-start.7 = (bf16[64,2048]{1,0:T(8,128)(2,1)}, bf16[64,2048]{1,0:T(8,128)(2,1)S(1)}, u32[]{:S(2)}) copy-start(bf16[64,2048]{1,0:T(8,128)(2,1)S(1)} %collective-permute-done.5.x2) | copy-start | bytes 786436
  158.5 0.7 copy-start.8

commit v3 on v2

v3 whole, which is shorter than its diff:
```python
import functools
import math

import jax
import jax.numpy as jnp
from jax import lax
from jax.experimental import pallas as pl
from jax.experimental.pallas import tpu as pltpu
from jax.sharding import Mesh, PartitionSpec as P

NBR_LEN = 128
HEAD = 128
GROUP = 64
PAIR = 2 * GROUP
ROWS = 256
BLOCK = 256
HALF = 4 * BLOCK
INV = 1.0 / math.sqrt(HEAD)
F32 = jnp.float32
BF16 = jnp.bfloat16

SECTION = ("zh", "y", "c")
TENSOR = ("z4", "z2", "x")
SPREAD = ("zh", "y", "c", "z4")
FLIP = [(0, 1), (1, 0)]


def across(k):
    return [(i, i ^ k) for i in range(4)]


def nt(a, b):
    return lax.dot_general(a, b, (((1,), (1,)), ((), ())), preferred_element_type=F32)


def nn(a, b):
    return jnp.dot(a, b, preferred_element_type=F32)


def cost(flops, nbytes):
    return pl.CostEstimate(flops=flops, bytes_accessed=nbytes, transcendentals=0)


def full(shape):
    return pl.BlockSpec(shape, lambda i, s: (0,) * len(shape))


VMEM = pl.BlockSpec(memory_space=pltpu.VMEM)
SMEM = pl.BlockSpec(memory_space=pltpu.SMEM)
LIMIT = pltpu.CompilerParams(vmem_limit_bytes=16 << 20)


def whole(kernel, n_args, out_shape, estimate):
    return pl.pallas_call(
        kernel,
        in_specs=[SMEM] + [VMEM] * n_args,
        out_specs=jax.tree.map(lambda _: VMEM, out_shape),
        out_shape=out_shape,
        cost_estimate=estimate,
        compiler_params=LIMIT,
    )


def streamed(kernel, in_specs, out_specs, out_shape, estimate, scratch=()):
    return pl.pallas_call(
        kernel,
        grid_spec=pltpu.PrefetchScalarGridSpec(
            num_scalar_prefetch=1,
            grid=(4,),
            in_specs=in_specs,
            out_specs=out_specs,
            scratch_shapes=scratch,
        ),
        out_shape=out_shape,
        cost_estimate=estimate,
        compiler_params=LIMIT,
    )


W_SPEC = pl.BlockSpec((1, 2, 4, BLOCK, HEAD), lambda i, s: (i, 0, 0, 0, 0))
E_SHAPE = (16, 4, 16, BLOCK)


def block_at(p, b):
    return pl.ds(pl.multiple_of(p * HALF + b * BLOCK, BLOCK), BLOCK)


def project_kernel(s_ref, q_ref, ct_ref, wk_ref, wv_ref, *out_refs):
    b = pl.program_id(0)
    for k in range(4):
        for p in range(2):
            key, value = (w[0, s_ref[0] ^ p, s_ref[1] ^ k] for w in (wk_ref, wv_ref))
            out_refs[k][0:GROUP, block_at(p, b)] = nt(q_ref[...], key).astype(BF16)
            out_refs[k][GROUP:PAIR, block_at(p, b)] = nt(ct_ref[...], value).astype(BF16)


def project(scalars, q, ct, wk, wv):
    small = full((GROUP, HEAD))
    return streamed(
        project_kernel,
        [small, small, W_SPEC, W_SPEC],
        [full((PAIR, 2 * HALF))] * 4,
        [jax.ShapeDtypeStruct((PAIR, 2 * HALF), BF16)] * 4,
        cost(2 * 128 * 8192 * 128, 6 << 20),
    )(scalars, q, ct, wk, wv)


def heads(a_refs, p, b):
    at = p * HALF + b * BLOCK
    return jnp.concatenate([r[:, at : at + BLOCK] for r in a_refs], axis=0)


def partial_scores(a_refs, e_ref, p):
    total = None
    for b in range(4):
        part = nt(heads(a_refs, p, b), e_ref[:, b].reshape(ROWS, BLOCK))
        total = part if total is None else total + part
    return total


def first_scores_kernel(s_ref, a0, a1, a2, a3, e_ref, out_ref):
    out_ref[...] = partial_scores((a0, a1, a2, a3), e_ref, 0)


def last_scores_kernel(s_ref, a0, a1, a2, a3, e_ref, first_ref, out_ref):
    total = first_ref[...] + partial_scores((a0, a1, a2, a3), e_ref, 1)
    for k in range(4):
        out_ref[s_ref[1] ^ k] = total[k * PAIR : (k + 1) * PAIR].astype(BF16)


HALF_COST = cost(2 * 512 * 1024 * 256, 2 << 20)


def first_scores(scalars, a, e):
    out = jax.ShapeDtypeStruct((4 * PAIR, ROWS), F32)
    return whole(first_scores_kernel, 5, out, HALF_COST)(scalars, *a, e)


def last_scores(scalars, a, e, first):
    out = jax.ShapeDtypeStruct((4, PAIR, ROWS), BF16)
    return whole(last_scores_kernel, 6, out, HALF_COST)(scalars, *a, e, first)


def attend_kernel(count_ref, s_ref, out_ref):
    total = s_ref[0].astype(F32)
    for k in range(1, 4):
        total = total + s_ref[k].astype(F32)
    scores = total[0:GROUP] * INV
    grad_probs = total[GROUP:PAIR]
    count = count_ref[0]
    row = lax.broadcasted_iota(jnp.int32, scores.shape, 1)
    weighted = jnp.where(row < count * NBR_LEN, jnp.exp(scores), 0.0)
    empty = jnp.where(count == 0, 1.0, 0.0)
    probs = weighted / (jnp.sum(weighted, axis=1, keepdims=True) + empty)
    centre = jnp.sum(probs * grad_probs, axis=1, keepdims=True)
    grad_scores = probs * (grad_probs - centre) * INV
    both = jnp.concatenate([grad_scores, probs], axis=0).T.astype(BF16)
    for k in range(4):
        out_ref[k] = both


def attend(counts, s):
    out = jax.ShapeDtypeStruct((4, ROWS, PAIR), BF16)
    return whole(attend_kernel, 1, out, cost(1 << 20, 1 << 19))(counts, s)


def term_kernel(p, s_ref, g_ref, a0, a1, a2, a3, out_ref):
    g = jnp.concatenate([g_ref[s_ref[1] ^ k] for k in range(4)], axis=1)
    for b in range(4):
        part = nn(g, heads((a0, a1, a2, a3), p, b))
        out_ref[:, b] = part.astype(out_ref.dtype).reshape(16, 16, BLOCK)


def term(scalars, g, a, p, kind):
    out = jax.ShapeDtypeStruct(E_SHAPE, kind)
    return whole(functools.partial(term_kernel, p), 5, out, HALF_COST)(scalars, g, *a)


def mix_kernel(s_ref, g_ref, own_ref, other_ref, *out_refs):
    gs = jnp.concatenate([g_ref[s_ref[1] ^ k, :, 0:GROUP] for k in range(4)], axis=1)
    gs = gs.astype(F32).T.astype(BF16)
    for p, e_ref in enumerate((own_ref, other_ref)):
        for b in range(4):
            part = nn(gs, e_ref[:, b].reshape(ROWS, BLOCK)).astype(BF16)
            at = p * HALF + b * BLOCK
            for k in range(4):
                out_refs[k][:, at : at + BLOCK] = part[k * GROUP : (k + 1) * GROUP]


def mix(scalars, g, own, other):
    out = [jax.ShapeDtypeStruct((GROUP, 2 * HALF), BF16)] * 4
    return whole(mix_kernel, 3, out, cost(2 * 256 * 256 * 2048, 2 << 20))(scalars, g, own, other)


def query_kernel(s_ref, x0, x1, x2, x3, w_ref, out_ref, acc_ref):
    b = pl.program_id(0)
    total = None
    for k, x_ref in enumerate((x0, x1, x2, x3)):
        for p in range(2):
            part = nn(x_ref[:, block_at(p, b)], w_ref[0, s_ref[0] ^ p, s_ref[1] ^ k])
            total = part if total is None else total + part

    @pl.when(b == 0)
    def _():
        acc_ref[...] = total

    @pl.when(b > 0)
    def _():
        acc_ref[...] += total

    @pl.when(b == 3)
    def _():
        out_ref[...] = acc_ref[...].astype(BF16)


def query(scalars, x, wk):
    return streamed(
        query_kernel,
        [full((GROUP, 2 * HALF))] * 4 + [W_SPEC],
        full((GROUP, HEAD)),
        jax.ShapeDtypeStruct((GROUP, HEAD), BF16),
        cost(2 * 64 * 8192 * 128, 3 << 20),
        [pltpu.VMEM((GROUP, HEAD), F32)],
    )(scalars, *x, wk)


def to_members(parts):
    return [parts[0]] + [lax.ppermute(parts[k], "x", across(k)) for k in range(1, 4)]


def local(encoded, w_key, w_value, queries, cotangent, counts):
    scalars = jnp.stack([lax.axis_index("z2"), lax.axis_index("x")]).astype(jnp.int32)
    wk = w_key.reshape(4, 2, 4, BLOCK, HEAD)
    wv = w_value.reshape(4, 2, 4, BLOCK, HEAD)
    out_rows = jnp.broadcast_to(encoded[:, None], (16, 4, 16, BLOCK)).reshape(64, 16, BLOCK)
    own = lax.all_to_all(out_rows, SPREAD, 0, 0, tiled=True).reshape(16, 4, 16, BLOCK)
    shared = to_members(project(scalars, queries[0], cotangent[0], wk, wv))
    other = lax.ppermute(own, "z2", FLIP)
    first = first_scores(scalars, shared, own)
    sums = last_scores(scalars, shared, other, first)
    parts = lax.all_to_all(sums, "x", 0, 0, tiled=True)
    grads = lax.all_to_all(attend(counts.reshape(1), parts), "x", 0, 0, tiled=True)
    passed = lax.ppermute(term(scalars, grads, shared, 1, BF16), "z2", FLIP)
    kept = term(scalars, grads, shared, 0, F32)
    mixture = mix(scalars, grads, own, other)
    kept, mixture = lax.optimization_barrier((kept, mixture))
    sent = (kept + passed.astype(F32)).astype(BF16).reshape(64, 16, BLOCK)
    terms = lax.all_to_all(sent, SPREAD, 0, 0, tiled=True).reshape(16, 4, 16, BLOCK)
    mixed = to_members(mixture)
    grad_queries = query(scalars, mixed, wk)
    grad_encoded = jnp.sum(terms.astype(F32), axis=1)
    return grad_queries[None], grad_encoded


def solution(mesh):
    fine = Mesh(mesh.devices.reshape(2, 4, 2, 4, 2, 4), ("zh", "y", "c", "z4", "z2", "x"))
    by_head = P(SECTION, None, TENSOR)
    return jax.shard_map(
        local,
        mesh=fine,
        in_specs=(P(None, SECTION, TENSOR), by_head, by_head, by_head, by_head, P(SECTION, None)),
        out_specs=(by_head, P(None, SECTION, TENSOR)),
        check_vma=False,
    )
```

time: 167 us -> 153 us (0.916)
  the two profiles are of different devices: /device:TPU:1 before, /device:TPU:8 now
where the time goes in v3:
time: 153 us; the launch traced here: 152 us
  starting transfers between devices  63.1 us (41%)
  waiting for transfers between devices  56.5 us (37%)
  Pallas kernels  11.8 us (8%)
  blocking collectives  9.07 us (6%)
  local copies, waits for them, and re-layouts  7.09 us (5%)
  other arithmetic  2.9 us (2%)
    ppermute x6, waiting for transfers between devices, to_members(): lax.ppermute(parts[k], 'x', across(k))  20.8 us
    ppermute x6, starting transfers between devices, to_members(): lax.ppermute(parts[k], 'x', across(k))  20.8 us
    all_to_all x1, starting transfers between devices, local(): lax.all_to_all(out_rows, SPREAD, 0, 0, tiled=True).reshape(16, 4, 16, BLOCK)  18.7 us
    all_to_all x1, waiting for transfers between devices, local(): lax.all_to_all(out_rows, SPREAD, 0, 0, tiled=True).reshape(16, 4, 16, BLOCK)  14.5 us
    all_to_all x1, starting transfers between devices, local(): lax.all_to_all(sent, SPREAD, 0, 0, tiled=True).reshape(16, 4, 16, BLOCK)  13.7 us
    all_to_all x1, blocking collectives, local(): lax.all_to_all(attend(counts.reshape(1), parts), 'x', 0, 0, tiled=True)  9.07 us
    all_to_all x1, waiting for transfers between devices, local(): lax.all_to_all(sent, SPREAD, 0, 0, tiled=True).reshape(16, 4, 16, BLOCK)  8.81 us
    all_to_all x1, waiting for transfers between devices, local(): parts = lax.all_to_all(sums, 'x', 0, 0, tiled=True)  6.03 us
  transfers between devices with their start and end apart: 11, of which 10 were waited for; matrix products, arithmetic and copies ran while one was open for 0% of the time, Pallas kernels for 6%

profile of v3, /device:TPU:8, one launch (start us, length us, event | category | flops | bytes accessed | tf_op | source)
XLA Modules:
  0.0 151.9 jit_solution(35648003687342925)
XLA Ops:
  0.6 1.8 %broadcast_in_dim.4 = bf16[16,4,16,256]{3,2,1,0:T(8,128)(2,1)} broadcast(bf16[16,16,256]{2,1,0:T(8,128)(2,1)} %param.6), dimensions={0,2,3} | broadcast | bytes 655360 | tf_op jit(solution)/shard_map/broadcast_in_dim | solution.py:235
  2.4 18.7 %all-to-all-start = ((bf16[64,16,256]{2,1,0:T(8,128)(2,1)}), bf16[64,16,256]{2,1,0:T(8,128)(2,1)S(1)}, u32[]{:S(2)}, u32[]{:S(2)}) async-start(bf16[64,16,256]{2,1,0:T(8,128)(2,1)} %bitcast.7), calls=%async_computation | async-start | bytes 1048576 | tf_op jit(solution)/shard_map/all_to_all | solution.py:236
  21.1 0.1 pad_add_fusion.s_ref
  21.2 0.0 copy-start
  21.2 1.6 %copy-done = bf16[1,8192,128]{2,1,0:T(8,128)(2,1)S(1)} copy-done((bf16[1,8192,128]{2,1,0:T(8,128)(2,1)S(1)}, bf16[1,8192,128]{2,1,0:T(8,128)(2,1)}, u32[]{:S(2)}) %copy-start) | copy-done | bytes 2097176
  22.8 0.0 copy-start.2
  22.8 1.6 %copy-done.2 = bf16[1,8192,128]{2,1,0:T(8,128)(2,1)S(1)} copy-done((bf16[1,8192,128]{2,1,0:T(8,128)(2,1)S(1)}, bf16[1,8192,128]{2,1,0:T(8,128)(2,1)}, u32[]{:S(2)}) %copy-start.2) | copy-done | bytes 2097176
  24.4 0.0 copy-start.3
  24.4 0.7 copy-done.3
  25.1 0.0 copy-start.4
  25.1 0.7 copy-done.4
  25.8 3.5 %shard_map.77 = (bf16[128,2048]{1,0:T(8,128)(2,1)S(1)}, bf16[128,2048]{1,0:T(8,128)(2,1)}, bf16[128,2048]{1,0:T(8,128)(2,1)}, bf16[128,2048]{1,0:T(8,128)(2,1)}) custom-call(s32[2]{0:T(128)S(1)} %pad_add_fusion.s_ref, bf16[64,128]{1,0:T(8,128)(2,1)S(1)} %bitcast.21, bf16[64,128]{1,0:T(8,128)(2,1)S(1)} %bitcast.22, bf16[4,2,4,256,128]{4,3,2,1,0:T(8,128)(2,1)S(1)} %bitcast.15, ...), custom_call_target="tpu_custom_call" | custom-call | flops 268435456 | bytes 6291456 | tf_op jit(solution)/shard_map/pallas_call | solution.py:99
  29.4 3.4 %collective-permute-start = (bf16[128,2048]{1,0:T(8,128)(2,1)}, bf16[128,2048]{1,0:T(8,128)(2,1)S(1)}, u32[]{:S(2)}, u32[]{:S(2)}) collective-permute-start(bf16[128,2048]{1,0:T(8,128)(2,1)} %get-tuple-element.16), channel_id=1, source_target_pairs={{0,1},{1,0},{2,3},{3,2},{4,5},{5,4},{6,7},{7,6},{8,9},{9,8},{10,11... | collective-permute-start | bytes 1572872 | tf_op jit(solution)/shard_map/ppermute | solution.py:228
  32.8 4.6 %collective-permute-start.1 = (bf16[128,2048]{1,0:T(8,128)(2,1)}, bf16[128,2048]{1,0:T(8,128)(2,1)S(1)}, u32[]{:S(2)}, u32[]{:S(2)}) collective-permute-start(bf16[128,2048]{1,0:T(8,128)(2,1)} %get-tuple-element.17), channel_id=1, source_target_pairs={{0,2},{1,3},{2,0},{3,1},{4,6},{5,7},{6,4},{7,5},{8,10},{9,11},{10,... | collective-permute-start | bytes 1572872 | tf_op jit(solution)/shard_map/ppermute | solution.py:228
  37.4 2.4 %collective-permute-start.2 = (bf16[128,2048]{1,0:T(8,128)(2,1)}, bf16[128,2048]{1,0:T(8,128)(2,1)S(1)}, u32[]{:S(2)}, u32[]{:S(2)}) collective-permute-start(bf16[128,2048]{1,0:T(8,128)(2,1)} %get-tuple-element.18), channel_id=1, source_target_pairs={{0,3},{1,2},{2,1},{3,0},{4,7},{5,6},{6,5},{7,4},{8,11},{9,10},{10,... | collective-permute-start | bytes 1572872 | tf_op jit(solution)/shard_map/ppermute | solution.py:228
  39.8 14.5 %all-to-all-done = bf16[64,16,256]{2,1,0:T(8,128)(2,1)S(1)} async-done(((bf16[64,16,256]{2,1,0:T(8,128)(2,1)}), bf16[64,16,256]{2,1,0:T(8,128)(2,1)S(1)}, u32[]{:S(2)}, u32[]{:S(2)}) %all-to-all-start) | async-done | bytes 524320 | tf_op jit(solution)/shard_map/all_to_all | solution.py:236
  54.3 1.9 %collective-permute-start.3 = (bf16[16,4,16,256]{3,2,1,0:T(8,128)(2,1)S(1)}, bf16[16,4,16,256]{3,2,1,0:T(8,128)(2,1)S(1)}, u32[]{:S(2)}, u32[]{:S(2)}) collective-permute-start(bf16[16,4,16,256]{3,2,1,0:T(8,128)(2,1)S(1)} %bitcast.17), channel_id=1, source_target_pairs={{0,4},{4,0},{1,5},{5,1},{2,6},{6,2},{3,7},{7,3},{8,12},{12,8},{9,1... | collective-permute-start | bytes 1572872 | tf_op jit(solution)/shard_map/ppermute | solution.py:238
  56.2 0.0 collective-permute-done.a1
  56.2 2.8 %collective-permute-done.1.a2 = bf16[128,2048]{1,0:T(8,128)(2,1)S(1)} collective-permute-done((bf16[128,2048]{1,0:T(8,128)(2,1)}, bf16[128,2048]{1,0:T(8,128)(2,1)S(1)}, u32[]{:S(2)}, u32[]{:S(2)}) %collective-permute-start.1) | collective-permute-done | bytes 524320 | tf_op jit(solution)/shard_map/ppermute | solution.py:228
  59.0 6.4 %collective-permute-done.2.a3 = bf16[128,2048]{1,0:T(8,128)(2,1)S(1)} collective-permute-done((bf16[128,2048]{1,0:T(8,128)(2,1)}, bf16[128,2048]{1,0:T(8,128)(2,1)S(1)}, u32[]{:S(2)}, u32[]{:S(2)}) %collective-permute-start.2) | collective-permute-done | bytes 524320 | tf_op jit(solution)/shard_map/ppermute | solution.py:228
  65.4 1.0 shard_map.78.first_ref
  66.4 1.2 collective-permute-done.3.e_ref.other_ref
  67.6 1.7 %shard_map.79 = bf16[4,128,256]{2,1,0:T(8,128)(2,1)} custom-call(s32[2]{0:T(128)S(1)} %pad_add_fusion.s_ref, bf16[128,2048]{1,0:T(8,128)(2,1)S(1)} %get-tuple-element.15.a0, bf16[128,2048]{1,0:T(8,128)(2,1)S(1)} %collective-permute-done.a1, bf16[128,2048]{1,0:T(8,128)(2,1)S(1)} %collective-permute-done.1.a2, ...), custom_call_target="tpu_custom_call" | custom-call | flops 268435456 | bytes 2097152 | tf_op jit(solution)/shard_map/pallas_call | solution.py:141
  69.4 4.3 %all-to-all-start.1 = ((bf16[4,128,256]{2,1,0:T(8,128)(2,1)}), bf16[4,128,256]{2,1,0:T(8,128)(2,1)S(1)}, u32[]{:S(2)}, u32[]{:S(2)}) async-start(bf16[4,128,256]{2,1,0:T(8,128)(2,1)} %shard_map.79), calls=%async_computation.1 | async-start | bytes 524288 | tf_op jit(solution)/shard_map/all_to_all | solution.py:241
  74.3 6.0 %all-to-all-done.1.s_ref = bf16[4,128,256]{2,1,0:T(8,128)(2,1)S(1)} async-done(((bf16[4,128,256]{2,1,0:T(8,128)(2,1)}), bf16[4,128,256]{2,1,0:T(8,128)(2,1)S(1)}, u32[]{:S(2)}, u32[]{:S(2)}) %all-to-all-start.1) | async-done | bytes 262176 | tf_op jit(solution)/shard_map/all_to_all | solution.py:241
  80.3 0.3 shard_map.80
  80.6 9.1 %all_to_all.20.g_ref = bf16[4,256,128]{2,1,0:T(8,128)(2,1)S(1)} all-to-all(bf16[4,256,128]{2,1,0:T(8,128)(2,1)S(1)} %shard_map.80), channel_id=1, replica_groups=mesh['zh'=2,'y'=4,'c'=2,'z4'=4,'z2'=2,'x'=4] {'x'}, dimensions={0} | all-to-all | bytes 524288 | tf_op jit(solution)/shard_map/all_to_all | solution.py:242
  89.7 1.0 shard_map.84
  90.7 3.7 %collective-permute-start.7 = (bf16[16,4,16,256]{3,2,1,0:T(8,128)(2,1)S(1)}, bf16[16,4,16,256]{3,2,1,0:T(8,128)(2,1)S(1)}, u32[]{:S(2)}, u32[]{:S(2)}) collective-permute-start(bf16[16,4,16,256]{3,2,1,0:T(8,128)(2,1)S(1)} %shard_map.84), channel_id=1, source_target_pairs={{0,4},{4,0},{1,5},{5,1},{2,6},{6,2},{3,7},{7,3},{8,12},{12,8},{9,1... | collective-permute-start | bytes 1572872 | tf_op jit(solution)/shard_map/ppermute | solution.py:243
  94.3 1.1 shard_map.82
  95.4 0.0 copy-start.7
  95.5 0.7 copy-done.7
  96.2 0.0 copy-start.5
  96.2 0.0 copy-start.6
  96.2 1.0 shard_map.81
  97.1 0.0 copy-start.8
  97.1 0.0 copy-start.1
  97.2 5.2 %collective-permute-done.7 = bf16[16,4,16,256]{3,2,1,0:T(8,128)(2,1)S(1)} collective-permute-done((bf16[16,4,16,256]{3,2,1,0:T(8,128)(2,1)S(1)}, bf16[16,4,16,256]{3,2,1,0:T(8,128)(2,1)S(1)}, u32[]{:S(2)}, u32[]{:S(2)}) %collective-permute-start.7) | collective-permute-done | bytes 524320 | tf_op jit(solution)/shard_map/ppermute | solution.py:243
  102.3 1.0 add_convert_fusion
  103.3 0.0 copy-done.5
  103.3 0.0 copy-done.6
  103.3 13.7 %all-to-all-start.3 = ((bf16[64,16,256]{2,1,0:T(8,128)(2,1)}), bf16[64,16,256]{2,1,0:T(8,128)(2,1)}, u32[]{:S(2)}, u32[]{:S(2)}) async-start(bf16[64,16,256]{2,1,0:T(8,128)(2,1)} %bitcast.10), calls=%async_computation.3 | async-start | bytes 1048576 | tf_op jit(solution)/shard_map/all_to_all | solution.py:248
  117.0 0.0 copy-done.8
  117.0 2.5 %collective-permute-start.4 = (bf16[64,2048]{1,0:T(8,128)(2,1)S(1)}, bf16[64,2048]{1,0:T(8,128)(2,1)S(1)}, u32[]{:S(2)}, u32[]{:S(2)}) collective-permute-start(bf16[64,2048]{1,0:T(8,128)(2,1)S(1)} %copy-done.8), channel_id=1, source_target_pairs={{0,1},{1,0},{2,3},{3,2},{4,5},{5,4},{6,7},{7,6},{8,9},{9,8},{10,11... | collective-permute-start | bytes 786440 | tf_op jit(solution)/shard_map/ppermute | solution.py:228
  119.5 4.0 %collective-permute-start.5 = (bf16[64,2048]{1,0:T(8,128)(2,1)}, bf16[64,2048]{1,0:T(8,128)(2,1)S(1)}, u32[]{:S(2)}, u32[]{:S(2)}) collective-permute-start(bf16[64,2048]{1,0:T(8,128)(2,1)} %copy-done.6), channel_id=1, source_target_pairs={{0,2},{1,3},{2,0},{3,1},{4,6},{5,7},{6,4},{7,5},{8,10},{9,11},{10,... | collective-permute-start | bytes 786440 | tf_op jit(solution)/shard_map/ppermute | solution.py:228
  123.5 4.0 %collective-permute-start.6 = (bf16[64,2048]{1,0:T(8,128)(2,1)}, bf16[64,2048]{1,0:T(8,128)(2,1)S(1)}, u32[]{:S(2)}, u32[]{:S(2)}) collective-permute-start(bf16[64,2048]{1,0:T(8,128)(2,1)} %copy-done.5), channel_id=1, source_target_pairs={{0,3},{1,2},{2,1},{3,0},{4,7},{5,6},{6,5},{7,4},{8,11},{9,10},{10,... | collective-permute-start | bytes 786440 | tf_op jit(solution)/shard_map/ppermute | solution.py:228
  127.5 0.6 collective-permute-done.4.x1
  128.1 5.5 %collective-permute-done.5.x2 = bf16[64,2048]{1,0:T(8,128)(2,1)S(1)} collective-permute-done((bf16[64,2048]{1,0:T(8,128)(2,1)}, bf16[64,2048]{1,0:T(8,128)(2,1)S(1)}, u32[]{:S(2)}, u32[]{:S(2)}) %collective-permute-start.5) | collective-permute-done | bytes 262176 | tf_op jit(solution)/shard_map/ppermute | solution.py:228
  133.6 5.5 %collective-permute-done.6.x3 = bf16[64,2048]{1,0:T(8,128)(2,1)S(1)} collective-permute-done((bf16[64,2048]{1,0:T(8,128)(2,1)}, bf16[64,2048]{1,0:T(8,128)(2,1)S(1)}, u32[]{:S(2)}, u32[]{:S(2)}) %collective-permute-start.6) | collective-permute-done | bytes 262176 | tf_op jit(solution)/shard_map/ppermute | solution.py:228
  139.1 0.0 copy-done.1
  139.1 2.1 %shard_map.83 = bf16[64,128]{1,0:T(8,128)(2,1)} custom-call(s32[2]{0:T(128)S(1)} %pad_add_fusion.s_ref, bf16[64,2048]{1,0:T(8,128)(2,1)S(1)} %get-tuple-element.23.x0, bf16[64,2048]{1,0:T(8,128)(2,1)S(1)} %collective-permute-done.4.x1, bf16[64,2048]{1,0:T(8,128)(2,1)S(1)} %collective-permute-done.5.x2, bf16[64,2048]{1,0:T(8,128)(2,1)S(1)} %collective-permute-done.6.x3, ...), custom_call_target="tpu_custom_call" | custom-call | flops 134217728 | bytes 3145728 | tf_op jit(solution)/shard_map/pallas_call | solution.py:217
  141.3 8.8 %all-to-all-done.3 = bf16[64,16,256]{2,1,0:T(8,128)(2,1)} async-done(((bf16[64,16,256]{2,1,0:T(8,128)(2,1)}), bf16[64,16,256]{2,1,0:T(8,128)(2,1)}, u32[]{:S(2)}, u32[]{:S(2)}) %all-to-all-start.3) | async-done | bytes 524320 | tf_op jit(solution)/shard_map/all_to_all | solution.py:248
  150.1 1.8 %convert_reduce_fusion = f32[16,16,256]{2,1,0:T(8,128)} fusion(bf16[64,16,256]{2,1,0:T(8,128)(2,1)} %all-to-all-done.3), kind=kLoop, calls=%fused_computation | loop fusion | flops 458752 | bytes 786432 | tf_op jit(solution)/shard_map/reduce_sum | solution.py:251
Async XLA Ops:
  2.4 51.9 %all-to-all-start = ((bf16[64,16,256]{2,1,0:T(8,128)(2,1)}), bf16[64,16,256]{2,1,0:T(8,128)(2,1)S(1)}, u32[]{:S(2)}, u32[]{:S(2)}) async-start(bf16[64,16,256]{2,1,0:T(8,128)(2,1)} %bitcast.7), calls=%async_computation | async-start | bytes 1048576 | tf_op jit(solution)/shard_map/all_to_all | solution.py:236
  21.2 1.6 %copy-start = (bf16[1,8192,128]{2,1,0:T(8,128)(2,1)S(1)}, bf16[1,8192,128]{2,1,0:T(8,128)(2,1)}, u32[]{:S(2)}) copy-start(bf16[1,8192,128]{2,1,0:T(8,128)(2,1)} %param.7) | copy-start | bytes 6291460
  22.8 1.6 %copy-start.2 = (bf16[1,8192,128]{2,1,0:T(8,128)(2,1)S(1)}, bf16[1,8192,128]{2,1,0:T(8,128)(2,1)}, u32[]{:S(2)}) copy-start(bf16[1,8192,128]{2,1,0:T(8,128)(2,1)} %param.8) | copy-start | bytes 6291460
  24.4 0.7 copy-start.3
  25.1 0.7 copy-start.4
  29.4 26.8 %collective-permute-start = (bf16[128,2048]{1,0:T(8,128)(2,1)}, bf16[128,2048]{1,0:T(8,128)(2,1)S(1)}, u32[]{:S(2)}, u32[]{:S(2)}) collective-permute-start(bf16[128,2048]{1,0:T(8,128)(2,1)} %get-tuple-element.16), channel_id=1, source_target_pairs={{0,1},{1,0},{2,3},{3,2},{4,5},{5,4},{6,7},{7,6},{8,9},{9,8},{10,11... | collective-permute-start | bytes 1572872 | tf_op jit(solution)/shard_map/ppermute | solution.py:228
  32.8 26.2 %collective-permute-start.1 = (bf16[128,2048]{1,0:T(8,128)(2,1)}, bf16[128,2048]{1,0:T(8,128)(2,1)S(1)}, u32[]{:S(2)}, u32[]{:S(2)}) collective-permute-start(bf16[128,2048]{1,0:T(8,128)(2,1)} %get-tuple-element.17), channel_id=1, source_target_pairs={{0,2},{1,3},{2,0},{3,1},{4,6},{5,7},{6,4},{7,5},{8,10},{9,11},{10,... | collective-permute-start | bytes 1572872 | tf_op jit(solution)/shard_map/ppermute | solution.py:228
  37.4 28.0 %collective-permute-start.2 = (bf16[128,2048]{1,0:T(8,128)(2,1)}, bf16[128,2048]{1,0:T(8,128)(2,1)S(1)}, u32[]{:S(2)}, u32[]{:S(2)}) collective-permute-start(bf16[128,2048]{1,0:T(8,128)(2,1)} %get-tuple-element.18), channel_id=1, source_target_pairs={{0,3},{1,2},{2,1},{3,0},{4,7},{5,6},{6,5},{7,4},{8,11},{9,10},{10,... | collective-permute-start | bytes 1572872 | tf_op jit(solution)/shard_map/ppermute | solution.py:228
  54.3 13.4 %collective-permute-start.3 = (bf16[16,4,16,256]{3,2,1,0:T(8,128)(2,1)S(1)}, bf16[16,4,16,256]{3,2,1,0:T(8,128)(2,1)S(1)}, u32[]{:S(2)}, u32[]{:S(2)}) collective-permute-start(bf16[16,4,16,256]{3,2,1,0:T(8,128)(2,1)S(1)} %bitcast.17), channel_id=1, source_target_pairs={{0,4},{4,0},{1,5},{5,1},{2,6},{6,2},{3,7},{7,3},{8,12},{12,8},{9,1... | collective-permute-start | bytes 1572872 | tf_op jit(solution)/shard_map/ppermute | solution.py:238
  69.4 11.0 %all-to-all-start.1 = ((bf16[4,128,256]{2,1,0:T(8,128)(2,1)}), bf16[4,128,256]{2,1,0:T(8,128)(2,1)S(1)}, u32[]{:S(2)}, u32[]{:S(2)}) async-start(bf16[4,128,256]{2,1,0:T(8,128)(2,1)} %shard_map.79), calls=%async_computation.1 | async-start | bytes 524288 | tf_op jit(solution)/shard_map/all_to_all | solution.py:241
  90.7 11.6 %collective-permute-start.7 = (bf16[16,4,16,256]{3,2,1,0:T(8,128)(2,1)S(1)}, bf16[16,4,16,256]{3,2,1,0:T(8,128)(2,1)S(1)}, u32[]{:S(2)}, u32[]{:S(2)}) collective-permute-start(bf16[16,4,16,256]{3,2,1,0:T(8,128)(2,1)S(1)} %shard_map.84), channel_id=1, source_target_pairs={{0,4},{4,0},{1,5},{5,1},{2,6},{6,2},{3,7},{7,3},{8,12},{12,8},{9,1... | collective-permute-start | bytes 1572872 | tf_op jit(solution)/shard_map/ppermute | solution.py:243
  95.4 0.7 copy-start.7
  96.2 7.1 %copy-start.5 = (bf16[64,2048]{1,0:T(8,128)(2,1)}, bf16[64,2048]{1,0:T(8,128)(2,1)S(1)}, u32[]{:S(2)}) copy-start(bf16[64,2048]{1,0:T(8,128)(2,1)S(1)} %get-tuple-element.26) | copy-start | bytes 786436
  96.2 7.1 %copy-start.6 = (bf16[64,2048]{1,0:T(8,128)(2,1)}, bf16[64,2048]{1,0:T(8,128)(2,1)S(1)}, u32[]{:S(2)}) copy-start(bf16[64,2048]{1,0:T(8,128)(2,1)S(1)} %get-tuple-element.25) | copy-start | bytes 786436
  97.1 19.9 %copy-start.8 = (bf16[64,2048]{1,0:T(8,128)(2,1)S(1)}, bf16[64,2048]{1,0:T(8,128)(2,1)}, u32[]{:S(2)}) copy-start(bf16[64,2048]{1,0:T(8,128)(2,1)} %copy-done.7) | copy-start | bytes 786436
  97.1 42.0 %copy-start.1 = (bf16[1,8192,128]{2,1,0:T(8,128)(2,1)S(1)}, bf16[1,8192,128]{2,1,0:T(8,128)(2,1)}, u32[]{:S(2)}) copy-start(bf16[1,8192,128]{2,1,0:T(8,128)(2,1)} %param.7) | copy-start | bytes 6291460
  103.3 46.8 %all-to-all-start.3 = ((bf16[64,16,256]{2,1,0:T(8,128)(2,1)}), bf16[64,16,256]{2,1,0:T(8,128)(2,1)}, u32[]{:S(2)}, u32[]{:S(2)}) async-start(bf16[64,16,256]{2,1,0:T(8,128)(2,1)} %bitcast.10), calls=%async_computation.3 | async-start | bytes 1048576 | tf_op jit(solution)/shard_map/all_to_all | solution.py:248
  117.0 11.0 %collective-permute-start.4 = (bf16[64,2048]{1,0:T(8,128)(2,1)S(1)}, bf16[64,2048]{1,0:T(8,128)(2,1)S(1)}, u32[]{:S(2)}, u32[]{:S(2)}) collective-permute-start(bf16[64,2048]{1,0:T(8,128)(2,1)S(1)} %copy-done.8), channel_id=1, source_target_pairs={{0,1},{1,0},{2,3},{3,2},{4,5},{5,4},{6,7},{7,6},{8,9},{9,8},{10,11... | collective-permute-start | bytes 786440 | tf_op jit(solution)/shard_map/ppermute | solution.py:228
  119.5 14.1 %collective-permute-start.5 = (bf16[64,2048]{1,0:T(8,128)(2,1)}, bf16[64,2048]{1,0:T(8,128)(2,1)S(1)}, u32[]{:S(2)}, u32[]{:S(2)}) collective-permute-start(bf16[64,2048]{1,0:T(8,128)(2,1)} %copy-done.6), channel_id=1, source_target_pairs={{0,2},{1,3},{2,0},{3,1},{4,6},{5,7},{6,4},{7,5},{8,10},{9,11},{10,... | collective-permute-start | bytes 786440 | tf_op jit(solution)/shard_map/ppermute | solution.py:228
  123.5 15.6 %collective-permute-start.6 = (bf16[64,2048]{1,0:T(8,128)(2,1)}, bf16[64,2048]{1,0:T(8,128)(2,1)S(1)}, u32[]{:S(2)}, u32[]{:S(2)}) collective-permute-start(bf16[64,2048]{1,0:T(8,128)(2,1)} %copy-done.5), channel_id=1, source_target_pairs={{0,3},{1,2},{2,1},{3,0},{4,7},{5,6},{6,5},{7,4},{8,11},{9,10},{10,... | collective-permute-start | bytes 786440 | tf_op jit(solution)/shard_map/ppermute | solution.py:228

commit v4 on v3

--- a/solution.py
+++ b/solution.py
@@ -21,8 +21,16 @@
 
 SECTION = ("zh", "y", "c")
 TENSOR = ("z4", "z2", "x")
-SPREAD = ("zh", "y", "c", "z4")
 FLIP = [(0, 1), (1, 0)]
+COLUMN = ("zh", "y", "c", "z4", "z2")
+SPREAD = [[2 * i + (w ^ (i // 32)) for i in range(64)] for w in range(2)]
+
+
+def spread(blocks):
+    out = lax.all_to_all(
+        blocks.reshape(64, 16, BLOCK), COLUMN, 0, 0, axis_index_groups=SPREAD, tiled=True
+    )
+    return out.reshape(E_SHAPE)
 
 
 def across(k):
@@ -47,7 +55,9 @@
 
 VMEM = pl.BlockSpec(memory_space=pltpu.VMEM)
 SMEM = pl.BlockSpec(memory_space=pltpu.SMEM)
+HBM = pl.BlockSpec(memory_space=pltpu.HBM)
 LIMIT = pltpu.CompilerParams(vmem_limit_bytes=16 << 20)
+ALONE = pltpu.CompilerParams(vmem_limit_bytes=62 << 20)
 
 
 def whole(kernel, n_args, out_shape, estimate):
@@ -85,23 +95,44 @@
     return pl.ds(pl.multiple_of(p * HALF + b * BLOCK, BLOCK), BLOCK)
 
 
-def project_kernel(s_ref, q_ref, ct_ref, wk_ref, wv_ref, *out_refs):
-    b = pl.program_id(0)
-    for k in range(4):
-        for p in range(2):
-            key, value = (w[0, s_ref[0] ^ p, s_ref[1] ^ k] for w in (wk_ref, wv_ref))
-            out_refs[k][0:GROUP, block_at(p, b)] = nt(q_ref[...], key).astype(BF16)
-            out_refs[k][GROUP:PAIR, block_at(p, b)] = nt(ct_ref[...], value).astype(BF16)
+def project_kernel(s_ref, q_hbm, ct_hbm, wk_hbm, wv_hbm, o0, o1, o2, o3, rows, weights, sems):
+    small = [
+        pltpu.make_async_copy(src, rows.at[i], sems.at[8 + i])
+        for i, src in enumerate((q_hbm, ct_hbm))
+    ]
+    large = [
+        [pltpu.make_async_copy(w.at[b], weights.at[i, b], sems.at[2 * b + i]) for i, w in enumerate((wk_hbm, wv_hbm))]
+        for b in range(4)
+    ]
+    for c in small + [c for pair in large for c in pair]:
+        c.start()
+    for c in small:
+        c.wait()
+
+    for b in range(4):
+        for c in large[b]:
+            c.wait()
+        for k, out_ref in enumerate((o0, o1, o2, o3)):
+            for p in range(2):
+                at = slice(p * HALF + b * BLOCK, p * HALF + (b + 1) * BLOCK)
+                for i in range(2):
+                    part = nt(rows[i], weights[i, b, s_ref[0] ^ p, s_ref[1] ^ k])
+                    out_ref[i * GROUP : (i + 1) * GROUP, at] = part.astype(BF16)
 
 
 def project(scalars, q, ct, wk, wv):
-    small = full((GROUP, HEAD))
-    return streamed(
+    return pl.pallas_call(
         project_kernel,
-        [small, small, W_SPEC, W_SPEC],
-        [full((PAIR, 2 * HALF))] * 4,
-        [jax.ShapeDtypeStruct((PAIR, 2 * HALF), BF16)] * 4,
-        cost(2 * 128 * 8192 * 128, 6 << 20),
+        in_specs=[SMEM] + [HBM] * 4,
+        out_specs=[VMEM] * 4,
+        out_shape=[jax.ShapeDtypeStruct((PAIR, 2 * HALF), BF16)] * 4,
+        scratch_shapes=[
+            pltpu.VMEM((2, GROUP, HEAD), BF16),
+            pltpu.VMEM((2, 4, 2, 4, BLOCK, HEAD), BF16),
+            pltpu.SemaphoreType.DMA((10,)),
+        ],
+        cost_estimate=cost(2 * 128 * 8192 * 128, 6 << 20),
+        compiler_params=ALONE,
     )(scalars, q, ct, wk, wv)
 
 
@@ -113,7 +144,10 @@
 def partial_scores(a_refs, e_ref, p):
     total = None
     for b in range(4):
-        part = nt(heads(a_refs, p, b), e_ref[:, b].reshape(ROWS, BLOCK))
+        part = jnp.concatenate(
+            [nt(heads(a_refs, p ^ r, b), e_ref[8 * r : 8 * r + 8, b].reshape(128, BLOCK)) for r in range(2)],
+            axis=1,
+        )
         total = part if total is None else total + part
     return total
 
@@ -166,9 +200,10 @@
 
 def term_kernel(p, s_ref, g_ref, a0, a1, a2, a3, out_ref):
     g = jnp.concatenate([g_ref[s_ref[1] ^ k] for k in range(4)], axis=1)
-    for b in range(4):
-        part = nn(g, heads((a0, a1, a2, a3), p, b))
-        out_ref[:, b] = part.astype(out_ref.dtype).reshape(16, 16, BLOCK)
+    for r in range(2):
+        for b in range(4):
+            part = nn(g[128 * r : 128 * r + 128], heads((a0, a1, a2, a3), p ^ r, b))
+            out_ref[8 * r : 8 * r + 8, b] = part.astype(out_ref.dtype).reshape(8, 16, BLOCK)
 
 
 def term(scalars, g, a, p, kind):
@@ -179,9 +214,11 @@
 def mix_kernel(s_ref, g_ref, own_ref, other_ref, *out_refs):
     gs = jnp.concatenate([g_ref[s_ref[1] ^ k, :, 0:GROUP] for k in range(4)], axis=1)
     gs = gs.astype(F32).T.astype(BF16)
-    for p, e_ref in enumerate((own_ref, other_ref)):
+    for p in range(2):
+        halves = (own_ref, other_ref) if p == 0 else (other_ref, own_ref)
         for b in range(4):
-            part = nn(gs, e_ref[:, b].reshape(ROWS, BLOCK)).astype(BF16)
+            e = [h[8 * r : 8 * r + 8, b].reshape(128, BLOCK) for r, h in enumerate(halves)]
+            part = nn(gs, jnp.concatenate(e, axis=0)).astype(BF16)
             at = p * HALF + b * BLOCK
             for k in range(4):
                 out_refs[k][:, at : at + BLOCK] = part[k * GROUP : (k + 1) * GROUP]
@@ -229,11 +266,11 @@
 
 
 def local(encoded, w_key, w_value, queries, cotangent, counts):
-    scalars = jnp.stack([lax.axis_index("z2"), lax.axis_index("x")]).astype(jnp.int32)
+    w = lax.axis_index("zh") ^ lax.axis_index("z2")
+    scalars = jnp.stack([w, lax.axis_index("x")]).astype(jnp.int32)
     wk = w_key.reshape(4, 2, 4, BLOCK, HEAD)
     wv = w_value.reshape(4, 2, 4, BLOCK, HEAD)
-    out_rows = jnp.broadcast_to(encoded[:, None], (16, 4, 16, BLOCK)).reshape(64, 16, BLOCK)
-    own = lax.all_to_all(out_rows, SPREAD, 0, 0, tiled=True).reshape(16, 4, 16, BLOCK)
+    own = spread(jnp.broadcast_to(encoded[:, None], E_SHAPE))
     shared = to_members(project(scalars, queries[0], cotangent[0], wk, wv))
     other = lax.ppermute(own, "z2", FLIP)
     first = first_scores(scalars, shared, own)
@@ -244,8 +281,7 @@
     kept = term(scalars, grads, shared, 0, F32)
     mixture = mix(scalars, grads, own, other)
     kept, mixture = lax.optimization_barrier((kept, mixture))
-    sent = (kept + passed.astype(F32)).astype(BF16).reshape(64, 16, BLOCK)
-    terms = lax.all_to_all(sent, SPREAD, 0, 0, tiled=True).reshape(16, 4, 16, BLOCK)
+    terms = spread((kept + passed.astype(F32)).astype(BF16))
     mixed = to_members(mixture)
     grad_queries = query(scalars, mixed, wk)
     grad_encoded = jnp.sum(terms.astype(F32), axis=1)

time: 153 us -> 150 us (0.980)
  the two profiles are of different devices: /device:TPU:8 before, /device:TPU:1 now
where the time goes in v4:
time: 150 us; the launch traced here: 149 us
  starting transfers between devices  63.5 us (42%)
  waiting for transfers between devices  55.3 us (37%)
  Pallas kernels  13.8 us (9%)
  blocking collectives  7.92 us (5%)
  local copies, waits for them, and re-layouts  3.5 us (2%)
  other arithmetic  3.37 us (2%)
    all_to_all x2, starting transfers between devices, spread(): lax.all_to_all(blocks.reshape(64, 16, BLOCK), COLUMN, 0, 0, axis_index_gr...  34.7 us
    all_to_all x2, waiting for transfers between devices, spread(): lax.all_to_all(blocks.reshape(64, 16, BLOCK), COLUMN, 0, 0, axis_index_gr...  23.2 us
    ppermute x6, starting transfers between devices, to_members(): lax.ppermute(parts[k], 'x', across(k))  19.2 us
    ppermute x6, waiting for transfers between devices, to_members(): lax.ppermute(parts[k], 'x', across(k))  18.4 us
    all_to_all x1, blocking collectives, local(): lax.all_to_all(attend(counts.reshape(1), parts), 'x', 0, 0, tiled=True)  7.92 us
    ppermute x1, waiting for transfers between devices, local(): passed = lax.ppermute(term(scalars, grads, shared, 1, BF16), 'z2', FLIP)  5.23 us
    pallas_call x1, Pallas kernels, project(): pl.pallas_call(project_kernel, in_specs=[SMEM] + [HBM] * 4, out_specs=[VM...  5.06 us
    all_to_all x1, waiting for transfers between devices, local(): parts = lax.all_to_all(sums, 'x', 0, 0, tiled=True)  4.88 us
  transfers between devices with their start and end apart: 11, of which 9 were waited for; matrix products, arithmetic and copies ran while one was open for 0% of the time, Pallas kernels for 7%

profile of v4, /device:TPU:1, one launch (start us, length us, event | category | flops | bytes accessed | tf_op | source)
XLA Modules:
  0.0 148.8 jit_solution(4468041105833053761)
XLA Ops:
  0.6 1.7 %broadcast_in_dim.4 = bf16[16,4,16,256]{3,2,1,0:T(8,128)(2,1)} broadcast(bf16[16,16,256]{2,1,0:T(8,128)(2,1)} %param.6), dimensions={0,2,3} | broadcast | bytes 655360 | tf_op jit(solution)/shard_map/broadcast_in_dim | solution.py:273
  2.4 19.3 %all-to-all-start = ((bf16[64,16,256]{2,1,0:T(8,128)(2,1)}), bf16[64,16,256]{2,1,0:T(8,128)(2,1)S(1)}, u32[]{:S(2)}, u32[]{:S(2)}) async-start(bf16[64,16,256]{2,1,0:T(8,128)(2,1)} %bitcast.7), calls=%async_computation | async-start | bytes 1048576 | tf_op jit(solution)/shard_map/all_to_all | solution.py:30
  21.7 0.6 pad_add_fusion.s_ref
  22.3 0.0 copy-start.3
  22.3 5.1 %shard_map.77 = (bf16[128,2048]{1,0:T(8,128)(2,1)}, bf16[128,2048]{1,0:T(8,128)(2,1)}, bf16[128,2048]{1,0:T(8,128)(2,1)}, bf16[128,2048]{1,0:T(8,128)(2,1)}) custom-call(s32[2]{0:T(128)} %pad_add_fusion.s_ref, bf16[64,128]{1,0:T(8,128)(2,1)} %bitcast.21, bf16[64,128]{1,0:T(8,128)(2,1)} %bitcast.22, bf16[4,2,4,256,128]{4,3,2,1,0:T(8,128)(2,1)} %bitcast.15, ...), custom_call_target="tpu_custom_call" | custom-call | flops 268435456 | bytes 6291456 | tf_op jit(solution)/shard_map/pallas_call | solution.py:124
  27.3 3.1 %collective-permute-start = (bf16[128,2048]{1,0:T(8,128)(2,1)}, bf16[128,2048]{1,0:T(8,128)(2,1)S(1)}, u32[]{:S(2)}, u32[]{:S(2)}) collective-permute-start(bf16[128,2048]{1,0:T(8,128)(2,1)} %get-tuple-element.16), channel_id=1, source_target_pairs={{0,1},{1,0},{2,3},{3,2},{4,5},{5,4},{6,7},{7,6},{8,9},{9,8},{10,11... | collective-permute-start | bytes 1572872 | tf_op jit(solution)/shard_map/ppermute | solution.py:265
  30.5 4.4 %collective-permute-start.1 = (bf16[128,2048]{1,0:T(8,128)(2,1)}, bf16[128,2048]{1,0:T(8,128)(2,1)S(1)}, u32[]{:S(2)}, u32[]{:S(2)}) collective-permute-start(bf16[128,2048]{1,0:T(8,128)(2,1)} %get-tuple-element.17), channel_id=1, source_target_pairs={{0,2},{1,3},{2,0},{3,1},{4,6},{5,7},{6,4},{7,5},{8,10},{9,11},{10,... | collective-permute-start | bytes 1572872 | tf_op jit(solution)/shard_map/ppermute | solution.py:265
  34.8 2.1 %collective-permute-start.2 = (bf16[128,2048]{1,0:T(8,128)(2,1)}, bf16[128,2048]{1,0:T(8,128)(2,1)S(1)}, u32[]{:S(2)}, u32[]{:S(2)}) collective-permute-start(bf16[128,2048]{1,0:T(8,128)(2,1)} %get-tuple-element.18), channel_id=1, source_target_pairs={{0,3},{1,2},{2,1},{3,0},{4,7},{5,6},{6,5},{7,4},{8,11},{9,10},{10,... | collective-permute-start | bytes 1572872 | tf_op jit(solution)/shard_map/ppermute | solution.py:265
  36.9 16.1 %all-to-all-done = bf16[64,16,256]{2,1,0:T(8,128)(2,1)S(1)} async-done(((bf16[64,16,256]{2,1,0:T(8,128)(2,1)}), bf16[64,16,256]{2,1,0:T(8,128)(2,1)S(1)}, u32[]{:S(2)}, u32[]{:S(2)}) %all-to-all-start) | async-done | bytes 524320 | tf_op jit(solution)/shard_map/all_to_all | solution.py:30
  53.1 2.7 %collective-permute-start.3 = (bf16[16,4,16,256]{3,2,1,0:T(8,128)(2,1)S(1)}, bf16[16,4,16,256]{3,2,1,0:T(8,128)(2,1)S(1)}, u32[]{:S(2)}, u32[]{:S(2)}) collective-permute-start(bf16[16,4,16,256]{3,2,1,0:T(8,128)(2,1)S(1)} %bitcast.17), channel_id=1, source_target_pairs={{0,4},{4,0},{1,5},{5,1},{2,6},{6,2},{3,7},{7,3},{8,12},{12,8},{9,1... | collective-permute-start | bytes 1572872 | tf_op jit(solution)/shard_map/ppermute | solution.py:275
  55.8 0.0 collective-permute-done.a1
  55.8 0.1 collective-permute-done.1.a2
  55.9 5.8 %collective-permute-done.2.a3 = bf16[128,2048]{1,0:T(8,128)(2,1)S(1)} collective-permute-done((bf16[128,2048]{1,0:T(8,128)(2,1)}, bf16[128,2048]{1,0:T(8,128)(2,1)S(1)}, u32[]{:S(2)}, u32[]{:S(2)}) %collective-permute-start.2) | collective-permute-done | bytes 524320 | tf_op jit(solution)/shard_map/ppermute | solution.py:265
  61.8 0.0 copy-done.3
  61.8 0.0 copy-start.1
  61.8 1.0 copy-done.1
  62.8 1.2 shard_map.78.first_ref
  64.1 0.0 copy-start.2
  64.1 3.5 %collective-permute-done.3.e_ref.other_ref = bf16[16,4,16,256]{3,2,1,0:T(8,128)(2,1)S(1)} collective-permute-done((bf16[16,4,16,256]{3,2,1,0:T(8,128)(2,1)S(1)}, bf16[16,4,16,256]{3,2,1,0:T(8,128)(2,1)S(1)}, u32[]{:S(2)}, u32[]{:S(2)}) %collective-permute-start.3) | collective-permute-done | bytes 524320 | tf_op jit(solution)/shard_map/ppermute | solution.py:275
  67.6 2.0 %shard_map.79 = bf16[4,128,256]{2,1,0:T(8,128)(2,1)} custom-call(s32[2]{0:T(128)S(1)} %copy-done.3, bf16[128,2048]{1,0:T(8,128)(2,1)S(1)} %copy-done.1, bf16[128,2048]{1,0:T(8,128)(2,1)S(1)} %collective-permute-done.a1, bf16[128,2048]{1,0:T(8,128)(2,1)S(1)} %collective-permute-done.1.a2, bf16[128,2048]{1,0:T(8,128)(2,1)S(1)} %collective-permute-done.2.a3, ...), custom_call_target="tpu_custom_call" | custom-call | flops 268435456 | bytes 2097152 | tf_op jit(solution)/shard_map/pallas_call | solution.py:175
  69.6 4.0 %all-to-all-start.1 = ((bf16[4,128,256]{2,1,0:T(8,128)(2,1)}), bf16[4,128,256]{2,1,0:T(8,128)(2,1)S(1)}, u32[]{:S(2)}, u32[]{:S(2)}) async-start(bf16[4,128,256]{2,1,0:T(8,128)(2,1)} %shard_map.79), calls=%async_computation.1 | async-start | bytes 524288 | tf_op jit(solution)/shard_map/all_to_all | solution.py:278
  74.2 4.9 %all-to-all-done.1.s_ref = bf16[4,128,256]{2,1,0:T(8,128)(2,1)S(1)} async-done(((bf16[4,128,256]{2,1,0:T(8,128)(2,1)}), bf16[4,128,256]{2,1,0:T(8,128)(2,1)S(1)}, u32[]{:S(2)}, u32[]{:S(2)}) %all-to-all-start.1) | async-done | bytes 262176 | tf_op jit(solution)/shard_map/all_to_all | solution.py:278
  79.1 0.3 shard_map.80
  79.4 7.9 %all_to_all.20.g_ref = bf16[4,256,128]{2,1,0:T(8,128)(2,1)S(1)} all-to-all(bf16[4,256,128]{2,1,0:T(8,128)(2,1)S(1)} %shard_map.80), channel_id=1, replica_groups=mesh['zh'=2,'y'=4,'c'=2,'z4'=4,'z2'=2,'x'=4] {'x'}, dimensions={0} | all-to-all | bytes 524288 | tf_op jit(solution)/shard_map/all_to_all | solution.py:279
  87.3 0.0 copy-done.2
  87.3 1.0 shard_map.84
  88.3 3.0 %collective-permute-start.7 = (bf16[16,4,16,256]{3,2,1,0:T(8,128)(2,1)S(1)}, bf16[16,4,16,256]{3,2,1,0:T(8,128)(2,1)S(1)}, u32[]{:S(2)}, u32[]{:S(2)}) collective-permute-start(bf16[16,4,16,256]{3,2,1,0:T(8,128)(2,1)S(1)} %shard_map.84), channel_id=1, source_target_pairs={{0,4},{4,0},{1,5},{5,1},{2,6},{6,2},{3,7},{7,3},{8,12},{12,8},{9,1... | collective-permute-start | bytes 1572872 | tf_op jit(solution)/shard_map/ppermute | solution.py:280
  91.3 1.1 shard_map.82
  92.4 0.0 copy-start.6
  92.4 0.7 copy-done.6
  93.1 0.0 copy-start.4
  93.1 0.0 copy-start.5
  93.1 1.0 shard_map.81
  94.1 0.0 copy-start.7
  94.1 0.0 copy-start
  94.1 5.2 %collective-permute-done.7 = bf16[16,4,16,256]{3,2,1,0:T(8,128)(2,1)S(1)} collective-permute-done((bf16[16,4,16,256]{3,2,1,0:T(8,128)(2,1)S(1)}, bf16[16,4,16,256]{3,2,1,0:T(8,128)(2,1)S(1)}, u32[]{:S(2)}, u32[]{:S(2)}) %collective-permute-start.7) | collective-permute-done | bytes 524320 | tf_op jit(solution)/shard_map/ppermute | solution.py:280
  99.4 1.0 add_convert_fusion
  100.3 0.0 copy-done.4
  100.3 0.0 copy-done.5
  100.4 15.3 %all-to-all-start.3 = ((bf16[64,16,256]{2,1,0:T(8,128)(2,1)}), bf16[64,16,256]{2,1,0:T(8,128)(2,1)}, u32[]{:S(2)}, u32[]{:S(2)}) async-start(bf16[64,16,256]{2,1,0:T(8,128)(2,1)} %bitcast.10), calls=%async_computation.3 | async-start | bytes 1048576 | tf_op jit(solution)/shard_map/all_to_all | solution.py:30
  115.7 0.0 copy-done.7
  115.7 2.2 %collective-permute-start.4 = (bf16[64,2048]{1,0:T(8,128)(2,1)S(1)}, bf16[64,2048]{1,0:T(8,128)(2,1)S(1)}, u32[]{:S(2)}, u32[]{:S(2)}) collective-permute-start(bf16[64,2048]{1,0:T(8,128)(2,1)S(1)} %copy-done.7), channel_id=1, source_target_pairs={{0,1},{1,0},{2,3},{3,2},{4,5},{5,4},{6,7},{7,6},{8,9},{9,8},{10,11... | collective-permute-start | bytes 786440 | tf_op jit(solution)/shard_map/ppermute | solution.py:265
  117.9 3.7 %collective-permute-start.5 = (bf16[64,2048]{1,0:T(8,128)(2,1)}, bf16[64,2048]{1,0:T(8,128)(2,1)S(1)}, u32[]{:S(2)}, u32[]{:S(2)}) collective-permute-start(bf16[64,2048]{1,0:T(8,128)(2,1)} %copy-done.5), channel_id=1, source_target_pairs={{0,2},{1,3},{2,0},{3,1},{4,6},{5,7},{6,4},{7,5},{8,10},{9,11},{10,... | collective-permute-start | bytes 786440 | tf_op jit(solution)/shard_map/ppermute | solution.py:265
  121.6 3.7 %collective-permute-start.6 = (bf16[64,2048]{1,0:T(8,128)(2,1)}, bf16[64,2048]{1,0:T(8,128)(2,1)S(1)}, u32[]{:S(2)}, u32[]{:S(2)}) collective-permute-start(bf16[64,2048]{1,0:T(8,128)(2,1)} %copy-done.4), channel_id=1, source_target_pairs={{0,3},{1,2},{2,1},{3,0},{4,7},{5,6},{6,5},{7,4},{8,11},{9,10},{10,... | collective-permute-start | bytes 786440 | tf_op jit(solution)/shard_map/ppermute | solution.py:265
  125.3 0.0 collective-permute-done.4.x1
  125.3 6.0 %collective-permute-done.5.x2 = bf16[64,2048]{1,0:T(8,128)(2,1)S(1)} collective-permute-done((bf16[64,2048]{1,0:T(8,128)(2,1)}, bf16[64,2048]{1,0:T(8,128)(2,1)S(1)}, u32[]{:S(2)}, u32[]{:S(2)}) %collective-permute-start.5) | collective-permute-done | bytes 262176 | tf_op jit(solution)/shard_map/ppermute | solution.py:265
  131.3 6.5 %collective-permute-done.6.x3 = bf16[64,2048]{1,0:T(8,128)(2,1)S(1)} collective-permute-done((bf16[64,2048]{1,0:T(8,128)(2,1)}, bf16[64,2048]{1,0:T(8,128)(2,1)S(1)}, u32[]{:S(2)}, u32[]{:S(2)}) %collective-permute-start.6) | collective-permute-done | bytes 262176 | tf_op jit(solution)/shard_map/ppermute | solution.py:265
  137.7 0.0 copy-done
  137.7 2.1 %shard_map.83 = bf16[64,128]{1,0:T(8,128)(2,1)} custom-call(s32[2]{0:T(128)S(1)} %copy-done.3, bf16[64,2048]{1,0:T(8,128)(2,1)S(1)} %get-tuple-element.23.x0, bf16[64,2048]{1,0:T(8,128)(2,1)S(1)} %collective-permute-done.4.x1, bf16[64,2048]{1,0:T(8,128)(2,1)S(1)} %collective-permute-done.5.x2, bf16[64,2048]{1,0:T(8,128)(2,1)S(1)} %collective-permute-done.6.x3, ...), custom_call_target="tpu_custom_call" | custom-call | flops 134217728 | bytes 3145728 | tf_op jit(solution)/shard_map/pallas_call | solution.py:254
  139.9 7.1 %all-to-all-done.3 = bf16[64,16,256]{2,1,0:T(8,128)(2,1)} async-done(((bf16[64,16,256]{2,1,0:T(8,128)(2,1)}), bf16[64,16,256]{2,1,0:T(8,128)(2,1)}, u32[]{:S(2)}, u32[]{:S(2)}) %all-to-all-start.3) | async-done | bytes 524320 | tf_op jit(solution)/shard_map/all_to_all | solution.py:30
  147.0 1.8 %convert_reduce_fusion = f32[16,16,256]{2,1,0:T(8,128)} fusion(bf16[64,16,256]{2,1,0:T(8,128)(2,1)} %all-to-all-done.3), kind=kLoop, calls=%fused_computation | loop fusion | flops 458752 | bytes 786432 | tf_op jit(solution)/shard_map/reduce_sum | solution.py:287
Async XLA Ops:
  2.4 50.7 %all-to-all-start = ((bf16[64,16,256]{2,1,0:T(8,128)(2,1)}), bf16[64,16,256]{2,1,0:T(8,128)(2,1)S(1)}, u32[]{:S(2)}, u32[]{:S(2)}) async-start(bf16[64,16,256]{2,1,0:T(8,128)(2,1)} %bitcast.7), calls=%async_computation | async-start | bytes 1048576 | tf_op jit(solution)/shard_map/all_to_all | solution.py:30
  22.3 39.5 %copy-start.3 = (s32[2]{0:T(128)S(1)}, s32[2]{0:T(128)}, u32[]{:S(2)}) copy-start(s32[2]{0:T(128)} %pad_add_fusion.s_ref) | copy-start | bytes 28
  27.3 28.5 %collective-permute-start = (bf16[128,2048]{1,0:T(8,128)(2,1)}, bf16[128,2048]{1,0:T(8,128)(2,1)S(1)}, u32[]{:S(2)}, u32[]{:S(2)}) collective-permute-start(bf16[128,2048]{1,0:T(8,128)(2,1)} %get-tuple-element.16), channel_id=1, source_target_pairs={{0,1},{1,0},{2,3},{3,2},{4,5},{5,4},{6,7},{7,6},{8,9},{9,8},{10,11... | collective-permute-start | bytes 1572872 | tf_op jit(solution)/shard_map/ppermute | solution.py:265
  30.5 25.5 %collective-permute-start.1 = (bf16[128,2048]{1,0:T(8,128)(2,1)}, bf16[128,2048]{1,0:T(8,128)(2,1)S(1)}, u32[]{:S(2)}, u32[]{:S(2)}) collective-permute-start(bf16[128,2048]{1,0:T(8,128)(2,1)} %get-tuple-element.17), channel_id=1, source_target_pairs={{0,2},{1,3},{2,0},{3,1},{4,6},{5,7},{6,4},{7,5},{8,10},{9,11},{10,... | collective-permute-start | bytes 1572872 | tf_op jit(solution)/shard_map/ppermute | solution.py:265
  34.8 26.9 %collective-permute-start.2 = (bf16[128,2048]{1,0:T(8,128)(2,1)}, bf16[128,2048]{1,0:T(8,128)(2,1)S(1)}, u32[]{:S(2)}, u32[]{:S(2)}) collective-permute-start(bf16[128,2048]{1,0:T(8,128)(2,1)} %get-tuple-element.18), channel_id=1, source_target_pairs={{0,3},{1,2},{2,1},{3,0},{4,7},{5,6},{6,5},{7,4},{8,11},{9,10},{10,... | collective-permute-start | bytes 1572872 | tf_op jit(solution)/shard_map/ppermute | solution.py:265
  53.1 14.5 %collective-permute-start.3 = (bf16[16,4,16,256]{3,2,1,0:T(8,128)(2,1)S(1)}, bf16[16,4,16,256]{3,2,1,0:T(8,128)(2,1)S(1)}, u32[]{:S(2)}, u32[]{:S(2)}) collective-permute-start(bf16[16,4,16,256]{3,2,1,0:T(8,128)(2,1)S(1)} %bitcast.17), channel_id=1, source_target_pairs={{0,4},{4,0},{1,5},{5,1},{2,6},{6,2},{3,7},{7,3},{8,12},{12,8},{9,1... | collective-permute-start | bytes 1572872 | tf_op jit(solution)/shard_map/ppermute | solution.py:275
  61.8 1.0 copy-start.1
  64.1 23.3 %copy-start.2 = (bf16[128,2048]{1,0:T(8,128)(2,1)S(1)}, bf16[128,2048]{1,0:T(8,128)(2,1)}, u32[]{:S(2)}) copy-start(bf16[128,2048]{1,0:T(8,128)(2,1)} %get-tuple-element.15.a0) | copy-start | bytes 1572868
  69.6 9.5 %all-to-all-start.1 = ((bf16[4,128,256]{2,1,0:T(8,128)(2,1)}), bf16[4,128,256]{2,1,0:T(8,128)(2,1)S(1)}, u32[]{:S(2)}, u32[]{:S(2)}) async-start(bf16[4,128,256]{2,1,0:T(8,128)(2,1)} %shard_map.79), calls=%async_computation.1 | async-start | bytes 524288 | tf_op jit(solution)/shard_map/all_to_all | solution.py:278
  88.3 11.0 %collective-permute-start.7 = (bf16[16,4,16,256]{3,2,1,0:T(8,128)(2,1)S(1)}, bf16[16,4,16,256]{3,2,1,0:T(8,128)(2,1)S(1)}, u32[]{:S(2)}, u32[]{:S(2)}) collective-permute-start(bf16[16,4,16,256]{3,2,1,0:T(8,128)(2,1)S(1)} %shard_map.84), channel_id=1, source_target_pairs={{0,4},{4,0},{1,5},{5,1},{2,6},{6,2},{3,7},{7,3},{8,12},{12,8},{9,1... | collective-permute-start | bytes 1572872 | tf_op jit(solution)/shard_map/ppermute | solution.py:280
  92.4 0.7 copy-start.6
  93.1 7.2 %copy-start.4 = (bf16[64,2048]{1,0:T(8,128)(2,1)}, bf16[64,2048]{1,0:T(8,128)(2,1)S(1)}, u32[]{:S(2)}) copy-start(bf16[64,2048]{1,0:T(8,128)(2,1)S(1)} %get-tuple-element.26) | copy-start | bytes 786436
  93.1 7.2 %copy-start.5 = (bf16[64,2048]{1,0:T(8,128)(2,1)}, bf16[64,2048]{1,0:T(8,128)(2,1)S(1)}, u32[]{:S(2)}) copy-start(bf16[64,2048]{1,0:T(8,128)(2,1)S(1)} %get-tuple-element.25) | copy-start | bytes 786436
  94.1 21.6 %copy-start.7 = (bf16[64,2048]{1,0:T(8,128)(2,1)S(1)}, bf16[64,2048]{1,0:T(8,128)(2,1)}, u32[]{:S(2)}) copy-start(bf16[64,2048]{1,0:T(8,128)(2,1)} %copy-done.6) | copy-start | bytes 786436
  94.1 43.6 %copy-start = (bf16[1,8192,128]{2,1,0:T(8,128)(2,1)S(1)}, bf16[1,8192,128]{2,1,0:T(8,128)(2,1)}, u32[]{:S(2)}) copy-start(bf16[1,8192,128]{2,1,0:T(8,128)(2,1)} %param.7) | copy-start | bytes 6291460
  100.4 46.6 %all-to-all-start.3 = ((bf16[64,16,256]{2,1,0:T(8,128)(2,1)}), bf16[64,16,256]{2,1,0:T(8,128)(2,1)}, u32[]{:S(2)}, u32[]{:S(2)}) async-start(bf16[64,16,256]{2,1,0:T(8,128)(2,1)} %bitcast.10), calls=%async_computation.3 | async-start | bytes 1048576 | tf_op jit(solution)/shard_map/all_to_all | solution.py:30
  115.7 9.6 %collective-permute-start.4 = (bf16[64,2048]{1,0:T(8,128)(2,1)S(1)}, bf16[64,2048]{1,0:T(8,128)(2,1)S(1)}, u32[]{:S(2)}, u32[]{:S(2)}) collective-permute-start(bf16[64,2048]{1,0:T(8,128)(2,1)S(1)} %copy-done.7), channel_id=1, source_target_pairs={{0,1},{1,0},{2,3},{3,2},{4,5},{5,4},{6,7},{7,6},{8,9},{9,8},{10,11... | collective-permute-start | bytes 786440 | tf_op jit(solution)/shard_map/ppermute | solution.py:265
  117.9 13.4 %collective-permute-start.5 = (bf16[64,2048]{1,0:T(8,128)(2,1)}, bf16[64,2048]{1,0:T(8,128)(2,1)S(1)}, u32[]{:S(2)}, u32[]{:S(2)}) collective-permute-start(bf16[64,2048]{1,0:T(8,128)(2,1)} %copy-done.5), channel_id=1, source_target_pairs={{0,2},{1,3},{2,0},{3,1},{4,6},{5,7},{6,4},{7,5},{8,10},{9,11},{10,... | collective-permute-start | bytes 786440 | tf_op jit(solution)/shard_map/ppermute | solution.py:265
  121.6 16.2 %collective-permute-start.6 = (bf16[64,2048]{1,0:T(8,128)(2,1)}, bf16[64,2048]{1,0:T(8,128)(2,1)S(1)}, u32[]{:S(2)}, u32[]{:S(2)}) collective-permute-start(bf16[64,2048]{1,0:T(8,128)(2,1)} %copy-done.4), channel_id=1, source_target_pairs={{0,3},{1,2},{2,1},{3,0},{4,7},{5,6},{6,5},{7,4},{8,11},{9,10},{10,... | collective-permute-start | bytes 786440 | tf_op jit(solution)/shard_map/ppermute | solution.py:265

commit v5 on v4

v5 whole, which is shorter than its diff:
```python
import functools
import math

import jax
import jax.numpy as jnp
from jax import lax
from jax.experimental import pallas as pl
from jax.experimental.pallas import tpu as pltpu
from jax.sharding import Mesh, PartitionSpec as P

NBR_LEN = 128
HEAD = 128
GROUP = 64
PAIR = 2 * GROUP
ROWS = 256
BLOCK = 256
SPAN = 2 * BLOCK
COLUMN = 4 * SPAN
INV = 1.0 / math.sqrt(HEAD)
F32 = jnp.float32
BF16 = jnp.bfloat16

AXES = {"zh": 2, "y": 4, "c": 2, "za": 2, "zb": 2, "z2": 2, "x": 4}
SECTION = ("zh", "y", "c")
TENSOR = ("za", "zb", "z2", "x")
QUAD = ("zb", "z2")

SPREAD_AXES = ("zh", "y", "c", "za", "zb", "z2")
ROW_GROUPS = [[4 * i + (w ^ (i // 16)) for i in range(32)] for w in range(4)]
TERM_GROUPS = [[2 * i + (w ^ (i // 32)) for i in range(64)] for w in range(2)]
E_SHAPE = (16, 2, 16, BLOCK)
T_SHAPE = (16, 4, 16, BLOCK)


def spread(blocks, groups):
    out = lax.all_to_all(
        blocks.reshape(-1, 16, BLOCK), SPREAD_AXES, 0, 0, axis_index_groups=groups, tiled=True
    )
    return out.reshape(blocks.shape)


def swap(array, axes, k):
    return lax.ppermute(array, axes, [(i, i ^ k) for i in range(4)])


def to_members(parts):
    two, one, three = [swap(parts[k], "x", k) for k in (2, 1, 3)]
    return [parts[0], one, two, three]


def nt(a, b):
    return lax.dot_general(a, b, (((1,), (1,)), ((), ())), preferred_element_type=F32)


def nn(a, b):
    return jnp.dot(a, b, preferred_element_type=F32)


def cost(flops, nbytes):
    return pl.CostEstimate(flops=flops, bytes_accessed=nbytes, transcendentals=0)


VMEM = pl.BlockSpec(memory_space=pltpu.VMEM)
SMEM = pl.BlockSpec(memory_space=pltpu.SMEM)
HBM = pl.BlockSpec(memory_space=pltpu.HBM)
LIMIT = pltpu.CompilerParams(vmem_limit_bytes=16 << 20)
ALONE = pltpu.CompilerParams(vmem_limit_bytes=62 << 20)


def whole(kernel, n_args, out_shape, estimate):
    return pl.pallas_call(
        kernel,
        in_specs=[SMEM] + [VMEM] * n_args,
        out_specs=jax.tree.map(lambda _: VMEM, out_shape),
        out_shape=out_shape,
        cost_estimate=estimate,
        compiler_params=LIMIT,
    )


def project_kernel(s_ref, q_hbm, ct_hbm, wk_hbm, wv_hbm, o0, o1, o2, o3, rows, weights, sems):
    small = [
        pltpu.make_async_copy(src, rows.at[i], sems.at[4 + i])
        for i, src in enumerate((q_hbm, ct_hbm))
    ]
    large = [
        [
            pltpu.make_async_copy(w.at[b], weights.at[i, b], sems.at[2 * b + i])
            for i, w in enumerate((wk_hbm, wv_hbm))
        ]
        for b in range(2)
    ]
    for c in small + large[0] + large[1]:
        c.start()
    for c in small:
        c.wait()
    for b in range(2):
        for c in large[b]:
            c.wait()
        for k, out_ref in enumerate((o0, o1, o2, o3)):
            for p in range(4):
                at = slice(p * SPAN + b * BLOCK, p * SPAN + (b + 1) * BLOCK)
                for i in range(2):
                    part = nt(rows[i], weights[i, b, s_ref[0] ^ p, s_ref[1] ^ k])
                    out_ref[i * GROUP : (i + 1) * GROUP, at] = part.astype(BF16)


def project(scalars, q, ct, wk, wv):
    return pl.pallas_call(
        project_kernel,
        in_specs=[SMEM] + [HBM] * 4,
        out_specs=[VMEM] * 4,
        out_shape=[jax.ShapeDtypeStruct((PAIR, COLUMN), BF16)] * 4,
        scratch_shapes=[
            pltpu.VMEM((2, GROUP, HEAD), BF16),
            pltpu.VMEM((2, 2, 4, 4, BLOCK, HEAD), BF16),
            pltpu.SemaphoreType.DMA((6,)),
        ],
        cost_estimate=cost(2 * 128 * 8192 * 128, 6 << 20),
        compiler_params=ALONE,
    )(scalars, q, ct, wk, wv)


def heads(a_refs, p):
    return jnp.concatenate([r[:, p * SPAN : (p + 1) * SPAN] for r in a_refs], axis=0)


def half_rows(e_ref, r):
    halves = [e_ref[8 * r : 8 * r + 8, b].reshape(128, BLOCK) for b in range(2)]
    return jnp.concatenate(halves, axis=1)


def scores_kernel(pieces, has_sum, last, s_ref, a0, a1, a2, a3, *refs):
    e_refs, out_ref = refs[: len(pieces)], refs[-1]
    sides = []
    for r in range(2):
        total = refs[len(pieces)][:, 128 * r : 128 * r + 128] if has_sum else None
        for j, e_ref in zip(pieces, e_refs, strict=True):
            part = nt(heads((a0, a1, a2, a3), j ^ r), half_rows(e_ref, r))
            total = part if total is None else total + part
        sides.append(total)
    for r in range(2):
        at = slice(128 * r, 128 * r + 128)
        if last:
            for k in range(4):
                out_ref[s_ref[1] ^ k, :, at] = sides[r][k * PAIR : (k + 1) * PAIR].astype(BF16)
        else:
            out_ref[:, at] = sides[r]


def scores(scalars, a, pieces, blocks, before, last):
    kernel = functools.partial(scores_kernel, pieces, before is not None, last)
    if last:
        out = jax.ShapeDtypeStruct((4, PAIR, ROWS), BF16)
    else:
        out = jax.ShapeDtypeStruct((4 * PAIR, ROWS), F32)
    args = (*a, *blocks) + (() if before is None else (before,))
    flops = len(pieces) * 2 * 512 * SPAN * ROWS
    return whole(kernel, len(args), out, cost(flops, 2 << 20))(scalars, *args)


def attend_kernel(count_ref, s_ref, out_ref):
    total = s_ref[0].astype(F32)
    for k in range(1, 4):
        total = total + s_ref[k].astype(F32)
    scores = total[0:GROUP] * INV
    grad_probs = total[GROUP:PAIR]
    count = count_ref[0]
    row = lax.broadcasted_iota(jnp.int32, scores.shape, 1)
    weighted = jnp.where(row < count * NBR_LEN, jnp.exp(scores), 0.0)
    empty = jnp.where(count == 0, 1.0, 0.0)
    probs = weighted / (jnp.sum(weighted, axis=1, keepdims=True) + empty)
    centre = jnp.sum(probs * grad_probs, axis=1, keepdims=True)
    grad_scores = probs * (grad_probs - centre) * INV
    both = jnp.concatenate([grad_scores, probs], axis=0).T.astype(BF16)
    for k in range(4):
        out_ref[k] = both


def attend(counts, s):
    out = jax.ShapeDtypeStruct((4, ROWS, PAIR), BF16)
    return whole(attend_kernel, 1, out, cost(1 << 20, 1 << 19))(counts, s)


def term_kernel(p2, s_ref, g_ref, a0, a1, a2, a3, out_ref):
    g = jnp.concatenate([g_ref[s_ref[1] ^ k] for k in range(4)], axis=1)
    for r in range(2):
        for pb in range(2):
            part = nn(g[128 * r : 128 * r + 128], heads((a0, a1, a2, a3), 2 * pb + (p2 ^ r)))
            for b in range(2):
                side = part[:, b * BLOCK : (b + 1) * BLOCK].astype(out_ref.dtype)
                zb = (s_ref[0] // 2) ^ pb
                out_ref[8 * r : 8 * r + 8, 2 * b + zb] = side.reshape(8, 16, BLOCK)


def term(scalars, g, a, p2, kind):
    out = jax.ShapeDtypeStruct(T_SHAPE, kind)
    kernel = functools.partial(term_kernel, p2)
    return whole(kernel, 5, out, cost(2 * 512 * 1024 * ROWS, 2 << 20))(scalars, g, *a)


def mix_kernel(s_ref, g_ref, e0, e1, e2, e3, *out_refs):
    gs = jnp.concatenate([g_ref[s_ref[1] ^ k, :, 0:GROUP] for k in range(4)], axis=1)
    gs = gs.astype(F32).T.astype(BF16)
    e_refs = (e0, e1, e2, e3)
    for p in range(4):
        e = jnp.concatenate([half_rows(e_refs[p ^ r], r) for r in range(2)], axis=0)
        part = nn(gs, e).astype(BF16)
        for k in range(4):
            out_refs[k][:, p * SPAN : (p + 1) * SPAN] = part[k * GROUP : (k + 1) * GROUP]


def mix(scalars, g, rows):
    out = [jax.ShapeDtypeStruct((GROUP, COLUMN), BF16)] * 4
    return whole(mix_kernel, 5, out, cost(2 * 256 * 256 * 2048, 2 << 20))(scalars, g, *rows)


def query_kernel(s_ref, x0, x1, x2, x3, w_ref, out_ref, acc_ref):
    b = pl.program_id(0)
    total = None
    for k, x_ref in enumerate((x0, x1, x2, x3)):
        for p in range(4):
            at = pl.ds(pl.multiple_of(p * SPAN + b * BLOCK, BLOCK), BLOCK)
            part = nn(x_ref[:, at], w_ref[0, s_ref[0] ^ p, s_ref[1] ^ k])
            total = part if total is None else total + part

    @pl.when(b == 0)
    def _():
        acc_ref[...] = total

    @pl.when(b == 1)
    def _():
        out_ref[...] = (acc_ref[...] + total).astype(BF16)


def query(scalars, x, wk):
    x_spec = pl.BlockSpec((GROUP, COLUMN), lambda i, s: (0, 0))
    return pl.pallas_call(
        query_kernel,
        grid_spec=pltpu.PrefetchScalarGridSpec(
            num_scalar_prefetch=1,
            grid=(2,),
            in_specs=[x_spec] * 4
            + [pl.BlockSpec((1, 4, 4, BLOCK, HEAD), lambda i, s: (i, 0, 0, 0, 0))],
            out_specs=pl.BlockSpec((GROUP, HEAD), lambda i, s: (0, 0)),
            scratch_shapes=[pltpu.VMEM((GROUP, HEAD), F32)],
        ),
        out_shape=jax.ShapeDtypeStruct((GROUP, HEAD), BF16),
        cost_estimate=cost(2 * 64 * 8192 * 128, 3 << 20),
        compiler_params=LIMIT,
    )(scalars, *x, wk)


def total_kernel(t_ref, out_ref):
    total = t_ref[:, 0].astype(F32)
    for b in range(1, 4):
        total = total + t_ref[:, b].astype(F32)
    out_ref[...] = total


def total_terms(terms):
    return pl.pallas_call(
        total_kernel,
        in_specs=[VMEM],
        out_specs=VMEM,
        out_shape=jax.ShapeDtypeStruct((16, 16, BLOCK), F32),
        cost_estimate=cost(1 << 18, 3 << 18),
        compiler_params=LIMIT,
    )(terms)


def local(encoded, w_key, w_value, queries, cotangent, counts):
    w = 2 * lax.axis_index("zb") + (lax.axis_index("zh") ^ lax.axis_index("z2"))
    scalars = jnp.stack([w, lax.axis_index("x")]).astype(jnp.int32)
    wk = w_key.reshape(2, 4, 4, BLOCK, HEAD)
    wv = w_value.reshape(2, 4, 4, BLOCK, HEAD)
    own = spread(jnp.broadcast_to(encoded[:, None], E_SHAPE), ROW_GROUPS)
    shared = to_members(project(scalars, queries[0], cotangent[0], wk, wv))
    rows = [own] + [swap(own, QUAD, j) for j in range(1, 4)]
    sums = scores(scalars, shared, (0, 1, 3), [rows[0], rows[1], rows[3]], None, False)
    sums = scores(scalars, shared, (2,), [rows[2]], sums, True)
    parts = lax.all_to_all(sums, "x", 0, 0, tiled=True)
    grads = lax.all_to_all(attend(counts.reshape(1), parts), "x", 0, 0, tiled=True)
    passed = swap(term(scalars, grads, shared, 1, BF16), QUAD, 1)
    kept = term(scalars, grads, shared, 0, F32)
    mixture = mix(scalars, grads, rows)
    kept, mixture = lax.optimization_barrier((kept, mixture))
    terms = spread((kept + passed.astype(F32)).astype(BF16), TERM_GROUPS)
    mixed = to_members(mixture)
    grad_queries = query(scalars, mixed, wk)
    grad_encoded = total_terms(terms)
    return grad_queries[None], grad_encoded


def solution(mesh):
    fine = Mesh(mesh.devices.reshape(tuple(AXES.values())), tuple(AXES))
    by_head = P(SECTION, None, TENSOR)
    return jax.shard_map(
        local,
        mesh=fine,
        in_specs=(P(None, SECTION, TENSOR), by_head, by_head, by_head, by_head, P(SECTION, None)),
        out_specs=(by_head, P(None, SECTION, TENSOR)),
        check_vma=False,
    )
```

time: 150 us -> 148 us (0.987)
  other arithmetic: 3.37 us -> 1.6 us
    all_to_all x2, waiting for transfers between devices: 23.2 us -> 12.3 us  [spread(): lax.all_to_all(blocks.reshape(-1, 16, BLOCK), SPREAD_AXES, 0, 0, axis_ind...]
    ppermute x8 -> x10, waiting for transfers between devices: 27.2 us -> 37.3 us  [swap(): return lax.ppermute(array, axes, [(i, i ^ k) for i in range(4)])]
    ppermute x8 -> x10, starting transfers between devices: 24.9 us -> 30.5 us  [swap(): return lax.ppermute(array, axes, [(i, i ^ k) for i in range(4)])]
    all_to_all x2, starting transfers between devices: 34.7 us -> 29.8 us  [spread(): lax.all_to_all(blocks.reshape(-1, 16, BLOCK), SPREAD_AXES, 0, 0, axis_ind...]
    reduce_sum x1 -> x0, other arithmetic: 1.84 us -> none  [local(): grad_encoded = jnp.sum(terms.astype(F32), axis=1)]
    pallas_call x6 -> x7, Pallas kernels: 8.41 us -> 8.16 us  [the longest x2 2.49 us: scores(): return whole(kernel, len(args), out, cost(flops, 2 << 20))(scalars, *args)]
  transfers between devices with their start and end apart: 11 -> 13, of which waited for: 9 -> 9; matrix products, arithmetic and copies ran while one was open for 0% -> 0% of each run, Pallas kernels for 7% -> 7%
where the time goes in v5:
time: 148 us; the launch traced here: 147 us
  starting transfers between devices  64.3 us (43%)
  waiting for transfers between devices  54.7 us (37%)
  Pallas kernels  13.4 us (9%)
  blocking collectives  7.92 us (5%)
  local copies, waits for them, and re-layouts  3.39 us (2%)
  other arithmetic  1.6 us (1%)
  between operations  1.52 us (1%)
    ppermute x10, waiting for transfers between devices, swap(): return lax.ppermute(array, axes, [(i, i ^ k) for i in range(4)])  37.3 us
    ppermute x10, starting transfers between devices, swap(): return lax.ppermute(array, axes, [(i, i ^ k) for i in range(4)])  30.5 us
    all_to_all x2, starting transfers between devices, spread(): lax.all_to_all(blocks.reshape(-1, 16, BLOCK), SPREAD_AXES, 0, 0, axis_ind...  29.8 us
    all_to_all x2, waiting for transfers between devices, spread(): lax.all_to_all(blocks.reshape(-1, 16, BLOCK), SPREAD_AXES, 0, 0, axis_ind...  12.3 us
    all_to_all x1, blocking collectives, local(): lax.all_to_all(attend(counts.reshape(1), parts), 'x', 0, 0, tiled=True)  7.92 us
    all_to_all x1, waiting for transfers between devices, local(): parts = lax.all_to_all(sums, 'x', 0, 0, tiled=True)  5.01 us
    pallas_call x1, Pallas kernels, project(): pl.pallas_call(project_kernel, in_specs=[SMEM] + [HBM] * 4, out_specs=[VM...  4.96 us
    all_to_all x1, starting transfers between devices, local(): parts = lax.all_to_all(sums, 'x', 0, 0, tiled=True)  4.01 us
  transfers between devices with their start and end apart: 13, of which 9 were waited for; matrix products, arithmetic and copies ran while one was open for 0% of the time, Pallas kernels for 7%

profile of v5, /device:TPU:1, one launch (start us, length us, event | category | flops | bytes accessed | tf_op | source)
XLA Modules:
  0.0 146.8 jit_solution(18306881738587847214)
XLA Ops:
  0.6 1.6 %broadcast_in_dim.4 = bf16[16,2,16,256]{3,2,1,0:T(8,128)(2,1)} broadcast(bf16[16,16,256]{2,1,0:T(8,128)(2,1)} %param.6), dimensions={0,2,3} | broadcast | bytes 393216 | tf_op jit(solution)/shard_map/broadcast_in_dim | solution.py:277
  2.3 18.9 %all-to-all-start = ((bf16[32,16,256]{2,1,0:T(8,128)(2,1)}), bf16[32,16,256]{2,1,0:T(8,128)(2,1)S(1)}, u32[]{:S(2)}, u32[]{:S(2)}) async-start(bf16[32,16,256]{2,1,0:T(8,128)(2,1)} %bitcast.7), calls=%async_computation | async-start | bytes 524288 | tf_op jit(solution)/shard_map/all_to_all | solution.py:36
  21.2 0.6 pad_add_fusion.s_ref
  21.8 0.0 copy-start.4
  21.8 5.0 %shard_map.77 = (bf16[128,2048]{1,0:T(8,128)(2,1)}, bf16[128,2048]{1,0:T(8,128)(2,1)}, bf16[128,2048]{1,0:T(8,128)(2,1)}, bf16[128,2048]{1,0:T(8,128)(2,1)}) custom-call(s32[2]{0:T(128)} %pad_add_fusion.s_ref, bf16[64,128]{1,0:T(8,128)(2,1)} %bitcast.23, bf16[64,128]{1,0:T(8,128)(2,1)} %bitcast.24, bf16[2,4,4,256,128]{4,3,2,1,0:T(8,128)(2,1)} %bitcast.13, ...), custom_call_target="tpu_custom_call" | custom-call | flops 268435456 | bytes 6291456 | tf_op jit(solution)/shard_map/pallas_call | solution.py:109
  26.8 3.1 %collective-permute-start = (bf16[128,2048]{1,0:T(8,128)(2,1)}, bf16[128,2048]{1,0:T(8,128)(2,1)S(1)}, u32[]{:S(2)}, u32[]{:S(2)}) collective-permute-start(bf16[128,2048]{1,0:T(8,128)(2,1)} %get-tuple-element.16), channel_id=1, source_target_pairs={{0,1},{1,0},{2,3},{3,2},{4,5},{5,4},{6,7},{7,6},{8,9},{9,8},{10,11... | collective-permute-start | bytes 1572872 | tf_op jit(solution)/shard_map/ppermute | solution.py:43
  29.9 4.4 %collective-permute-start.1 = (bf16[128,2048]{1,0:T(8,128)(2,1)}, bf16[128,2048]{1,0:T(8,128)(2,1)S(1)}, u32[]{:S(2)}, u32[]{:S(2)}) collective-permute-start(bf16[128,2048]{1,0:T(8,128)(2,1)} %get-tuple-element.17), channel_id=1, source_target_pairs={{0,2},{1,3},{2,0},{3,1},{4,6},{5,7},{6,4},{7,5},{8,10},{9,11},{10,... | collective-permute-start | bytes 1572872 | tf_op jit(solution)/shard_map/ppermute | solution.py:43
  34.3 2.1 %collective-permute-start.2 = (bf16[128,2048]{1,0:T(8,128)(2,1)}, bf16[128,2048]{1,0:T(8,128)(2,1)S(1)}, u32[]{:S(2)}, u32[]{:S(2)}) collective-permute-start(bf16[128,2048]{1,0:T(8,128)(2,1)} %get-tuple-element.18), channel_id=1, source_target_pairs={{0,3},{1,2},{2,1},{3,0},{4,7},{5,6},{6,5},{7,4},{8,11},{9,10},{10,... | collective-permute-start | bytes 1572872 | tf_op jit(solution)/shard_map/ppermute | solution.py:43
  36.4 5.0 %all-to-all-done = bf16[32,16,256]{2,1,0:T(8,128)(2,1)S(1)} async-done(((bf16[32,16,256]{2,1,0:T(8,128)(2,1)}), bf16[32,16,256]{2,1,0:T(8,128)(2,1)S(1)}, u32[]{:S(2)}, u32[]{:S(2)}) %all-to-all-start) | async-done | bytes 262176 | tf_op jit(solution)/shard_map/all_to_all | solution.py:36
  41.3 4.6 %collective-permute-start.5 = (bf16[16,2,16,256]{3,2,1,0:T(8,128)(2,1)S(1)}, bf16[16,2,16,256]{3,2,1,0:T(8,128)(2,1)S(1)}, u32[]{:S(2)}, u32[]{:S(2)}) collective-permute-start(bf16[16,2,16,256]{3,2,1,0:T(8,128)(2,1)S(1)} %bitcast.15), channel_id=1, source_target_pairs={{0,12},{4,8},{8,4},{12,0},{1,13},{5,9},{9,5},{13,1},{2,14},{6,10},... | collective-permute-start | bytes 786440 | tf_op jit(solution)/shard_map/ppermute | solution.py:43
  45.9 2.5 %collective-permute-start.4 = (bf16[16,2,16,256]{3,2,1,0:T(8,128)(2,1)S(1)}, bf16[16,2,16,256]{3,2,1,0:T(8,128)(2,1)S(1)}, u32[]{:S(2)}, u32[]{:S(2)}) collective-permute-start(bf16[16,2,16,256]{3,2,1,0:T(8,128)(2,1)S(1)} %bitcast.16), channel_id=1, source_target_pairs={{0,4},{4,0},{8,12},{12,8},{1,5},{5,1},{9,13},{13,9},{2,6},{6,2},{1... | collective-permute-start | bytes 786440 | tf_op jit(solution)/shard_map/ppermute | solution.py:43
  48.4 0.0 collective-permute-done.a1
  48.4 2.4 %collective-permute-start.3 = (bf16[16,2,16,256]{3,2,1,0:T(8,128)(2,1)S(1)}, bf16[16,2,16,256]{3,2,1,0:T(8,128)(2,1)S(1)}, u32[]{:S(2)}, u32[]{:S(2)}) collective-permute-start(bf16[16,2,16,256]{3,2,1,0:T(8,128)(2,1)S(1)} %bitcast.17), channel_id=1, source_target_pairs={{0,8},{4,12},{8,0},{12,4},{1,9},{5,13},{9,1},{13,5},{2,10},{6,14},... | collective-permute-start | bytes 786440 | tf_op jit(solution)/shard_map/ppermute | solution.py:43
  50.8 4.8 %collective-permute-done.1.a2 = bf16[128,2048]{1,0:T(8,128)(2,1)S(1)} collective-permute-done((bf16[128,2048]{1,0:T(8,128)(2,1)}, bf16[128,2048]{1,0:T(8,128)(2,1)S(1)}, u32[]{:S(2)}, u32[]{:S(2)}) %collective-permute-start.1) | collective-permute-done | bytes 524320 | tf_op jit(solution)/shard_map/ppermute | solution.py:43
  55.7 5.8 %collective-permute-done.2.a3 = bf16[128,2048]{1,0:T(8,128)(2,1)S(1)} collective-permute-done((bf16[128,2048]{1,0:T(8,128)(2,1)}, bf16[128,2048]{1,0:T(8,128)(2,1)S(1)}, u32[]{:S(2)}, u32[]{:S(2)}) %collective-permute-start.2) | collective-permute-done | bytes 524320 | tf_op jit(solution)/shard_map/ppermute | solution.py:43
  61.5 0.0 collective-permute-done.5.refs_2_.e3
  61.5 0.0 collective-permute-done.4.refs_1_.e1
  61.5 0.0 copy-done.4
  61.5 0.0 copy-start.1
  61.5 1.0 copy-done.1
  62.5 1.5 %shard_map.78.refs_1_ = f32[512,256]{1,0:T(8,128)S(1)} custom-call(s32[2]{0:T(128)S(1)} %copy-done.4, bf16[128,2048]{1,0:T(8,128)(2,1)S(1)} %copy-done.1, bf16[128,2048]{1,0:T(8,128)(2,1)S(1)} %collective-permute-done.a1, bf16[128,2048]{1,0:T(8,128)(2,1)S(1)} %collective-permute-done.1.a2, bf16[128,2048]{1,0:T(8,128)(2,1)S(1)} %collective-permute-done.2.a3, ...), custom_call_target="tpu_custom_call" | custom-call | flops 402653184 | bytes 2097152 | tf_op jit(solution)/shard_map/pallas_call | solution.py:159
  64.1 0.0 copy-start.2
  64.1 6.0 %collective-permute-done.3.refs_0_.e2 = bf16[16,2,16,256]{3,2,1,0:T(8,128)(2,1)S(1)} collective-permute-done((bf16[16,2,16,256]{3,2,1,0:T(8,128)(2,1)S(1)}, bf16[16,2,16,256]{3,2,1,0:T(8,128)(2,1)S(1)}, u32[]{:S(2)}, u32[]{:S(2)}) %collective-permute-start.3) | collective-permute-done | bytes 262176 | tf_op jit(solution)/shard_map/ppermute | solution.py:43
  70.1 1.0 shard_map.79
  71.1 0.0 copy-start.3
  71.1 0.7 copy-done.3
  71.8 4.0 %all-to-all-start.1 = ((bf16[4,128,256]{2,1,0:T(8,128)(2,1)}), bf16[4,128,256]{2,1,0:T(8,128)(2,1)S(1)}, u32[]{:S(2)}, u32[]{:S(2)}) async-start(bf16[4,128,256]{2,1,0:T(8,128)(2,1)} %copy-done.3), calls=%async_computation.1 | async-start | bytes 524288 | tf_op jit(solution)/shard_map/all_to_all | solution.py:282
  76.5 5.0 %all-to-all-done.1.s_ref = bf16[4,128,256]{2,1,0:T(8,128)(2,1)S(1)} async-done(((bf16[4,128,256]{2,1,0:T(8,128)(2,1)}), bf16[4,128,256]{2,1,0:T(8,128)(2,1)S(1)}, u32[]{:S(2)}, u32[]{:S(2)}) %all-to-all-start.1) | async-done | bytes 262176 | tf_op jit(solution)/shard_map/all_to_all | solution.py:282
  81.5 0.3 shard_map.80
  81.8 7.9 %all_to_all.20.g_ref = bf16[4,256,128]{2,1,0:T(8,128)(2,1)S(1)} all-to-all(bf16[4,256,128]{2,1,0:T(8,128)(2,1)S(1)} %shard_map.80), channel_id=1, replica_groups=mesh['zh'=2,'y'=4,'c'=2,'za'=2,'zb'=2,'z2'=2,'x'=4] {'x'}, dimensions={0} | all-to-all | bytes 524288 | tf_op jit(solution)/shard_map/all_to_all | solution.py:283
  89.7 0.0 copy-done.2
  89.7 1.0 shard_map.84
  90.7 1.9 %collective-permute-start.9 = (bf16[16,4,16,256]{3,2,1,0:T(8,128)(2,1)S(1)}, bf16[16,4,16,256]{3,2,1,0:T(8,128)(2,1)S(1)}, u32[]{:S(2)}, u32[]{:S(2)}) collective-permute-start(bf16[16,4,16,256]{3,2,1,0:T(8,128)(2,1)S(1)} %shard_map.84), channel_id=1, source_target_pairs={{0,4},{4,0},{8,12},{12,8},{1,5},{5,1},{9,13},{13,9},{2,6},{6,2},{1... | collective-permute-start | bytes 1572872 | tf_op jit(solution)/shard_map/ppermute | solution.py:43
  92.6 1.1 shard_map.82
  93.7 0.0 copy-start.5
  93.7 0.0 copy-start.6
  93.7 0.0 copy-start.7
  93.7 1.0 shard_map.81
  94.7 0.0 copy-start
  94.8 8.1 %collective-permute-done.9 = bf16[16,4,16,256]{3,2,1,0:T(8,128)(2,1)S(1)} collective-permute-done((bf16[16,4,16,256]{3,2,1,0:T(8,128)(2,1)S(1)}, bf16[16,4,16,256]{3,2,1,0:T(8,128)(2,1)S(1)}, u32[]{:S(2)}, u32[]{:S(2)}) %collective-permute-start.9) | collective-permute-done | bytes 524320 | tf_op jit(solution)/shard_map/ppermute | solution.py:43
  102.9 1.0 add_convert_fusion
  103.9 0.0 copy-done.5
  103.9 0.0 copy-done.6
  103.9 0.0 copy-done.7
  103.9 10.8 %all-to-all-start.3 = ((bf16[64,16,256]{2,1,0:T(8,128)(2,1)}), bf16[64,16,256]{2,1,0:T(8,128)(2,1)S(1)}, u32[]{:S(2)}, u32[]{:S(2)}) async-start(bf16[64,16,256]{2,1,0:T(8,128)(2,1)} %bitcast.22), calls=%async_computation.3 | async-start | bytes 1048576 | tf_op jit(solution)/shard_map/all_to_all | solution.py:36
  114.7 2.2 %collective-permute-start.6 = (bf16[64,2048]{1,0:T(8,128)(2,1)}, bf16[64,2048]{1,0:T(8,128)(2,1)S(1)}, u32[]{:S(2)}, u32[]{:S(2)}) collective-permute-start(bf16[64,2048]{1,0:T(8,128)(2,1)} %copy-done.7), channel_id=1, source_target_pairs={{0,1},{1,0},{2,3},{3,2},{4,5},{5,4},{6,7},{7,6},{8,9},{9,8},{10,11... | collective-permute-start | bytes 786440 | tf_op jit(solution)/shard_map/ppermute | solution.py:43
  116.9 3.7 %collective-permute-start.7 = (bf16[64,2048]{1,0:T(8,128)(2,1)}, bf16[64,2048]{1,0:T(8,128)(2,1)S(1)}, u32[]{:S(2)}, u32[]{:S(2)}) collective-permute-start(bf16[64,2048]{1,0:T(8,128)(2,1)} %copy-done.6), channel_id=1, source_target_pairs={{0,2},{1,3},{2,0},{3,1},{4,6},{5,7},{6,4},{7,5},{8,10},{9,11},{10,... | collective-permute-start | bytes 786440 | tf_op jit(solution)/shard_map/ppermute | solution.py:43
  120.6 3.7 %collective-permute-start.8 = (bf16[64,2048]{1,0:T(8,128)(2,1)}, bf16[64,2048]{1,0:T(8,128)(2,1)S(1)}, u32[]{:S(2)}, u32[]{:S(2)}) collective-permute-start(bf16[64,2048]{1,0:T(8,128)(2,1)} %copy-done.5), channel_id=1, source_target_pairs={{0,3},{1,2},{2,1},{3,0},{4,7},{5,6},{6,5},{7,4},{8,11},{9,10},{10,... | collective-permute-start | bytes 786440 | tf_op jit(solution)/shard_map/ppermute | solution.py:43
  124.3 0.0 collective-permute-done.6.x1
  124.3 6.2 %collective-permute-done.7.x2 = bf16[64,2048]{1,0:T(8,128)(2,1)S(1)} collective-permute-done((bf16[64,2048]{1,0:T(8,128)(2,1)}, bf16[64,2048]{1,0:T(8,128)(2,1)S(1)}, u32[]{:S(2)}, u32[]{:S(2)}) %collective-permute-start.7) | collective-permute-done | bytes 262176 | tf_op jit(solution)/shard_map/ppermute | solution.py:43
  130.5 6.4 %collective-permute-done.8.x3 = bf16[64,2048]{1,0:T(8,128)(2,1)S(1)} collective-permute-done((bf16[64,2048]{1,0:T(8,128)(2,1)}, bf16[64,2048]{1,0:T(8,128)(2,1)S(1)}, u32[]{:S(2)}, u32[]{:S(2)}) %collective-permute-start.8) | collective-permute-done | bytes 262176 | tf_op jit(solution)/shard_map/ppermute | solution.py:43
  136.9 0.0 copy-done
  136.9 1.8 %shard_map.83 = bf16[64,128]{1,0:T(8,128)(2,1)} custom-call(s32[2]{0:T(128)S(1)} %copy-done.4, bf16[64,2048]{1,0:T(8,128)(2,1)S(1)} %get-tuple-element.23.x0, bf16[64,2048]{1,0:T(8,128)(2,1)S(1)} %collective-permute-done.6.x1, bf16[64,2048]{1,0:T(8,128)(2,1)S(1)} %collective-permute-done.7.x2, bf16[64,2048]{1,0:T(8,128)(2,1)S(1)} %collective-permute-done.8.x3, ...), custom_call_target="tpu_custom_call" | custom-call | flops 134217728 | bytes 3145728 | tf_op jit(solution)/shard_map/pallas_call | solution.py:238
  138.7 7.4 %all-to-all-done.3 = bf16[64,16,256]{2,1,0:T(8,128)(2,1)S(1)} async-done(((bf16[64,16,256]{2,1,0:T(8,128)(2,1)}), bf16[64,16,256]{2,1,0:T(8,128)(2,1)S(1)}, u32[]{:S(2)}, u32[]{:S(2)}) %all-to-all-start.3) | async-done | bytes 524320 | tf_op jit(solution)/shard_map/all_to_all | solution.py:36
  146.1 0.8 shard_map.85
Async XLA Ops:
  2.3 39.1 %all-to-all-start = ((bf16[32,16,256]{2,1,0:T(8,128)(2,1)}), bf16[32,16,256]{2,1,0:T(8,128)(2,1)S(1)}, u32[]{:S(2)}, u32[]{:S(2)}) async-start(bf16[32,16,256]{2,1,0:T(8,128)(2,1)} %bitcast.7), calls=%async_computation | async-start | bytes 524288 | tf_op jit(solution)/shard_map/all_to_all | solution.py:36
  21.8 39.7 %copy-start.4 = (s32[2]{0:T(128)S(1)}, s32[2]{0:T(128)}, u32[]{:S(2)}) copy-start(s32[2]{0:T(128)} %pad_add_fusion.s_ref) | copy-start | bytes 28
  26.8 21.6 %collective-permute-start = (bf16[128,2048]{1,0:T(8,128)(2,1)}, bf16[128,2048]{1,0:T(8,128)(2,1)S(1)}, u32[]{:S(2)}, u32[]{:S(2)}) collective-permute-start(bf16[128,2048]{1,0:T(8,128)(2,1)} %get-tuple-element.16), channel_id=1, source_target_pairs={{0,1},{1,0},{2,3},{3,2},{4,5},{5,4},{6,7},{7,6},{8,9},{9,8},{10,11... | collective-permute-start | bytes 1572872 | tf_op jit(solution)/shard_map/ppermute | solution.py:43
  29.9 25.8 %collective-permute-start.1 = (bf16[128,2048]{1,0:T(8,128)(2,1)}, bf16[128,2048]{1,0:T(8,128)(2,1)S(1)}, u32[]{:S(2)}, u32[]{:S(2)}) collective-permute-start(bf16[128,2048]{1,0:T(8,128)(2,1)} %get-tuple-element.17), channel_id=1, source_target_pairs={{0,2},{1,3},{2,0},{3,1},{4,6},{5,7},{6,4},{7,5},{8,10},{9,11},{10,... | collective-permute-start | bytes 1572872 | tf_op jit(solution)/shard_map/ppermute | solution.py:43
  34.3 27.2 %collective-permute-start.2 = (bf16[128,2048]{1,0:T(8,128)(2,1)}, bf16[128,2048]{1,0:T(8,128)(2,1)S(1)}, u32[]{:S(2)}, u32[]{:S(2)}) collective-permute-start(bf16[128,2048]{1,0:T(8,128)(2,1)} %get-tuple-element.18), channel_id=1, source_target_pairs={{0,3},{1,2},{2,1},{3,0},{4,7},{5,6},{6,5},{7,4},{8,11},{9,10},{10,... | collective-permute-start | bytes 1572872 | tf_op jit(solution)/shard_map/ppermute | solution.py:43
  41.3 20.1 %collective-permute-start.5 = (bf16[16,2,16,256]{3,2,1,0:T(8,128)(2,1)S(1)}, bf16[16,2,16,256]{3,2,1,0:T(8,128)(2,1)S(1)}, u32[]{:S(2)}, u32[]{:S(2)}) collective-permute-start(bf16[16,2,16,256]{3,2,1,0:T(8,128)(2,1)S(1)} %bitcast.15), channel_id=1, source_target_pairs={{0,12},{4,8},{8,4},{12,0},{1,13},{5,9},{9,5},{13,1},{2,14},{6,10},... | collective-permute-start | bytes 786440 | tf_op jit(solution)/shard_map/ppermute | solution.py:43
  45.9 15.6 %collective-permute-start.4 = (bf16[16,2,16,256]{3,2,1,0:T(8,128)(2,1)S(1)}, bf16[16,2,16,256]{3,2,1,0:T(8,128)(2,1)S(1)}, u32[]{:S(2)}, u32[]{:S(2)}) collective-permute-start(bf16[16,2,16,256]{3,2,1,0:T(8,128)(2,1)S(1)} %bitcast.16), channel_id=1, source_target_pairs={{0,4},{4,0},{8,12},{12,8},{1,5},{5,1},{9,13},{13,9},{2,6},{6,2},{1... | collective-permute-start | bytes 786440 | tf_op jit(solution)/shard_map/ppermute | solution.py:43
  48.4 21.7 %collective-permute-start.3 = (bf16[16,2,16,256]{3,2,1,0:T(8,128)(2,1)S(1)}, bf16[16,2,16,256]{3,2,1,0:T(8,128)(2,1)S(1)}, u32[]{:S(2)}, u32[]{:S(2)}) collective-permute-start(bf16[16,2,16,256]{3,2,1,0:T(8,128)(2,1)S(1)} %bitcast.17), channel_id=1, source_target_pairs={{0,8},{4,12},{8,0},{12,4},{1,9},{5,13},{9,1},{13,5},{2,10},{6,14},... | collective-permute-start | bytes 786440 | tf_op jit(solution)/shard_map/ppermute | solution.py:43
  61.5 1.0 copy-start.1
  64.1 25.6 %copy-start.2 = (bf16[128,2048]{1,0:T(8,128)(2,1)S(1)}, bf16[128,2048]{1,0:T(8,128)(2,1)}, u32[]{:S(2)}) copy-start(bf16[128,2048]{1,0:T(8,128)(2,1)} %get-tuple-element.15.a0) | copy-start | bytes 1572868
  71.1 0.7 copy-start.3
  71.8 9.7 %all-to-all-start.1 = ((bf16[4,128,256]{2,1,0:T(8,128)(2,1)}), bf16[4,128,256]{2,1,0:T(8,128)(2,1)S(1)}, u32[]{:S(2)}, u32[]{:S(2)}) async-start(bf16[4,128,256]{2,1,0:T(8,128)(2,1)} %copy-done.3), calls=%async_computation.1 | async-start | bytes 524288 | tf_op jit(solution)/shard_map/all_to_all | solution.py:282
  90.7 12.2 %collective-permute-start.9 = (bf16[16,4,16,256]{3,2,1,0:T(8,128)(2,1)S(1)}, bf16[16,4,16,256]{3,2,1,0:T(8,128)(2,1)S(1)}, u32[]{:S(2)}, u32[]{:S(2)}) collective-permute-start(bf16[16,4,16,256]{3,2,1,0:T(8,128)(2,1)S(1)} %shard_map.84), channel_id=1, source_target_pairs={{0,4},{4,0},{8,12},{12,8},{1,5},{5,1},{9,13},{13,9},{2,6},{6,2},{1... | collective-permute-start | bytes 1572872 | tf_op jit(solution)/shard_map/ppermute | solution.py:43
  93.7 10.2 %copy-start.5 = (bf16[64,2048]{1,0:T(8,128)(2,1)}, bf16[64,2048]{1,0:T(8,128)(2,1)S(1)}, u32[]{:S(2)}) copy-start(bf16[64,2048]{1,0:T(8,128)(2,1)S(1)} %get-tuple-element.26) | copy-start | bytes 786436
  93.7 10.2 %copy-start.6 = (bf16[64,2048]{1,0:T(8,128)(2,1)}, bf16[64,2048]{1,0:T(8,128)(2,1)S(1)}, u32[]{:S(2)}) copy-start(bf16[64,2048]{1,0:T(8,128)(2,1)S(1)} %get-tuple-element.25) | copy-start | bytes 786436
  93.7 10.1 %copy-start.7 = (bf16[64,2048]{1,0:T(8,128)(2,1)}, bf16[64,2048]{1,0:T(8,128)(2,1)S(1)}, u32[]{:S(2)}) copy-start(bf16[64,2048]{1,0:T(8,128)(2,1)S(1)} %get-tuple-element.24) | copy-start | bytes 786436
  94.7 42.1 %copy-start = (bf16[1,8192,128]{2,1,0:T(8,128)(2,1)S(1)}, bf16[1,8192,128]{2,1,0:T(8,128)(2,1)}, u32[]{:S(2)}) copy-start(bf16[1,8192,128]{2,1,0:T(8,128)(2,1)} %param.7) | copy-start | bytes 6291460
  103.9 42.2 %all-to-all-start.3 = ((bf16[64,16,256]{2,1,0:T(8,128)(2,1)}), bf16[64,16,256]{2,1,0:T(8,128)(2,1)S(1)}, u32[]{:S(2)}, u32[]{:S(2)}) async-start(bf16[64,16,256]{2,1,0:T(8,128)(2,1)} %bitcast.22), calls=%async_computation.3 | async-start | bytes 1048576 | tf_op jit(solution)/shard_map/all_to_all | solution.py:36
  114.7 9.6 %collective-permute-start.6 = (bf16[64,2048]{1,0:T(8,128)(2,1)}, bf16[64,2048]{1,0:T(8,128)(2,1)S(1)}, u32[]{:S(2)}, u32[]{:S(2)}) collective-permute-start(bf16[64,2048]{1,0:T(8,128)(2,1)} %copy-done.7), channel_id=1, source_target_pairs={{0,1},{1,0},{2,3},{3,2},{4,5},{5,4},{6,7},{7,6},{8,9},{9,8},{10,11... | collective-permute-start | bytes 786440 | tf_op jit(solution)/shard_map/ppermute | solution.py:43
  116.9 13.6 %collective-permute-start.7 = (bf16[64,2048]{1,0:T(8,128)(2,1)}, bf16[64,2048]{1,0:T(8,128)(2,1)S(1)}, u32[]{:S(2)}, u32[]{:S(2)}) collective-permute-start(bf16[64,2048]{1,0:T(8,128)(2,1)} %copy-done.6), channel_id=1, source_target_pairs={{0,2},{1,3},{2,0},{3,1},{4,6},{5,7},{6,4},{7,5},{8,10},{9,11},{10,... | collective-permute-start | bytes 786440 | tf_op jit(solution)/shard_map/ppermute | solution.py:43
  120.6 16.3 %collective-permute-start.8 = (bf16[64,2048]{1,0:T(8,128)(2,1)}, bf16[64,2048]{1,0:T(8,128)(2,1)S(1)}, u32[]{:S(2)}, u32[]{:S(2)}) collective-permute-start(bf16[64,2048]{1,0:T(8,128)(2,1)} %copy-done.5), channel_id=1, source_target_pairs={{0,3},{1,2},{2,1},{3,0},{4,7},{5,6},{6,5},{7,4},{8,11},{9,10},{10,... | collective-permute-start | bytes 786440 | tf_op jit(solution)/shard_map/ppermute | solution.py:43

commit v6 on v5

--- a/solution.py
+++ b/solution.py
@@ -78,15 +78,17 @@
     )
 
 
-def project_kernel(s_ref, q_hbm, ct_hbm, wk_hbm, wv_hbm, o0, o1, o2, o3, rows, weights, sems):
+def project_kernel(q_hbm, ct_hbm, wk_hbm, wv_hbm, o1, o2, o3, rows, weights, sems):
+    w = 2 * lax.axis_index("zb") + (lax.axis_index("zh") ^ lax.axis_index("z2"))
+    x = lax.axis_index("x")
     small = [
         pltpu.make_async_copy(src, rows.at[i], sems.at[4 + i])
         for i, src in enumerate((q_hbm, ct_hbm))
     ]
     large = [
         [
-            pltpu.make_async_copy(w.at[b], weights.at[i, b], sems.at[2 * b + i])
-            for i, w in enumerate((wk_hbm, wv_hbm))
+            pltpu.make_async_copy(src.at[b], weights.at[i, b], sems.at[2 * b + i])
+            for i, src in enumerate((wk_hbm, wv_hbm))
         ]
         for b in range(2)
     ]
@@ -97,27 +99,58 @@
     for b in range(2):
         for c in large[b]:
             c.wait()
-        for k, out_ref in enumerate((o0, o1, o2, o3)):
+        for k, out_ref in enumerate((o1, o2, o3), 1):
             for p in range(4):
                 at = slice(p * SPAN + b * BLOCK, p * SPAN + (b + 1) * BLOCK)
                 for i in range(2):
-                    part = nt(rows[i], weights[i, b, s_ref[0] ^ p, s_ref[1] ^ k])
+                    part = nt(rows[i], weights[i, b, w ^ p, x ^ k])
                     out_ref[i * GROUP : (i + 1) * GROUP, at] = part.astype(BF16)
 
 
-def project(scalars, q, ct, wk, wv):
+def project(q, ct, wk, wv):
     return pl.pallas_call(
         project_kernel,
-        in_specs=[SMEM] + [HBM] * 4,
-        out_specs=[VMEM] * 4,
-        out_shape=[jax.ShapeDtypeStruct((PAIR, COLUMN), BF16)] * 4,
+        in_specs=[HBM] * 4,
+        out_specs=[VMEM] * 3,
+        out_shape=[jax.ShapeDtypeStruct((PAIR, COLUMN), BF16)] * 3,
         scratch_shapes=[
             pltpu.VMEM((2, GROUP, HEAD), BF16),
             pltpu.VMEM((2, 2, 4, 4, BLOCK, HEAD), BF16),
             pltpu.SemaphoreType.DMA((6,)),
         ],
-        cost_estimate=cost(2 * 128 * 8192 * 128, 6 << 20),
+        cost_estimate=cost(2 * 128 * 6144 * 128, 6 << 20),
         compiler_params=ALONE,
+    )(q, ct, wk, wv)
+
+
+def project_own_kernel(s_ref, q_ref, ct_ref, wk_hbm, wv_hbm, out_ref, weights, sems):
+    copies = [
+        pltpu.make_async_copy(src.at[:, :, s_ref[1]], weights.at[i], sems.at[i])
+        for i, src in enumerate((wk_hbm, wv_hbm))
+    ]
+    for c in copies:
+        c.start()
+    for i, r_ref in enumerate((q_ref, ct_ref)):
+        copies[i].wait()
+        for p in range(4):
+            for b in range(2):
+                at = slice(p * SPAN + b * BLOCK, p * SPAN + (b + 1) * BLOCK)
+                part = nt(r_ref[...], weights[i, b, s_ref[0] ^ p])
+                out_ref[i * GROUP : (i + 1) * GROUP, at] = part.astype(BF16)
+
+
+def project_own(scalars, q, ct, wk, wv):
+    return pl.pallas_call(
+        project_own_kernel,
+        in_specs=[SMEM, VMEM, VMEM, HBM, HBM],
+        out_specs=VMEM,
+        out_shape=jax.ShapeDtypeStruct((PAIR, COLUMN), BF16),
+        scratch_shapes=[
+            pltpu.VMEM((2, 2, 4, BLOCK, HEAD), BF16),
+            pltpu.SemaphoreType.DMA((2,)),
+        ],
+        cost_estimate=cost(2 * 128 * 2048 * 128, 2 << 20),
+        compiler_params=LIMIT,
     )(scalars, q, ct, wk, wv)
 
 
@@ -125,38 +158,30 @@
     return jnp.concatenate([r[:, p * SPAN : (p + 1) * SPAN] for r in a_refs], axis=0)
 
 
-def half_rows(e_ref, r):
-    halves = [e_ref[8 * r : 8 * r + 8, b].reshape(128, BLOCK) for b in range(2)]
-    return jnp.concatenate(halves, axis=1)
-
-
-def scores_kernel(pieces, has_sum, last, s_ref, a0, a1, a2, a3, *refs):
-    e_refs, out_ref = refs[: len(pieces)], refs[-1]
-    sides = []
+def half_rows(e_refs, j, r):
+    if j < 2:
+        halves = [e_refs[j][8 * r : 8 * r + 8, b] for b in range(2)]
+    else:
+        halves = [e_refs[2 * j - 2 + r][:, b] for b in range(2)]
+    return jnp.concatenate([h.reshape(128, BLOCK) for h in halves], axis=1)
+
+
+def scores_kernel(s_ref, a0, a1, a2, a3, *refs):
+    e_refs, out_ref = refs[:-1], refs[-1]
     for r in range(2):
-        total = refs[len(pieces)][:, 128 * r : 128 * r + 128] if has_sum else None
-        for j, e_ref in zip(pieces, e_refs, strict=True):
-            part = nt(heads((a0, a1, a2, a3), j ^ r), half_rows(e_ref, r))
+        total = None
+        for j in range(4):
+            part = nt(heads((a0, a1, a2, a3), j ^ r), half_rows(e_refs, j, r))
             total = part if total is None else total + part
-        sides.append(total)
-    for r in range(2):
-        at = slice(128 * r, 128 * r + 128)
-        if last:
-            for k in range(4):
-                out_ref[s_ref[1] ^ k, :, at] = sides[r][k * PAIR : (k + 1) * PAIR].astype(BF16)
-        else:
-            out_ref[:, at] = sides[r]
-
-
-def scores(scalars, a, pieces, blocks, before, last):
-    kernel = functools.partial(scores_kernel, pieces, before is not None, last)
-    if last:
-        out = jax.ShapeDtypeStruct((4, PAIR, ROWS), BF16)
-    else:
-        out = jax.ShapeDtypeStruct((4 * PAIR, ROWS), F32)
-    args = (*a, *blocks) + (() if before is None else (before,))
-    flops = len(pieces) * 2 * 512 * SPAN * ROWS
-    return whole(kernel, len(args), out, cost(flops, 2 << 20))(scalars, *args)
+        for k in range(4):
+            at = slice(128 * r, 128 * r + 128)
+            out_ref[s_ref[1] ^ k, :, at] = total[k * PAIR : (k + 1) * PAIR].astype(BF16)
+
+
+def scores(scalars, a, rows):
+    out = jax.ShapeDtypeStruct((4, PAIR, ROWS), BF16)
+    estimate = cost(2 * 512 * 2048 * ROWS, 4 << 20)
+    return whole(scores_kernel, 4 + len(rows), out, estimate)(scalars, *a, *rows)
 
 
 def attend_kernel(count_ref, s_ref, out_ref):
@@ -199,12 +224,12 @@
     return whole(kernel, 5, out, cost(2 * 512 * 1024 * ROWS, 2 << 20))(scalars, g, *a)
 
 
-def mix_kernel(s_ref, g_ref, e0, e1, e2, e3, *out_refs):
+def mix_kernel(s_ref, g_ref, *refs):
+    e_refs, out_refs = refs[:6], refs[6:]
     gs = jnp.concatenate([g_ref[s_ref[1] ^ k, :, 0:GROUP] for k in range(4)], axis=1)
     gs = gs.astype(F32).T.astype(BF16)
-    e_refs = (e0, e1, e2, e3)
     for p in range(4):
-        e = jnp.concatenate([half_rows(e_refs[p ^ r], r) for r in range(2)], axis=0)
+        e = jnp.concatenate([half_rows(e_refs, p ^ r, r) for r in range(2)], axis=0)
         part = nn(gs, e).astype(BF16)
         for k in range(4):
             out_refs[k][:, p * SPAN : (p + 1) * SPAN] = part[k * GROUP : (k + 1) * GROUP]
@@ -212,7 +237,7 @@
 
 def mix(scalars, g, rows):
     out = [jax.ShapeDtypeStruct((GROUP, COLUMN), BF16)] * 4
-    return whole(mix_kernel, 5, out, cost(2 * 256 * 256 * 2048, 2 << 20))(scalars, g, *rows)
+    return whole(mix_kernel, 1 + len(rows), out, cost(2 * 256 * 256 * 2048, 2 << 20))(scalars, g, *rows)
 
 
 def query_kernel(s_ref, x0, x1, x2, x3, w_ref, out_ref, acc_ref):
@@ -275,10 +300,14 @@
     wk = w_key.reshape(2, 4, 4, BLOCK, HEAD)
     wv = w_value.reshape(2, 4, 4, BLOCK, HEAD)
     own = spread(jnp.broadcast_to(encoded[:, None], E_SHAPE), ROW_GROUPS)
-    shared = to_members(project(scalars, queries[0], cotangent[0], wk, wv))
-    rows = [own] + [swap(own, QUAD, j) for j in range(1, 4)]
-    sums = scores(scalars, shared, (0, 1, 3), [rows[0], rows[1], rows[3]], None, False)
-    sums = scores(scalars, shared, (2,), [rows[2]], sums, True)
+    mine = (queries[0], cotangent[0], wk, wv)
+    others = [swap(part, "x", k) for k, part in enumerate(project(*mine), 1)]
+    third = [swap(own[8 * r : 8 * r + 8], QUAD, 3) for r in range(2)]
+    rows = [own, swap(own, QUAD, 1), *[swap(t, QUAD, 1) for t in third], *third]
+    mine, third = lax.optimization_barrier((mine, third))
+    shared = [project_own(scalars, *mine), *others]
+    rows = [*rows[:4], *third]
+    sums = scores(scalars, shared, rows)
     parts = lax.all_to_all(sums, "x", 0, 0, tiled=True)
     grads = lax.all_to_all(attend(counts.reshape(1), parts), "x", 0, 0, tiled=True)
     passed = swap(term(scalars, grads, shared, 1, BF16), QUAD, 1)

time: 148 us -> 144 us (0.973)
  waiting for transfers between devices: 54.7 us -> 39.3 us
  starting transfers between devices: 64.3 us -> 75.1 us
    ppermute x10 -> x12, waiting for transfers between devices: 37.3 us -> 20.4 us  [swap(): return lax.ppermute(array, axes, [(i, i ^ k) for i in range(4)])]
    ppermute x10 -> x12, starting transfers between devices: 30.5 us -> 40.9 us  [swap(): return lax.ppermute(array, axes, [(i, i ^ k) for i in range(4)])]
    all_to_all x2, waiting for transfers between devices: 12.3 us -> 14.1 us  [spread(): lax.all_to_all(blocks.reshape(-1, 16, BLOCK), SPREAD_AXES, 0, 0, axis_ind...]
  transfers between devices with their start and end apart: 13 -> 15, of which waited for: 9 -> 7; matrix products, arithmetic and copies ran while one was open for 0% -> 0% of each run, Pallas kernels for 7% -> 6%
where the time goes in v6:
time: 144 us; the launch traced here: 143 us
  starting transfers between devices  75.1 us (52%)
  waiting for transfers between devices  39.3 us (27%)
  Pallas kernels  13.5 us (9%)
  blocking collectives  7.92 us (6%)
  local copies, waits for them, and re-layouts  4.86 us (3%)
  between operations  1.56 us (1%)
    ppermute x12, starting transfers between devices, swap(): return lax.ppermute(array, axes, [(i, i ^ k) for i in range(4)])  40.9 us
    all_to_all x2, starting transfers between devices, spread(): lax.all_to_all(blocks.reshape(-1, 16, BLOCK), SPREAD_AXES, 0, 0, axis_ind...  30.2 us
    ppermute x12, waiting for transfers between devices, swap(): return lax.ppermute(array, axes, [(i, i ^ k) for i in range(4)])  20.4 us
    all_to_all x2, waiting for transfers between devices, spread(): lax.all_to_all(blocks.reshape(-1, 16, BLOCK), SPREAD_AXES, 0, 0, axis_ind...  14.1 us
    all_to_all x1, blocking collectives, local(): lax.all_to_all(attend(counts.reshape(1), parts), 'x', 0, 0, tiled=True)  7.92 us
    all_to_all x1, waiting for transfers between devices, local(): parts = lax.all_to_all(sums, 'x', 0, 0, tiled=True)  4.88 us
    all_to_all x1, starting transfers between devices, local(): parts = lax.all_to_all(sums, 'x', 0, 0, tiled=True)  4.01 us
    pallas_call x1, Pallas kernels, project(): pl.pallas_call(project_kernel, in_specs=[HBM] * 4, out_specs=[VMEM] * 3,...  3.84 us
  transfers between devices with their start and end apart: 15, of which 7 were waited for; matrix products, arithmetic and copies ran while one was open for 0% of the time, Pallas kernels for 6%

profile of v6, /device:TPU:1, one launch (start us, length us, event | category | flops | bytes accessed | tf_op | source)
XLA Modules:
  0.0 143.4 jit_solution(1795646551114479741)
XLA Ops:
  0.6 1.6 %broadcast_in_dim.4 = bf16[16,2,16,256]{3,2,1,0:T(8,128)(2,1)} broadcast(bf16[16,16,256]{2,1,0:T(8,128)(2,1)} %param.6), dimensions={0,2,3} | broadcast | bytes 393216 | tf_op jit(solution)/shard_map/broadcast_in_dim | solution.py:302
  2.3 18.9 %all-to-all-start = ((bf16[32,16,256]{2,1,0:T(8,128)(2,1)}), bf16[32,16,256]{2,1,0:T(8,128)(2,1)S(1)}, u32[]{:S(2)}, u32[]{:S(2)}) async-start(bf16[32,16,256]{2,1,0:T(8,128)(2,1)} %bitcast.7), calls=%async_computation | async-start | bytes 524288 | tf_op jit(solution)/shard_map/all_to_all | solution.py:36
  21.2 0.0 copy-start.3
  21.2 0.0 copy-start.4
  21.2 3.8 %shard_map.78 = (bf16[128,2048]{1,0:T(8,128)(2,1)}, bf16[128,2048]{1,0:T(8,128)(2,1)}, bf16[128,2048]{1,0:T(8,128)(2,1)}) custom-call(bf16[64,128]{1,0:T(8,128)(2,1)} %bitcast.24, bf16[64,128]{1,0:T(8,128)(2,1)} %bitcast.26, bf16[2,4,4,256,128]{4,3,2,1,0:T(8,128)(2,1)} %bitcast.15, bf16[2,4,4,256,128]{4,3,2,1,0:T(8,128)(2,1)} %bitcast.18), custom_call_target="tpu_custom_call" | custom-call | flops 201326592 | bytes 6291456 | tf_op jit(solution)/shard_map/pallas_call | solution.py:111
  25.1 3.1 %collective-permute-start.2 = (bf16[128,2048]{1,0:T(8,128)(2,1)}, bf16[128,2048]{1,0:T(8,128)(2,1)S(1)}, u32[]{:S(2)}, u32[]{:S(2)}) collective-permute-start(bf16[128,2048]{1,0:T(8,128)(2,1)} %get-tuple-element.24), channel_id=1, source_target_pairs={{0,1},{1,0},{2,3},{3,2},{4,5},{5,4},{6,7},{7,6},{8,9},{9,8},{10,11... | collective-permute-start | bytes 1572872 | tf_op jit(solution)/shard_map/ppermute | solution.py:43
  28.2 4.4 %collective-permute-start.3 = (bf16[128,2048]{1,0:T(8,128)(2,1)}, bf16[128,2048]{1,0:T(8,128)(2,1)S(1)}, u32[]{:S(2)}, u32[]{:S(2)}) collective-permute-start(bf16[128,2048]{1,0:T(8,128)(2,1)} %get-tuple-element.25), channel_id=1, source_target_pairs={{0,2},{1,3},{2,0},{3,1},{4,6},{5,7},{6,4},{7,5},{8,10},{9,11},{10,... | collective-permute-start | bytes 1572872 | tf_op jit(solution)/shard_map/ppermute | solution.py:43
  32.6 2.1 %collective-permute-start.4 = (bf16[128,2048]{1,0:T(8,128)(2,1)}, bf16[128,2048]{1,0:T(8,128)(2,1)S(1)}, u32[]{:S(2)}, u32[]{:S(2)}) collective-permute-start(bf16[128,2048]{1,0:T(8,128)(2,1)} %get-tuple-element.26), channel_id=1, source_target_pairs={{0,3},{1,2},{2,1},{3,0},{4,7},{5,6},{6,5},{7,4},{8,11},{9,10},{10,... | collective-permute-start | bytes 1572872 | tf_op jit(solution)/shard_map/ppermute | solution.py:43
  34.7 6.7 %all-to-all-done = bf16[32,16,256]{2,1,0:T(8,128)(2,1)S(1)} async-done(((bf16[32,16,256]{2,1,0:T(8,128)(2,1)}), bf16[32,16,256]{2,1,0:T(8,128)(2,1)S(1)}, u32[]{:S(2)}, u32[]{:S(2)}) %all-to-all-start) | async-done | bytes 262176 | tf_op jit(solution)/shard_map/all_to_all | solution.py:36
  41.4 4.6 %collective-permute-start = (bf16[8,2,16,256]{3,2,1,0:T(8,128)(2,1)S(1)}, bf16[8,2,16,256]{3,2,1,0:T(8,128)(2,1)S(1)}, u32[]{:S(2)}, u32[]{:S(2)}) collective-permute-start(bf16[8,2,16,256]{3,2,1,0:T(8,128)(2,1)S(1)} %bitcast.29), channel_id=1, source_target_pairs={{0,12},{4,8},{8,4},{12,0},{1,13},{5,9},{9,5},{13,1},{2,14},{6,10},... | collective-permute-start | bytes 393224 | tf_op jit(solution)/shard_map/ppermute | solution.py:43
  46.0 2.5 %collective-permute-start.1 = (bf16[8,2,16,256]{3,2,1,0:T(8,128)(2,1)S(1)}, bf16[8,2,16,256]{3,2,1,0:T(8,128)(2,1)S(1)}, u32[]{:S(2)}, u32[]{:S(2)}) collective-permute-start(bf16[8,2,16,256]{3,2,1,0:T(8,128)(2,1)S(1)} %bitcast.28), channel_id=1, source_target_pairs={{0,12},{4,8},{8,4},{12,0},{1,13},{5,9},{9,5},{13,1},{2,14},{6,10},... | collective-permute-start | bytes 393224 | tf_op jit(solution)/shard_map/ppermute | solution.py:43
  48.5 0.0 collective-permute-done.2.a1
  48.5 2.7 %collective-permute-start.5 = (bf16[16,2,16,256]{3,2,1,0:T(8,128)(2,1)S(1)}, bf16[16,2,16,256]{3,2,1,0:T(8,128)(2,1)S(1)}, u32[]{:S(2)}, u32[]{:S(2)}) collective-permute-start(bf16[16,2,16,256]{3,2,1,0:T(8,128)(2,1)S(1)} %bitcast.20), channel_id=1, source_target_pairs={{0,4},{4,0},{8,12},{12,8},{1,5},{5,1},{9,13},{13,9},{2,6},{6,2},{1... | collective-permute-start | bytes 786440 | tf_op jit(solution)/shard_map/ppermute | solution.py:43
  51.1 0.0 collective-permute-done.refs_4_
  51.2 7.0 %collective-permute-start.6 = (bf16[8,2,16,256]{3,2,1,0:T(8,128)(2,1)S(1)}, bf16[8,2,16,256]{3,2,1,0:T(8,128)(2,1)S(1)}, u32[]{:S(2)}, u32[]{:S(2)}) collective-permute-start(bf16[8,2,16,256]{3,2,1,0:T(8,128)(2,1)S(1)} %collective-permute-done.refs_4_), channel_id=1, source_target_pairs={{0,4},{4,0},{8,12},{12,8},{1,5},{5,1},{9,13},{13,9},{2,6},{6,2},{1... | collective-permute-start | bytes 393224 | tf_op jit(solution)/shard_map/ppermute | solution.py:43
  58.2 0.0 collective-permute-done.1.refs_5_
  58.2 2.9 %collective-permute-start.7 = (bf16[8,2,16,256]{3,2,1,0:T(8,128)(2,1)S(1)}, bf16[8,2,16,256]{3,2,1,0:T(8,128)(2,1)S(1)}, u32[]{:S(2)}, u32[]{:S(2)}) collective-permute-start(bf16[8,2,16,256]{3,2,1,0:T(8,128)(2,1)S(1)} %collective-permute-done.1.refs_5_), channel_id=1, source_target_pairs={{0,4},{4,0},{8,12},{12,8},{1,5},{5,1},{9,13},{13,9},{2,6},{6,2},{1... | collective-permute-start | bytes 393224 | tf_op jit(solution)/shard_map/ppermute | solution.py:43
  61.1 0.1 pad_add_fusion.s_ref
  61.2 0.0 copy-done.3
  61.2 0.0 copy-done.4
  61.2 0.0 copy-start
  61.2 1.6 %copy-done = bf16[1,8192,128]{2,1,0:T(8,128)(2,1)S(1)} copy-done((bf16[1,8192,128]{2,1,0:T(8,128)(2,1)S(1)}, bf16[1,8192,128]{2,1,0:T(8,128)(2,1)}, u32[]{:S(2)}) %copy-start) | copy-done | bytes 2097176
  62.8 0.0 copy-start.2
  62.8 1.6 %copy-done.2 = bf16[1,8192,128]{2,1,0:T(8,128)(2,1)S(1)} copy-done((bf16[1,8192,128]{2,1,0:T(8,128)(2,1)S(1)}, bf16[1,8192,128]{2,1,0:T(8,128)(2,1)}, u32[]{:S(2)}) %copy-start.2) | copy-done | bytes 2097176
  64.4 1.2 shard_map.77.a0
  65.6 0.0 collective-permute-done.3.a2
  65.6 0.0 collective-permute-done.4.a3
  65.6 0.0 collective-permute-done.6.refs_2_
  65.6 0.3 collective-permute-done.7.refs_3_
  66.0 0.0 collective-permute-done.5.refs_1_
  66.0 2.5 %shard_map.79 = bf16[4,128,256]{2,1,0:T(8,128)(2,1)} custom-call(s32[2]{0:T(128)S(1)} %pad_add_fusion.s_ref, bf16[128,2048]{1,0:T(8,128)(2,1)S(1)} %shard_map.77.a0, bf16[128,2048]{1,0:T(8,128)(2,1)S(1)} %collective-permute-done.2.a1, bf16[128,2048]{1,0:T(8,128)(2,1)S(1)} %collective-permute-done.3.a2, bf16[128,2048]{1,0:T(8,128)(2,1)S(1)} %collective-permute-done.4.a3, ...), custom_call_target="tpu_custom_call" | custom-call | flops 536870912 | bytes 4194304 | tf_op jit(solution)/shard_map/pallas_call | solution.py:184
  68.5 4.0 %all-to-all-start.1 = ((bf16[4,128,256]{2,1,0:T(8,128)(2,1)}), bf16[4,128,256]{2,1,0:T(8,128)(2,1)S(1)}, u32[]{:S(2)}, u32[]{:S(2)}) async-start(bf16[4,128,256]{2,1,0:T(8,128)(2,1)} %shard_map.79), calls=%async_computation.1 | async-start | bytes 524288 | tf_op jit(solution)/shard_map/all_to_all | solution.py:311
  73.1 4.9 %all-to-all-done.1.s_ref = bf16[4,128,256]{2,1,0:T(8,128)(2,1)S(1)} async-done(((bf16[4,128,256]{2,1,0:T(8,128)(2,1)}), bf16[4,128,256]{2,1,0:T(8,128)(2,1)S(1)}, u32[]{:S(2)}, u32[]{:S(2)}) %all-to-all-start.1) | async-done | bytes 262176 | tf_op jit(solution)/shard_map/all_to_all | solution.py:311
  78.0 0.3 shard_map.80
  78.3 7.9 %all_to_all.20.g_ref = bf16[4,256,128]{2,1,0:T(8,128)(2,1)S(1)} all-to-all(bf16[4,256,128]{2,1,0:T(8,128)(2,1)S(1)} %shard_map.80), channel_id=1, replica_groups=mesh['zh'=2,'y'=4,'c'=2,'za'=2,'zb'=2,'z2'=2,'x'=4] {'x'}, dimensions={0} | all-to-all | bytes 524288 | tf_op jit(solution)/shard_map/all_to_all | solution.py:312
  86.2 1.0 shard_map.84
  87.2 2.1 %collective-permute-start.11 = (bf16[16,4,16,256]{3,2,1,0:T(8,128)(2,1)S(1)}, bf16[16,4,16,256]{3,2,1,0:T(8,128)(2,1)S(1)}, u32[]{:S(2)}, u32[]{:S(2)}) collective-permute-start(bf16[16,4,16,256]{3,2,1,0:T(8,128)(2,1)S(1)} %shard_map.84), channel_id=1, source_target_pairs={{0,4},{4,0},{8,12},{12,8},{1,5},{5,1},{9,13},{13,9},{2,6},{6,2},{1... | collective-permute-start | bytes 1572872 | tf_op jit(solution)/shard_map/ppermute | solution.py:43
  89.3 1.1 shard_map.82
  90.4 0.0 copy-start.5
  90.4 0.0 copy-start.6
  90.4 0.0 copy-start.7
  90.4 1.0 shard_map.81
  91.5 0.0 copy-start.1
  91.5 7.5 %collective-permute-done.11 = bf16[16,4,16,256]{3,2,1,0:T(8,128)(2,1)S(1)} collective-permute-done((bf16[16,4,16,256]{3,2,1,0:T(8,128)(2,1)S(1)}, bf16[16,4,16,256]{3,2,1,0:T(8,128)(2,1)S(1)}, u32[]{:S(2)}, u32[]{:S(2)}) %collective-permute-start.11) | collective-permute-done | bytes 524320 | tf_op jit(solution)/shard_map/ppermute | solution.py:43
  99.0 1.0 add_convert_fusion
  100.0 0.0 copy-done.5
  100.0 0.0 copy-done.6
  100.0 0.0 copy-done.7
  100.0 11.3 %all-to-all-start.3 = ((bf16[64,16,256]{2,1,0:T(8,128)(2,1)}), bf16[64,16,256]{2,1,0:T(8,128)(2,1)S(1)}, u32[]{:S(2)}, u32[]{:S(2)}) async-start(bf16[64,16,256]{2,1,0:T(8,128)(2,1)} %bitcast.12), calls=%async_computation.3 | async-start | bytes 1048576 | tf_op jit(solution)/shard_map/all_to_all | solution.py:36
  111.3 2.2 %collective-permute-start.8 = (bf16[64,2048]{1,0:T(8,128)(2,1)}, bf16[64,2048]{1,0:T(8,128)(2,1)S(1)}, u32[]{:S(2)}, u32[]{:S(2)}) collective-permute-start(bf16[64,2048]{1,0:T(8,128)(2,1)} %copy-done.7), channel_id=1, source_target_pairs={{0,1},{1,0},{2,3},{3,2},{4,5},{5,4},{6,7},{7,6},{8,9},{9,8},{10,11... | collective-permute-start | bytes 786440 | tf_op jit(solution)/shard_map/ppermute | solution.py:43
  113.5 3.7 %collective-permute-start.9 = (bf16[64,2048]{1,0:T(8,128)(2,1)}, bf16[64,2048]{1,0:T(8,128)(2,1)S(1)}, u32[]{:S(2)}, u32[]{:S(2)}) collective-permute-start(bf16[64,2048]{1,0:T(8,128)(2,1)} %copy-done.6), channel_id=1, source_target_pairs={{0,2},{1,3},{2,0},{3,1},{4,6},{5,7},{6,4},{7,5},{8,10},{9,11},{10,... | collective-permute-start | bytes 786440 | tf_op jit(solution)/shard_map/ppermute | solution.py:43
  117.2 3.7 %collective-permute-start.10 = (bf16[64,2048]{1,0:T(8,128)(2,1)}, bf16[64,2048]{1,0:T(8,128)(2,1)S(1)}, u32[]{:S(2)}, u32[]{:S(2)}) collective-permute-start(bf16[64,2048]{1,0:T(8,128)(2,1)} %copy-done.5), channel_id=1, source_target_pairs={{0,3},{1,2},{2,1},{3,0},{4,7},{5,6},{6,5},{7,4},{8,11},{9,10},{10,... | collective-permute-start | bytes 786440 | tf_op jit(solution)/shard_map/ppermute | solution.py:43
  120.9 0.0 collective-permute-done.8.x1
  120.9 6.2 %collective-permute-done.9.x2 = bf16[64,2048]{1,0:T(8,128)(2,1)S(1)} collective-permute-done((bf16[64,2048]{1,0:T(8,128)(2,1)}, bf16[64,2048]{1,0:T(8,128)(2,1)S(1)}, u32[]{:S(2)}, u32[]{:S(2)}) %collective-permute-start.9) | collective-permute-done | bytes 262176 | tf_op jit(solution)/shard_map/ppermute | solution.py:43
  127.1 6.4 %collective-permute-done.10.x3 = bf16[64,2048]{1,0:T(8,128)(2,1)S(1)} collective-permute-done((bf16[64,2048]{1,0:T(8,128)(2,1)}, bf16[64,2048]{1,0:T(8,128)(2,1)S(1)}, u32[]{:S(2)}, u32[]{:S(2)}) %collective-permute-start.10) | collective-permute-done | bytes 262176 | tf_op jit(solution)/shard_map/ppermute | solution.py:43
  133.4 0.0 copy-done.1
  133.4 1.8 %shard_map.83 = bf16[64,128]{1,0:T(8,128)(2,1)} custom-call(s32[2]{0:T(128)S(1)} %pad_add_fusion.s_ref, bf16[64,2048]{1,0:T(8,128)(2,1)S(1)} %get-tuple-element.33.x0, bf16[64,2048]{1,0:T(8,128)(2,1)S(1)} %collective-permute-done.8.x1, bf16[64,2048]{1,0:T(8,128)(2,1)S(1)} %collective-permute-done.9.x2, bf16[64,2048]{1,0:T(8,128)(2,1)S(1)} %collective-permute-done.10.x3, ...), custom_call_target="tpu_custom_call" | custom-call | flops 134217728 | bytes 3145728 | tf_op jit(solution)/shard_map/pallas_call | solution.py:263
  135.2 7.4 %all-to-all-done.3 = bf16[64,16,256]{2,1,0:T(8,128)(2,1)S(1)} async-done(((bf16[64,16,256]{2,1,0:T(8,128)(2,1)}), bf16[64,16,256]{2,1,0:T(8,128)(2,1)S(1)}, u32[]{:S(2)}, u32[]{:S(2)}) %all-to-all-start.3) | async-done | bytes 524320 | tf_op jit(solution)/shard_map/all_to_all | solution.py:36
  142.6 0.8 shard_map.85
  (1 shorter events, 0.0 us)
Async XLA Ops:
  2.3 39.1 %all-to-all-start = ((bf16[32,16,256]{2,1,0:T(8,128)(2,1)}), bf16[32,16,256]{2,1,0:T(8,128)(2,1)S(1)}, u32[]{:S(2)}, u32[]{:S(2)}) async-start(bf16[32,16,256]{2,1,0:T(8,128)(2,1)} %bitcast.7), calls=%async_computation | async-start | bytes 524288 | tf_op jit(solution)/shard_map/all_to_all | solution.py:36
  21.2 40.0 %copy-start.3 = (bf16[1,64,128]{2,1,0:T(8,128)(2,1)S(1)}, bf16[1,64,128]{2,1,0:T(8,128)(2,1)}, u32[]{:S(2)}) copy-start(bf16[1,64,128]{2,1,0:T(8,128)(2,1)} %param.9) | copy-start | bytes 49156
  21.2 40.0 %copy-start.4 = (bf16[1,64,128]{2,1,0:T(8,128)(2,1)S(1)}, bf16[1,64,128]{2,1,0:T(8,128)(2,1)}, u32[]{:S(2)}) copy-start(bf16[1,64,128]{2,1,0:T(8,128)(2,1)} %param.10) | copy-start | bytes 49156
  25.1 23.4 %collective-permute-start.2 = (bf16[128,2048]{1,0:T(8,128)(2,1)}, bf16[128,2048]{1,0:T(8,128)(2,1)S(1)}, u32[]{:S(2)}, u32[]{:S(2)}) collective-permute-start(bf16[128,2048]{1,0:T(8,128)(2,1)} %get-tuple-element.24), channel_id=1, source_target_pairs={{0,1},{1,0},{2,3},{3,2},{4,5},{5,4},{6,7},{7,6},{8,9},{9,8},{10,11... | collective-permute-start | bytes 1572872 | tf_op jit(solution)/shard_map/ppermute | solution.py:43
  28.2 37.4 %collective-permute-start.3 = (bf16[128,2048]{1,0:T(8,128)(2,1)}, bf16[128,2048]{1,0:T(8,128)(2,1)S(1)}, u32[]{:S(2)}, u32[]{:S(2)}) collective-permute-start(bf16[128,2048]{1,0:T(8,128)(2,1)} %get-tuple-element.25), channel_id=1, source_target_pairs={{0,2},{1,3},{2,0},{3,1},{4,6},{5,7},{6,4},{7,5},{8,10},{9,11},{10,... | collective-permute-start | bytes 1572872 | tf_op jit(solution)/shard_map/ppermute | solution.py:43
  32.6 33.1 %collective-permute-start.4 = (bf16[128,2048]{1,0:T(8,128)(2,1)}, bf16[128,2048]{1,0:T(8,128)(2,1)S(1)}, u32[]{:S(2)}, u32[]{:S(2)}) collective-permute-start(bf16[128,2048]{1,0:T(8,128)(2,1)} %get-tuple-element.26), channel_id=1, source_target_pairs={{0,3},{1,2},{2,1},{3,0},{4,7},{5,6},{6,5},{7,4},{8,11},{9,10},{10,... | collective-permute-start | bytes 1572872 | tf_op jit(solution)/shard_map/ppermute | solution.py:43
  41.4 9.8 %collective-permute-start = (bf16[8,2,16,256]{3,2,1,0:T(8,128)(2,1)S(1)}, bf16[8,2,16,256]{3,2,1,0:T(8,128)(2,1)S(1)}, u32[]{:S(2)}, u32[]{:S(2)}) collective-permute-start(bf16[8,2,16,256]{3,2,1,0:T(8,128)(2,1)S(1)} %bitcast.29), channel_id=1, source_target_pairs={{0,12},{4,8},{8,4},{12,0},{1,13},{5,9},{9,5},{13,1},{2,14},{6,10},... | collective-permute-start | bytes 393224 | tf_op jit(solution)/shard_map/ppermute | solution.py:43
  46.0 12.2 %collective-permute-start.1 = (bf16[8,2,16,256]{3,2,1,0:T(8,128)(2,1)S(1)}, bf16[8,2,16,256]{3,2,1,0:T(8,128)(2,1)S(1)}, u32[]{:S(2)}, u32[]{:S(2)}) collective-permute-start(bf16[8,2,16,256]{3,2,1,0:T(8,128)(2,1)S(1)} %bitcast.28), channel_id=1, source_target_pairs={{0,12},{4,8},{8,4},{12,0},{1,13},{5,9},{9,5},{13,1},{2,14},{6,10},... | collective-permute-start | bytes 393224 | tf_op jit(solution)/shard_map/ppermute | solution.py:43
  48.5 17.5 %collective-permute-start.5 = (bf16[16,2,16,256]{3,2,1,0:T(8,128)(2,1)S(1)}, bf16[16,2,16,256]{3,2,1,0:T(8,128)(2,1)S(1)}, u32[]{:S(2)}, u32[]{:S(2)}) collective-permute-start(bf16[16,2,16,256]{3,2,1,0:T(8,128)(2,1)S(1)} %bitcast.20), channel_id=1, source_target_pairs={{0,4},{4,0},{8,12},{12,8},{1,5},{5,1},{9,13},{13,9},{2,6},{6,2},{1... | collective-permute-start | bytes 786440 | tf_op jit(solution)/shard_map/ppermute | solution.py:43
  51.2 14.5 %collective-permute-start.6 = (bf16[8,2,16,256]{3,2,1,0:T(8,128)(2,1)S(1)}, bf16[8,2,16,256]{3,2,1,0:T(8,128)(2,1)S(1)}, u32[]{:S(2)}, u32[]{:S(2)}) collective-permute-start(bf16[8,2,16,256]{3,2,1,0:T(8,128)(2,1)S(1)} %collective-permute-done.refs_4_), channel_id=1, source_target_pairs={{0,4},{4,0},{8,12},{12,8},{1,5},{5,1},{9,13},{13,9},{2,6},{6,2},{1... | collective-permute-start | bytes 393224 | tf_op jit(solution)/shard_map/ppermute | solution.py:43
  58.2 7.8 %collective-permute-start.7 = (bf16[8,2,16,256]{3,2,1,0:T(8,128)(2,1)S(1)}, bf16[8,2,16,256]{3,2,1,0:T(8,128)(2,1)S(1)}, u32[]{:S(2)}, u32[]{:S(2)}) collective-permute-start(bf16[8,2,16,256]{3,2,1,0:T(8,128)(2,1)S(1)} %collective-permute-done.1.refs_5_), channel_id=1, source_target_pairs={{0,4},{4,0},{8,12},{12,8},{1,5},{5,1},{9,13},{13,9},{2,6},{6,2},{1... | collective-permute-start | bytes 393224 | tf_op jit(solution)/shard_map/ppermute | solution.py:43
  61.2 1.6 %copy-start = (bf16[1,8192,128]{2,1,0:T(8,128)(2,1)S(1)}, bf16[1,8192,128]{2,1,0:T(8,128)(2,1)}, u32[]{:S(2)}) copy-start(bf16[1,8192,128]{2,1,0:T(8,128)(2,1)} %param.7) | copy-start | bytes 6291460
  62.8 1.6 %copy-start.2 = (bf16[1,8192,128]{2,1,0:T(8,128)(2,1)S(1)}, bf16[1,8192,128]{2,1,0:T(8,128)(2,1)}, u32[]{:S(2)}) copy-start(bf16[1,8192,128]{2,1,0:T(8,128)(2,1)} %param.8) | copy-start | bytes 6291460
  68.5 9.5 %all-to-all-start.1 = ((bf16[4,128,256]{2,1,0:T(8,128)(2,1)}), bf16[4,128,256]{2,1,0:T(8,128)(2,1)S(1)}, u32[]{:S(2)}, u32[]{:S(2)}) async-start(bf16[4,128,256]{2,1,0:T(8,128)(2,1)} %shard_map.79), calls=%async_computation.1 | async-start | bytes 524288 | tf_op jit(solution)/shard_map/all_to_all | solution.py:311
  87.2 11.8 %collective-permute-start.11 = (bf16[16,4,16,256]{3,2,1,0:T(8,128)(2,1)S(1)}, bf16[16,4,16,256]{3,2,1,0:T(8,128)(2,1)S(1)}, u32[]{:S(2)}, u32[]{:S(2)}) collective-permute-start(bf16[16,4,16,256]{3,2,1,0:T(8,128)(2,1)S(1)} %shard_map.84), channel_id=1, source_target_pairs={{0,4},{4,0},{8,12},{12,8},{1,5},{5,1},{9,13},{13,9},{2,6},{6,2},{1... | collective-permute-start | bytes 1572872 | tf_op jit(solution)/shard_map/ppermute | solution.py:43
  90.4 9.6 %copy-start.5 = (bf16[64,2048]{1,0:T(8,128)(2,1)}, bf16[64,2048]{1,0:T(8,128)(2,1)S(1)}, u32[]{:S(2)}) copy-start(bf16[64,2048]{1,0:T(8,128)(2,1)S(1)} %get-tuple-element.36) | copy-start | bytes 786436
  90.4 9.6 %copy-start.6 = (bf16[64,2048]{1,0:T(8,128)(2,1)}, bf16[64,2048]{1,0:T(8,128)(2,1)S(1)}, u32[]{:S(2)}) copy-start(bf16[64,2048]{1,0:T(8,128)(2,1)S(1)} %get-tuple-element.35) | copy-start | bytes 786436
  90.4 9.5 %copy-start.7 = (bf16[64,2048]{1,0:T(8,128)(2,1)}, bf16[64,2048]{1,0:T(8,128)(2,1)S(1)}, u32[]{:S(2)}) copy-start(bf16[64,2048]{1,0:T(8,128)(2,1)S(1)} %get-tuple-element.34) | copy-start | bytes 786436
  91.5 42.0 %copy-start.1 = (bf16[1,8192,128]{2,1,0:T(8,128)(2,1)S(1)}, bf16[1,8192,128]{2,1,0:T(8,128)(2,1)}, u32[]{:S(2)}) copy-start(bf16[1,8192,128]{2,1,0:T(8,128)(2,1)} %param.7) | copy-start | bytes 6291460
  100.0 42.7 %all-to-all-start.3 = ((bf16[64,16,256]{2,1,0:T(8,128)(2,1)}), bf16[64,16,256]{2,1,0:T(8,128)(2,1)S(1)}, u32[]{:S(2)}, u32[]{:S(2)}) async-start(bf16[64,16,256]{2,1,0:T(8,128)(2,1)} %bitcast.12), calls=%async_computation.3 | async-start | bytes 1048576 | tf_op jit(solution)/shard_map/all_to_all | solution.py:36
  111.3 9.6 %collective-permute-start.8 = (bf16[64,2048]{1,0:T(8,128)(2,1)}, bf16[64,2048]{1,0:T(8,128)(2,1)S(1)}, u32[]{:S(2)}, u32[]{:S(2)}) collective-permute-start(bf16[64,2048]{1,0:T(8,128)(2,1)} %copy-done.7), channel_id=1, source_target_pairs={{0,1},{1,0},{2,3},{3,2},{4,5},{5,4},{6,7},{7,6},{8,9},{9,8},{10,11... | collective-permute-start | bytes 786440 | tf_op jit(solution)/shard_map/ppermute | solution.py:43
  113.5 13.6 %collective-permute-start.9 = (bf16[64,2048]{1,0:T(8,128)(2,1)}, bf16[64,2048]{1,0:T(8,128)(2,1)S(1)}, u32[]{:S(2)}, u32[]{:S(2)}) collective-permute-start(bf16[64,2048]{1,0:T(8,128)(2,1)} %copy-done.6), channel_id=1, source_target_pairs={{0,2},{1,3},{2,0},{3,1},{4,6},{5,7},{6,4},{7,5},{8,10},{9,11},{10,... | collective-permute-start | bytes 786440 | tf_op jit(solution)/shard_map/ppermute | solution.py:43
  117.2 16.3 %collective-permute-start.10 = (bf16[64,2048]{1,0:T(8,128)(2,1)}, bf16[64,2048]{1,0:T(8,128)(2,1)S(1)}, u32[]{:S(2)}, u32[]{:S(2)}) collective-permute-start(bf16[64,2048]{1,0:T(8,128)(2,1)} %copy-done.5), channel_id=1, source_target_pairs={{0,3},{1,2},{2,1},{3,0},{4,7},{5,6},{6,5},{7,4},{8,11},{9,10},{10,... | collective-permute-start | bytes 786440 | tf_op jit(solution)/shard_map/ppermute | solution.py:43

commit v7 on v6

--- a/solution.py
+++ b/solution.py
@@ -27,9 +27,7 @@
 
 SPREAD_AXES = ("zh", "y", "c", "za", "zb", "z2")
 ROW_GROUPS = [[4 * i + (w ^ (i // 16)) for i in range(32)] for w in range(4)]
-TERM_GROUPS = [[2 * i + (w ^ (i // 32)) for i in range(64)] for w in range(2)]
 E_SHAPE = (16, 2, 16, BLOCK)
-T_SHAPE = (16, 4, 16, BLOCK)
 
 
 def spread(blocks, groups):
@@ -207,21 +205,21 @@
     return whole(attend_kernel, 1, out, cost(1 << 20, 1 << 19))(counts, s)
 
 
-def term_kernel(p2, s_ref, g_ref, a0, a1, a2, a3, out_ref):
+def term_kernel(pieces, s_ref, g_ref, a0, a1, a2, a3, *out_refs):
     g = jnp.concatenate([g_ref[s_ref[1] ^ k] for k in range(4)], axis=1)
-    for r in range(2):
-        for pb in range(2):
-            part = nn(g[128 * r : 128 * r + 128], heads((a0, a1, a2, a3), 2 * pb + (p2 ^ r)))
+    for j, out_ref in zip(pieces, out_refs, strict=True):
+        for r in range(2):
+            part = nn(g[128 * r : 128 * r + 128], heads((a0, a1, a2, a3), j ^ r))
             for b in range(2):
                 side = part[:, b * BLOCK : (b + 1) * BLOCK].astype(out_ref.dtype)
-                zb = (s_ref[0] // 2) ^ pb
-                out_ref[8 * r : 8 * r + 8, 2 * b + zb] = side.reshape(8, 16, BLOCK)
-
-
-def term(scalars, g, a, p2, kind):
-    out = jax.ShapeDtypeStruct(T_SHAPE, kind)
-    kernel = functools.partial(term_kernel, p2)
-    return whole(kernel, 5, out, cost(2 * 512 * 1024 * ROWS, 2 << 20))(scalars, g, *a)
+                out_ref[8 * r : 8 * r + 8, b] = side.reshape(8, 16, BLOCK)
+
+
+def term(scalars, g, a, pieces, kind):
+    out = [jax.ShapeDtypeStruct(E_SHAPE, kind)] * len(pieces)
+    kernel = functools.partial(term_kernel, pieces)
+    flops = len(pieces) * 2 * 512 * SPAN * ROWS
+    return whole(kernel, 5, out, cost(flops, 2 << 20))(scalars, g, *a)
 
 
 def mix_kernel(s_ref, g_ref, *refs):
@@ -278,7 +276,7 @@
 
 def total_kernel(t_ref, out_ref):
     total = t_ref[:, 0].astype(F32)
-    for b in range(1, 4):
+    for b in range(1, 2):
         total = total + t_ref[:, b].astype(F32)
     out_ref[...] = total
 
@@ -304,18 +302,22 @@
     others = [swap(part, "x", k) for k, part in enumerate(project(*mine), 1)]
     third = [swap(own[8 * r : 8 * r + 8], QUAD, 3) for r in range(2)]
     rows = [own, swap(own, QUAD, 1), *[swap(t, QUAD, 1) for t in third], *third]
-    mine, third = lax.optimization_barrier((mine, third))
+    mine, own = lax.optimization_barrier((mine, own))
     shared = [project_own(scalars, *mine), *others]
-    rows = [*rows[:4], *third]
+    rows = [own, *rows[1:]]
     sums = scores(scalars, shared, rows)
     parts = lax.all_to_all(sums, "x", 0, 0, tiled=True)
     grads = lax.all_to_all(attend(counts.reshape(1), parts), "x", 0, 0, tiled=True)
-    passed = swap(term(scalars, grads, shared, 1, BF16), QUAD, 1)
-    kept = term(scalars, grads, shared, 0, F32)
+    far, near, third = term(scalars, grads, shared, (2, 1, 3), BF16)
+    far, near = swap(far, QUAD, 1), swap(near, QUAD, 1)
     mixture = mix(scalars, grads, rows)
-    kept, mixture = lax.optimization_barrier((kept, mixture))
-    terms = spread((kept + passed.astype(F32)).astype(BF16), TERM_GROUPS)
+    far, mixture = lax.optimization_barrier((far, mixture))
+    third = swap((third.astype(F32) + far.astype(F32)).astype(BF16), QUAD, 3)
+    kept = term(scalars, grads, shared, (0,), F32)[0]
+    sent = (kept + near.astype(F32) + third.astype(F32)).astype(BF16)
     mixed = to_members(mixture)
+    sent, mixed[3] = lax.optimization_barrier((sent, mixed[3]))
+    terms = spread(sent, ROW_GROUPS)
     grad_queries = query(scalars, mixed, wk)
     grad_encoded = total_terms(terms)
     return grad_queries[None], grad_encoded

time: 144 us -> 144 us (level)
  the two profiles are of different devices: /device:TPU:1 before, /device:TPU:33 now
where the time goes in v7:
time: 144 us; the launch traced here: 143 us
  starting transfers between devices  75.4 us (52%)
  waiting for transfers between devices  37.4 us (26%)
  Pallas kernels  13.5 us (9%)
  blocking collectives  7.92 us (6%)
  local copies, waits for them, and re-layouts  5.83 us (4%)
  between operations  1.64 us (1%)
    ppermute x14, starting transfers between devices, swap(): return lax.ppermute(array, axes, [(i, i ^ k) for i in range(4)])  38.7 us
    all_to_all x2, starting transfers between devices, spread(): lax.all_to_all(blocks.reshape(-1, 16, BLOCK), SPREAD_AXES, 0, 0, axis_ind...  32.7 us
    ppermute x14, waiting for transfers between devices, swap(): return lax.ppermute(array, axes, [(i, i ^ k) for i in range(4)])  20 us
    all_to_all x2, waiting for transfers between devices, spread(): lax.all_to_all(blocks.reshape(-1, 16, BLOCK), SPREAD_AXES, 0, 0, axis_ind...  12.5 us
    all_to_all x1, blocking collectives, local(): lax.all_to_all(attend(counts.reshape(1), parts), 'x', 0, 0, tiled=True)  7.92 us
    all_to_all x1, waiting for transfers between devices, local(): parts = lax.all_to_all(sums, 'x', 0, 0, tiled=True)  4.88 us
    unnamed x26, local copies, waits for them, and re-layouts  4.18 us
    all_to_all x1, starting transfers between devices, local(): parts = lax.all_to_all(sums, 'x', 0, 0, tiled=True)  4.01 us
  transfers between devices with their start and end apart: 17, of which 10 were waited for; matrix products, arithmetic and copies ran while one was open for 1% of the time, Pallas kernels for 6%

profile of v7, /device:TPU:33, one launch (start us, length us, event | category | flops | bytes accessed | tf_op | source)
XLA Modules:
  0.0 142.7 jit_solution(13713377381979703541)
XLA Ops:
  0.6 1.6 %broadcast_in_dim.4 = bf16[16,2,16,256]{3,2,1,0:T(8,128)(2,1)} broadcast(bf16[16,16,256]{2,1,0:T(8,128)(2,1)} %param.6), dimensions={0,2,3} | broadcast | bytes 393216 | tf_op jit(solution)/shard_map/broadcast_in_dim | solution.py:300
  2.3 17.2 %all-to-all-start = ((bf16[32,16,256]{2,1,0:T(8,128)(2,1)}), bf16[32,16,256]{2,1,0:T(8,128)(2,1)S(1)}, u32[]{:S(2)}, u32[]{:S(2)}) async-start(bf16[32,16,256]{2,1,0:T(8,128)(2,1)} %bitcast.7), calls=%async_computation | async-start | bytes 524288 | tf_op jit(solution)/shard_map/all_to_all | solution.py:34
  19.5 0.0 copy-start.9
  19.5 0.0 copy-start.10
  19.5 3.8 %shard_map.78 = (bf16[128,2048]{1,0:T(8,128)(2,1)}, bf16[128,2048]{1,0:T(8,128)(2,1)}, bf16[128,2048]{1,0:T(8,128)(2,1)}) custom-call(bf16[64,128]{1,0:T(8,128)(2,1)} %bitcast.24, bf16[64,128]{1,0:T(8,128)(2,1)} %bitcast.26, bf16[2,4,4,256,128]{4,3,2,1,0:T(8,128)(2,1)} %bitcast.15, bf16[2,4,4,256,128]{4,3,2,1,0:T(8,128)(2,1)} %bitcast.18), custom_call_target="tpu_custom_call" | custom-call | flops 201326592 | bytes 6291456 | tf_op jit(solution)/shard_map/pallas_call | solution.py:109
  23.3 3.1 %collective-permute-start = (bf16[128,2048]{1,0:T(8,128)(2,1)}, bf16[128,2048]{1,0:T(8,128)(2,1)S(1)}, u32[]{:S(2)}, u32[]{:S(2)}) collective-permute-start(bf16[128,2048]{1,0:T(8,128)(2,1)} %get-tuple-element.28), channel_id=1, source_target_pairs={{0,1},{1,0},{2,3},{3,2},{4,5},{5,4},{6,7},{7,6},{8,9},{9,8},{10,11... | collective-permute-start | bytes 1572872 | tf_op jit(solution)/shard_map/ppermute | solution.py:41
  26.4 4.4 %collective-permute-start.1 = (bf16[128,2048]{1,0:T(8,128)(2,1)}, bf16[128,2048]{1,0:T(8,128)(2,1)S(1)}, u32[]{:S(2)}, u32[]{:S(2)}) collective-permute-start(bf16[128,2048]{1,0:T(8,128)(2,1)} %get-tuple-element.29), channel_id=1, source_target_pairs={{0,2},{1,3},{2,0},{3,1},{4,6},{5,7},{6,4},{7,5},{8,10},{9,11},{10,... | collective-permute-start | bytes 1572872 | tf_op jit(solution)/shard_map/ppermute | solution.py:41
  30.8 2.1 %collective-permute-start.2 = (bf16[128,2048]{1,0:T(8,128)(2,1)}, bf16[128,2048]{1,0:T(8,128)(2,1)S(1)}, u32[]{:S(2)}, u32[]{:S(2)}) collective-permute-start(bf16[128,2048]{1,0:T(8,128)(2,1)} %get-tuple-element.30), channel_id=1, source_target_pairs={{0,3},{1,2},{2,1},{3,0},{4,7},{5,6},{6,5},{7,4},{8,11},{9,10},{10,... | collective-permute-start | bytes 1572872 | tf_op jit(solution)/shard_map/ppermute | solution.py:41
  32.9 8.5 %all-to-all-done = bf16[32,16,256]{2,1,0:T(8,128)(2,1)S(1)} async-done(((bf16[32,16,256]{2,1,0:T(8,128)(2,1)}), bf16[32,16,256]{2,1,0:T(8,128)(2,1)S(1)}, u32[]{:S(2)}, u32[]{:S(2)}) %all-to-all-start) | async-done | bytes 262176 | tf_op jit(solution)/shard_map/all_to_all | solution.py:34
  41.5 2.6 %collective-permute-start.4 = (bf16[8,2,16,256]{3,2,1,0:T(8,128)(2,1)S(1)}, bf16[8,2,16,256]{3,2,1,0:T(8,128)(2,1)S(1)}, u32[]{:S(2)}, u32[]{:S(2)}) collective-permute-start(bf16[8,2,16,256]{3,2,1,0:T(8,128)(2,1)S(1)} %bitcast.29), channel_id=1, source_target_pairs={{0,12},{4,8},{8,4},{12,0},{1,13},{5,9},{9,5},{13,1},{2,14},{6,10},... | collective-permute-start | bytes 393224 | tf_op jit(solution)/shard_map/ppermute | solution.py:41
  44.1 2.7 %collective-permute-start.6 = (bf16[8,2,16,256]{3,2,1,0:T(8,128)(2,1)S(1)}, bf16[8,2,16,256]{3,2,1,0:T(8,128)(2,1)S(1)}, u32[]{:S(2)}, u32[]{:S(2)}) collective-permute-start(bf16[8,2,16,256]{3,2,1,0:T(8,128)(2,1)S(1)} %bitcast.28), channel_id=1, source_target_pairs={{0,12},{4,8},{8,4},{12,0},{1,13},{5,9},{9,5},{13,1},{2,14},{6,10},... | collective-permute-start | bytes 393224 | tf_op jit(solution)/shard_map/ppermute | solution.py:41
  46.8 0.0 collective-permute-done.a1
  46.8 2.6 %collective-permute-start.3 = (bf16[16,2,16,256]{3,2,1,0:T(8,128)(2,1)S(1)}, bf16[16,2,16,256]{3,2,1,0:T(8,128)(2,1)S(1)}, u32[]{:S(2)}, u32[]{:S(2)}) collective-permute-start(bf16[16,2,16,256]{3,2,1,0:T(8,128)(2,1)S(1)} %bitcast.20), channel_id=1, source_target_pairs={{0,4},{4,0},{8,12},{12,8},{1,5},{5,1},{9,13},{13,9},{2,6},{6,2},{1... | collective-permute-start | bytes 786440 | tf_op jit(solution)/shard_map/ppermute | solution.py:41
  49.4 4.4 %collective-permute-done.4.refs_4_ = bf16[8,2,16,256]{3,2,1,0:T(8,128)(2,1)S(1)} collective-permute-done((bf16[8,2,16,256]{3,2,1,0:T(8,128)(2,1)S(1)}, bf16[8,2,16,256]{3,2,1,0:T(8,128)(2,1)S(1)}, u32[]{:S(2)}, u32[]{:S(2)}) %collective-permute-start.4) | collective-permute-done | bytes 131104 | tf_op jit(solution)/shard_map/ppermute | solution.py:41
  53.8 1.9 %collective-permute-start.5 = (bf16[8,2,16,256]{3,2,1,0:T(8,128)(2,1)S(1)}, bf16[8,2,16,256]{3,2,1,0:T(8,128)(2,1)S(1)}, u32[]{:S(2)}, u32[]{:S(2)}) collective-permute-start(bf16[8,2,16,256]{3,2,1,0:T(8,128)(2,1)S(1)} %collective-permute-done.4.refs_4_), channel_id=1, source_target_pairs={{0,4},{4,0},{8,12},{12,8},{1,5},{5,1},{9,13},{13,9},{2,6},{6,2},{1... | collective-permute-start | bytes 393224 | tf_op jit(solution)/shard_map/ppermute | solution.py:41
  55.7 1.0 collective-permute-done.6.refs_5_
  56.7 2.4 %collective-permute-start.7 = (bf16[8,2,16,256]{3,2,1,0:T(8,128)(2,1)S(1)}, bf16[8,2,16,256]{3,2,1,0:T(8,128)(2,1)S(1)}, u32[]{:S(2)}, u32[]{:S(2)}) collective-permute-start(bf16[8,2,16,256]{3,2,1,0:T(8,128)(2,1)S(1)} %collective-permute-done.6.refs_5_), channel_id=1, source_target_pairs={{0,4},{4,0},{8,12},{12,8},{1,5},{5,1},{9,13},{13,9},{2,6},{6,2},{1... | collective-permute-start | bytes 393224 | tf_op jit(solution)/shard_map/ppermute | solution.py:41
  59.1 0.1 pad_add_fusion.s_ref
  59.2 0.0 copy-done.9
  59.2 1.6 %copy-done = bf16[1,8192,128]{2,1,0:T(8,128)(2,1)S(1)} copy-done((bf16[1,8192,128]{2,1,0:T(8,128)(2,1)S(1)}, bf16[1,8192,128]{2,1,0:T(8,128)(2,1)}, u32[]{:S(2)}) %copy-start) | copy-done | bytes 2097176
  60.8 1.6 %copy-done.2 = bf16[1,8192,128]{2,1,0:T(8,128)(2,1)S(1)} copy-done((bf16[1,8192,128]{2,1,0:T(8,128)(2,1)S(1)}, bf16[1,8192,128]{2,1,0:T(8,128)(2,1)}, u32[]{:S(2)}) %copy-start.2) | copy-done | bytes 2097176
  62.4 1.2 shard_map.77.a0
  63.6 0.0 collective-permute-done.1.a2
  63.6 0.0 copy-start.3
  63.6 0.0 collective-permute-done.2.a3
  63.7 0.0 collective-permute-done.5.refs_2_
  63.7 0.0 collective-permute-done.7.refs_3_
  63.7 0.0 collective-permute-done.3.refs_1_
  63.7 2.5 %shard_map.79 = bf16[4,128,256]{2,1,0:T(8,128)(2,1)} custom-call(s32[2]{0:T(128)S(1)} %pad_add_fusion.s_ref, bf16[128,2048]{1,0:T(8,128)(2,1)S(1)} %shard_map.77.a0, bf16[128,2048]{1,0:T(8,128)(2,1)S(1)} %collective-permute-done.a1, bf16[128,2048]{1,0:T(8,128)(2,1)S(1)} %collective-permute-done.1.a2, bf16[128,2048]{1,0:T(8,128)(2,1)S(1)} %collective-permute-done.2.a3, ...), custom_call_target="tpu_custom_call" | custom-call | flops 536870912 | bytes 4194304 | tf_op jit(solution)/shard_map/pallas_call | solution.py:182
  66.2 4.0 %all-to-all-start.1 = ((bf16[4,128,256]{2,1,0:T(8,128)(2,1)}), bf16[4,128,256]{2,1,0:T(8,128)(2,1)S(1)}, u32[]{:S(2)}, u32[]{:S(2)}) async-start(bf16[4,128,256]{2,1,0:T(8,128)(2,1)} %shard_map.79), calls=%async_computation.1 | async-start | bytes 524288 | tf_op jit(solution)/shard_map/all_to_all | solution.py:309
  70.9 4.9 %all-to-all-done.1.s_ref = bf16[4,128,256]{2,1,0:T(8,128)(2,1)S(1)} async-done(((bf16[4,128,256]{2,1,0:T(8,128)(2,1)}), bf16[4,128,256]{2,1,0:T(8,128)(2,1)S(1)}, u32[]{:S(2)}, u32[]{:S(2)}) %all-to-all-start.1) | async-done | bytes 262176 | tf_op jit(solution)/shard_map/all_to_all | solution.py:309
  75.7 0.3 shard_map.80
  76.0 7.9 %all_to_all.20.g_ref = bf16[4,256,128]{2,1,0:T(8,128)(2,1)S(1)} all-to-all(bf16[4,256,128]{2,1,0:T(8,128)(2,1)S(1)} %shard_map.80), channel_id=1, replica_groups=mesh['zh'=2,'y'=4,'c'=2,'za'=2,'zb'=2,'z2'=2,'x'=4] {'x'}, dimensions={0} | all-to-all | bytes 524288 | tf_op jit(solution)/shard_map/all_to_all | solution.py:310
  84.0 0.0 copy-done.5
  84.0 1.2 shard_map.81
  85.1 3.3 %collective-permute-start.8 = (bf16[16,2,16,256]{3,2,1,0:T(8,128)(2,1)S(1)}, bf16[16,2,16,256]{3,2,1,0:T(8,128)(2,1)S(1)}, u32[]{:S(2)}, u32[]{:S(2)}) collective-permute-start(bf16[16,2,16,256]{3,2,1,0:T(8,128)(2,1)S(1)} %get-tuple-element.32), channel_id=1, source_target_pairs={{0,4},{4,0},{8,12},{12,8},{1,5},{5,1},{9,13},{13,9},{2,6},{6,2},{1... | collective-permute-start | bytes 786440 | tf_op jit(solution)/shard_map/ppermute | solution.py:41
  88.4 2.1 %collective-permute-start.11 = (bf16[16,2,16,256]{3,2,1,0:T(8,128)(2,1)S(1)}, bf16[16,2,16,256]{3,2,1,0:T(8,128)(2,1)S(1)}, u32[]{:S(2)}, u32[]{:S(2)}) collective-permute-start(bf16[16,2,16,256]{3,2,1,0:T(8,128)(2,1)S(1)} %get-tuple-element.40), channel_id=1, source_target_pairs={{0,4},{4,0},{8,12},{12,8},{1,5},{5,1},{9,13},{13,9},{2,6},{6,2},{1... | collective-permute-start | bytes 786440 | tf_op jit(solution)/shard_map/ppermute | solution.py:41
  90.6 1.1 shard_map.82
  91.7 0.0 copy-start.7
  91.7 0.0 copy-start.11
  91.7 0.0 copy-start.12
  91.7 0.7 collective-permute-done.8
  92.4 0.1 add_convert_fusion.1
  92.5 0.0 copy-start.1
  92.5 2.9 %collective-permute-start.12 = (bf16[16,2,16,256]{3,2,1,0:T(8,128)(2,1)S(1)}, bf16[16,2,16,256]{3,2,1,0:T(8,128)(2,1)S(1)}, u32[]{:S(2)}, u32[]{:S(2)}) collective-permute-start(bf16[16,2,16,256]{3,2,1,0:T(8,128)(2,1)S(1)} %add_convert_fusion.1), channel_id=1, source_target_pairs={{0,12},{4,8},{8,4},{12,0},{1,13},{5,9},{9,5},{13,1},{2,14},{6,10},... | collective-permute-start | bytes 786440 | tf_op jit(solution)/shard_map/ppermute | solution.py:41
  95.3 2.8 %collective-permute-start.13 = (bf16[64,2048]{1,0:T(8,128)(2,1)S(1)}, bf16[64,2048]{1,0:T(8,128)(2,1)S(1)}, u32[]{:S(2)}, u32[]{:S(2)}) collective-permute-start(bf16[64,2048]{1,0:T(8,128)(2,1)S(1)} %get-tuple-element.43), channel_id=1, source_target_pairs={{0,3},{1,2},{2,1},{3,0},{4,7},{5,6},{6,5},{7,4},{8,11},{9,10},{10,... | collective-permute-start | bytes 786440 | tf_op jit(solution)/shard_map/ppermute | solution.py:41
  98.1 0.0 copy-done.4
  98.2 0.0 copy-done.6
  98.2 0.8 shard_map.83
  99.0 0.0 collective-permute-done.11
  99.0 1.9 %collective-permute-done.12 = bf16[16,2,16,256]{3,2,1,0:T(8,128)(2,1)S(1)} collective-permute-done((bf16[16,2,16,256]{3,2,1,0:T(8,128)(2,1)S(1)}, bf16[16,2,16,256]{3,2,1,0:T(8,128)(2,1)S(1)}, u32[]{:S(2)}, u32[]{:S(2)}) %collective-permute-start.12) | collective-permute-done | bytes 262176 | tf_op jit(solution)/shard_map/ppermute | solution.py:41
  100.9 0.8 add_convert_fusion
  101.7 0.0 copy-done.7
  101.7 0.0 copy-done.12
  101.8 1.9 %collective-permute-done.13.x3 = bf16[64,2048]{1,0:T(8,128)(2,1)S(1)} collective-permute-done((bf16[64,2048]{1,0:T(8,128)(2,1)S(1)}, bf16[64,2048]{1,0:T(8,128)(2,1)S(1)}, u32[]{:S(2)}, u32[]{:S(2)}) %collective-permute-start.13) | collective-permute-done | bytes 262176 | tf_op jit(solution)/shard_map/ppermute | solution.py:41
  103.7 15.5 %all-to-all-start.3 = ((bf16[32,16,256]{2,1,0:T(8,128)(2,1)}), bf16[32,16,256]{2,1,0:T(8,128)(2,1)S(1)}, u32[]{:S(2)}, u32[]{:S(2)}) async-start(bf16[32,16,256]{2,1,0:T(8,128)(2,1)} %bitcast.12), calls=%async_computation.3 | async-start | bytes 524288 | tf_op jit(solution)/shard_map/all_to_all | solution.py:34
  119.2 1.9 %collective-permute-start.9 = (bf16[64,2048]{1,0:T(8,128)(2,1)}, bf16[64,2048]{1,0:T(8,128)(2,1)S(1)}, u32[]{:S(2)}, u32[]{:S(2)}) collective-permute-start(bf16[64,2048]{1,0:T(8,128)(2,1)} %copy-done.12), channel_id=1, source_target_pairs={{0,1},{1,0},{2,3},{3,2},{4,5},{5,4},{6,7},{7,6},{8,9},{9,8},{10,11... | collective-permute-start | bytes 786440 | tf_op jit(solution)/shard_map/ppermute | solution.py:41
  121.1 4.0 %collective-permute-start.10 = (bf16[64,2048]{1,0:T(8,128)(2,1)}, bf16[64,2048]{1,0:T(8,128)(2,1)S(1)}, u32[]{:S(2)}, u32[]{:S(2)}) collective-permute-start(bf16[64,2048]{1,0:T(8,128)(2,1)} %copy-done.11), channel_id=1, source_target_pairs={{0,2},{1,3},{2,0},{3,1},{4,6},{5,7},{6,4},{7,5},{8,10},{9,11},{10,... | collective-permute-start | bytes 786440 | tf_op jit(solution)/shard_map/ppermute | solution.py:41
  125.1 3.9 %collective-permute-done.9.x1 = bf16[64,2048]{1,0:T(8,128)(2,1)S(1)} collective-permute-done((bf16[64,2048]{1,0:T(8,128)(2,1)}, bf16[64,2048]{1,0:T(8,128)(2,1)S(1)}, u32[]{:S(2)}, u32[]{:S(2)}) %collective-permute-start.9) | collective-permute-done | bytes 262176 | tf_op jit(solution)/shard_map/ppermute | solution.py:41
  128.9 6.2 %collective-permute-done.10.x2 = bf16[64,2048]{1,0:T(8,128)(2,1)S(1)} collective-permute-done((bf16[64,2048]{1,0:T(8,128)(2,1)}, bf16[64,2048]{1,0:T(8,128)(2,1)S(1)}, u32[]{:S(2)}, u32[]{:S(2)}) %collective-permute-start.10) | collective-permute-done | bytes 262176 | tf_op jit(solution)/shard_map/ppermute | solution.py:41
  135.2 0.9 copy-done.8
  136.1 1.8 %shard_map.84 = bf16[64,128]{1,0:T(8,128)(2,1)} custom-call(s32[2]{0:T(128)S(1)} %pad_add_fusion.s_ref, bf16[64,2048]{1,0:T(8,128)(2,1)S(1)} %copy-done.8, bf16[64,2048]{1,0:T(8,128)(2,1)S(1)} %collective-permute-done.9.x1, bf16[64,2048]{1,0:T(8,128)(2,1)S(1)} %collective-permute-done.10.x2, bf16[64,2048]{1,0:T(8,128)(2,1)S(1)} %collective-permute-done.13.x3, ...), custom_call_target="tpu_custom_call" | custom-call | flops 134217728 | bytes 3145728 | tf_op jit(solution)/shard_map/pallas_call | solution.py:261
  137.9 4.0 %all-to-all-done.3 = bf16[32,16,256]{2,1,0:T(8,128)(2,1)S(1)} async-done(((bf16[32,16,256]{2,1,0:T(8,128)(2,1)}), bf16[32,16,256]{2,1,0:T(8,128)(2,1)S(1)}, u32[]{:S(2)}, u32[]{:S(2)}) %all-to-all-start.3) | async-done | bytes 262176 | tf_op jit(solution)/shard_map/all_to_all | solution.py:34
  142.0 0.7 shard_map.85
  (11 shorter events, 0.0 us)
Async XLA Ops:
  2.3 39.2 %all-to-all-start = ((bf16[32,16,256]{2,1,0:T(8,128)(2,1)}), bf16[32,16,256]{2,1,0:T(8,128)(2,1)S(1)}, u32[]{:S(2)}, u32[]{:S(2)}) async-start(bf16[32,16,256]{2,1,0:T(8,128)(2,1)} %bitcast.7), calls=%async_computation | async-start | bytes 524288 | tf_op jit(solution)/shard_map/all_to_all | solution.py:34
  19.5 39.7 %copy-start.9 = (bf16[1,64,128]{2,1,0:T(8,128)(2,1)S(1)}, bf16[1,64,128]{2,1,0:T(8,128)(2,1)}, u32[]{:S(2)}) copy-start(bf16[1,64,128]{2,1,0:T(8,128)(2,1)} %param.9) | copy-start | bytes 49156
  19.5 39.7 %copy-start.10 = (bf16[1,64,128]{2,1,0:T(8,128)(2,1)S(1)}, bf16[1,64,128]{2,1,0:T(8,128)(2,1)}, u32[]{:S(2)}) copy-start(bf16[1,64,128]{2,1,0:T(8,128)(2,1)} %param.10) | copy-start | bytes 49156
  23.3 23.4 %collective-permute-start = (bf16[128,2048]{1,0:T(8,128)(2,1)}, bf16[128,2048]{1,0:T(8,128)(2,1)S(1)}, u32[]{:S(2)}, u32[]{:S(2)}) collective-permute-start(bf16[128,2048]{1,0:T(8,128)(2,1)} %get-tuple-element.28), channel_id=1, source_target_pairs={{0,1},{1,0},{2,3},{3,2},{4,5},{5,4},{6,7},{7,6},{8,9},{9,8},{10,11... | collective-permute-start | bytes 1572872 | tf_op jit(solution)/shard_map/ppermute | solution.py:41
  26.4 37.2 %collective-permute-start.1 = (bf16[128,2048]{1,0:T(8,128)(2,1)}, bf16[128,2048]{1,0:T(8,128)(2,1)S(1)}, u32[]{:S(2)}, u32[]{:S(2)}) collective-permute-start(bf16[128,2048]{1,0:T(8,128)(2,1)} %get-tuple-element.29), channel_id=1, source_target_pairs={{0,2},{1,3},{2,0},{3,1},{4,6},{5,7},{6,4},{7,5},{8,10},{9,11},{10,... | collective-permute-start | bytes 1572872 | tf_op jit(solution)/shard_map/ppermute | solution.py:41
  30.8 32.8 %collective-permute-start.2 = (bf16[128,2048]{1,0:T(8,128)(2,1)}, bf16[128,2048]{1,0:T(8,128)(2,1)S(1)}, u32[]{:S(2)}, u32[]{:S(2)}) collective-permute-start(bf16[128,2048]{1,0:T(8,128)(2,1)} %get-tuple-element.30), channel_id=1, source_target_pairs={{0,3},{1,2},{2,1},{3,0},{4,7},{5,6},{6,5},{7,4},{8,11},{9,10},{10,... | collective-permute-start | bytes 1572872 | tf_op jit(solution)/shard_map/ppermute | solution.py:41
  41.5 12.4 %collective-permute-start.4 = (bf16[8,2,16,256]{3,2,1,0:T(8,128)(2,1)S(1)}, bf16[8,2,16,256]{3,2,1,0:T(8,128)(2,1)S(1)}, u32[]{:S(2)}, u32[]{:S(2)}) collective-permute-start(bf16[8,2,16,256]{3,2,1,0:T(8,128)(2,1)S(1)} %bitcast.29), channel_id=1, source_target_pairs={{0,12},{4,8},{8,4},{12,0},{1,13},{5,9},{9,5},{13,1},{2,14},{6,10},... | collective-permute-start | bytes 393224 | tf_op jit(solution)/shard_map/ppermute | solution.py:41
  44.1 12.6 %collective-permute-start.6 = (bf16[8,2,16,256]{3,2,1,0:T(8,128)(2,1)S(1)}, bf16[8,2,16,256]{3,2,1,0:T(8,128)(2,1)S(1)}, u32[]{:S(2)}, u32[]{:S(2)}) collective-permute-start(bf16[8,2,16,256]{3,2,1,0:T(8,128)(2,1)S(1)} %bitcast.28), channel_id=1, source_target_pairs={{0,12},{4,8},{8,4},{12,0},{1,13},{5,9},{9,5},{13,1},{2,14},{6,10},... | collective-permute-start | bytes 393224 | tf_op jit(solution)/shard_map/ppermute | solution.py:41
  46.8 16.9 %collective-permute-start.3 = (bf16[16,2,16,256]{3,2,1,0:T(8,128)(2,1)S(1)}, bf16[16,2,16,256]{3,2,1,0:T(8,128)(2,1)S(1)}, u32[]{:S(2)}, u32[]{:S(2)}) collective-permute-start(bf16[16,2,16,256]{3,2,1,0:T(8,128)(2,1)S(1)} %bitcast.20), channel_id=1, source_target_pairs={{0,4},{4,0},{8,12},{12,8},{1,5},{5,1},{9,13},{13,9},{2,6},{6,2},{1... | collective-permute-start | bytes 786440 | tf_op jit(solution)/shard_map/ppermute | solution.py:41
  53.8 9.9 %collective-permute-start.5 = (bf16[8,2,16,256]{3,2,1,0:T(8,128)(2,1)S(1)}, bf16[8,2,16,256]{3,2,1,0:T(8,128)(2,1)S(1)}, u32[]{:S(2)}, u32[]{:S(2)}) collective-permute-start(bf16[8,2,16,256]{3,2,1,0:T(8,128)(2,1)S(1)} %collective-permute-done.4.refs_4_), channel_id=1, source_target_pairs={{0,4},{4,0},{8,12},{12,8},{1,5},{5,1},{9,13},{13,9},{2,6},{6,2},{1... | collective-permute-start | bytes 393224 | tf_op jit(solution)/shard_map/ppermute | solution.py:41
  56.7 7.0 %collective-permute-start.7 = (bf16[8,2,16,256]{3,2,1,0:T(8,128)(2,1)S(1)}, bf16[8,2,16,256]{3,2,1,0:T(8,128)(2,1)S(1)}, u32[]{:S(2)}, u32[]{:S(2)}) collective-permute-start(bf16[8,2,16,256]{3,2,1,0:T(8,128)(2,1)S(1)} %collective-permute-done.6.refs_5_), channel_id=1, source_target_pairs={{0,4},{4,0},{8,12},{12,8},{1,5},{5,1},{9,13},{13,9},{2,6},{6,2},{1... | collective-permute-start | bytes 393224 | tf_op jit(solution)/shard_map/ppermute | solution.py:41
  59.2 1.6 %copy-start = (bf16[1,8192,128]{2,1,0:T(8,128)(2,1)S(1)}, bf16[1,8192,128]{2,1,0:T(8,128)(2,1)}, u32[]{:S(2)}) copy-start(bf16[1,8192,128]{2,1,0:T(8,128)(2,1)} %param.7) | copy-start | bytes 6291460
  60.8 1.6 %copy-start.2 = (bf16[1,8192,128]{2,1,0:T(8,128)(2,1)S(1)}, bf16[1,8192,128]{2,1,0:T(8,128)(2,1)}, u32[]{:S(2)}) copy-start(bf16[1,8192,128]{2,1,0:T(8,128)(2,1)} %param.8) | copy-start | bytes 6291460
  63.6 20.3 %copy-start.3 = (bf16[128,2048]{1,0:T(8,128)(2,1)}, bf16[128,2048]{1,0:T(8,128)(2,1)S(1)}, u32[]{:S(2)}) copy-start(bf16[128,2048]{1,0:T(8,128)(2,1)S(1)} %collective-permute-done.1.a2) | copy-start | bytes 1572868
  63.7 20.3 %copy-start.5 = (bf16[128,2048]{1,0:T(8,128)(2,1)}, bf16[128,2048]{1,0:T(8,128)(2,1)S(1)}, u32[]{:S(2)}) copy-start(bf16[128,2048]{1,0:T(8,128)(2,1)S(1)} %collective-permute-done.2.a3) | copy-start | bytes 1572868
  66.2 9.5 %all-to-all-start.1 = ((bf16[4,128,256]{2,1,0:T(8,128)(2,1)}), bf16[4,128,256]{2,1,0:T(8,128)(2,1)S(1)}, u32[]{:S(2)}, u32[]{:S(2)}) async-start(bf16[4,128,256]{2,1,0:T(8,128)(2,1)} %shard_map.79), calls=%async_computation.1 | async-start | bytes 524288 | tf_op jit(solution)/shard_map/all_to_all | solution.py:309
  85.1 13.0 %copy-start.4 = (bf16[128,2048]{1,0:T(8,128)(2,1)S(1)}, bf16[128,2048]{1,0:T(8,128)(2,1)}, u32[]{:S(2)}) copy-start(bf16[128,2048]{1,0:T(8,128)(2,1)} %copy-done.3) | copy-start | bytes 1572868
  85.1 13.0 %copy-start.6 = (bf16[128,2048]{1,0:T(8,128)(2,1)S(1)}, bf16[128,2048]{1,0:T(8,128)(2,1)}, u32[]{:S(2)}) copy-start(bf16[128,2048]{1,0:T(8,128)(2,1)} %copy-done.5) | copy-start | bytes 1572868
  85.1 7.2 %collective-permute-start.8 = (bf16[16,2,16,256]{3,2,1,0:T(8,128)(2,1)S(1)}, bf16[16,2,16,256]{3,2,1,0:T(8,128)(2,1)S(1)}, u32[]{:S(2)}, u32[]{:S(2)}) collective-permute-start(bf16[16,2,16,256]{3,2,1,0:T(8,128)(2,1)S(1)} %get-tuple-element.32), channel_id=1, source_target_pairs={{0,4},{4,0},{8,12},{12,8},{1,5},{5,1},{9,13},{13,9},{2,6},{6,2},{1... | collective-permute-start | bytes 786440 | tf_op jit(solution)/shard_map/ppermute | solution.py:41
  88.4 10.6 %collective-permute-start.11 = (bf16[16,2,16,256]{3,2,1,0:T(8,128)(2,1)S(1)}, bf16[16,2,16,256]{3,2,1,0:T(8,128)(2,1)S(1)}, u32[]{:S(2)}, u32[]{:S(2)}) collective-permute-start(bf16[16,2,16,256]{3,2,1,0:T(8,128)(2,1)S(1)} %get-tuple-element.40), channel_id=1, source_target_pairs={{0,4},{4,0},{8,12},{12,8},{1,5},{5,1},{9,13},{13,9},{2,6},{6,2},{1... | collective-permute-start | bytes 786440 | tf_op jit(solution)/shard_map/ppermute | solution.py:41
  91.7 10.1 %copy-start.7 = (bf16[64,2048]{1,0:T(8,128)(2,1)}, bf16[64,2048]{1,0:T(8,128)(2,1)S(1)}, u32[]{:S(2)}) copy-start(bf16[64,2048]{1,0:T(8,128)(2,1)S(1)} %get-tuple-element.37.x0) | copy-start | bytes 786436
  91.7 10.1 %copy-start.11 = (bf16[64,2048]{1,0:T(8,128)(2,1)}, bf16[64,2048]{1,0:T(8,128)(2,1)S(1)}, u32[]{:S(2)}) copy-start(bf16[64,2048]{1,0:T(8,128)(2,1)S(1)} %get-tuple-element.39) | copy-start | bytes 786436
  91.7 10.1 %copy-start.12 = (bf16[64,2048]{1,0:T(8,128)(2,1)}, bf16[64,2048]{1,0:T(8,128)(2,1)S(1)}, u32[]{:S(2)}) copy-start(bf16[64,2048]{1,0:T(8,128)(2,1)S(1)} %get-tuple-element.38) | copy-start | bytes 786436
  92.5 42.7 %copy-start.1 = (bf16[1,8192,128]{2,1,0:T(8,128)(2,1)S(1)}, bf16[1,8192,128]{2,1,0:T(8,128)(2,1)}, u32[]{:S(2)}) copy-start(bf16[1,8192,128]{2,1,0:T(8,128)(2,1)} %param.7) | copy-start | bytes 6291460
  92.5 8.4 %collective-permute-start.12 = (bf16[16,2,16,256]{3,2,1,0:T(8,128)(2,1)S(1)}, bf16[16,2,16,256]{3,2,1,0:T(8,128)(2,1)S(1)}, u32[]{:S(2)}, u32[]{:S(2)}) collective-permute-start(bf16[16,2,16,256]{3,2,1,0:T(8,128)(2,1)S(1)} %add_convert_fusion.1), channel_id=1, source_target_pairs={{0,12},{4,8},{8,4},{12,0},{1,13},{5,9},{9,5},{13,1},{2,14},{6,10},... | collective-permute-start | bytes 786440 | tf_op jit(solution)/shard_map/ppermute | solution.py:41
  95.3 8.3 %collective-permute-start.13 = (bf16[64,2048]{1,0:T(8,128)(2,1)S(1)}, bf16[64,2048]{1,0:T(8,128)(2,1)S(1)}, u32[]{:S(2)}, u32[]{:S(2)}) collective-permute-start(bf16[64,2048]{1,0:T(8,128)(2,1)S(1)} %get-tuple-element.43), channel_id=1, source_target_pairs={{0,3},{1,2},{2,1},{3,0},{4,7},{5,6},{6,5},{7,4},{8,11},{9,10},{10,... | collective-permute-start | bytes 786440 | tf_op jit(solution)/shard_map/ppermute | solution.py:41
  103.7 38.3 %all-to-all-start.3 = ((bf16[32,16,256]{2,1,0:T(8,128)(2,1)}), bf16[32,16,256]{2,1,0:T(8,128)(2,1)S(1)}, u32[]{:S(2)}, u32[]{:S(2)}) async-start(bf16[32,16,256]{2,1,0:T(8,128)(2,1)} %bitcast.12), calls=%async_computation.3 | async-start | bytes 524288 | tf_op jit(solution)/shard_map/all_to_all | solution.py:34
  119.2 9.8 %collective-permute-start.9 = (bf16[64,2048]{1,0:T(8,128)(2,1)}, bf16[64,2048]{1,0:T(8,128)(2,1)S(1)}, u32[]{:S(2)}, u32[]{:S(2)}) collective-permute-start(bf16[64,2048]{1,0:T(8,128)(2,1)} %copy-done.12), channel_id=1, source_target_pairs={{0,1},{1,0},{2,3},{3,2},{4,5},{5,4},{6,7},{7,6},{8,9},{9,8},{10,11... | collective-permute-start | bytes 786440 | tf_op jit(solution)/shard_map/ppermute | solution.py:41
  121.1 14.1 %collective-permute-start.10 = (bf16[64,2048]{1,0:T(8,128)(2,1)}, bf16[64,2048]{1,0:T(8,128)(2,1)S(1)}, u32[]{:S(2)}, u32[]{:S(2)}) collective-permute-start(bf16[64,2048]{1,0:T(8,128)(2,1)} %copy-done.11), channel_id=1, source_target_pairs={{0,2},{1,3},{2,0},{3,1},{4,6},{5,7},{6,4},{7,5},{8,10},{9,11},{10,... | collective-permute-start | bytes 786440 | tf_op jit(solution)/shard_map/ppermute | solution.py:41
  135.2 1.0 copy-start.8

commit v8 on v7

--- a/solution.py
+++ b/solution.py
@@ -316,7 +316,7 @@
     kept = term(scalars, grads, shared, (0,), F32)[0]
     sent = (kept + near.astype(F32) + third.astype(F32)).astype(BF16)
     mixed = to_members(mixture)
-    sent, mixed[3] = lax.optimization_barrier((sent, mixed[3]))
+    sent, mixed[1], mixed[3] = lax.optimization_barrier((sent, mixed[1], mixed[3]))
     terms = spread(sent, ROW_GROUPS)
     grad_queries = query(scalars, mixed, wk)
     grad_encoded = total_terms(terms)

time: 144 us -> 147 us (1.021)
  waiting for transfers between devices: 37.4 us -> 40.2 us
  local copies, waits for them, and re-layouts: 5.83 us -> 7.48 us
    all_to_all x2, waiting for transfers between devices: 12.5 us -> 16.3 us  [spread(): lax.all_to_all(blocks.reshape(-1, 16, BLOCK), SPREAD_AXES, 0, 0, axis_ind...]
    unnamed x26 -> x28, local copies, waits for them, and re-layouts: 4.18 us -> 5.83 us
    ppermute x14, starting transfers between devices: 38.7 us -> 37.2 us  [swap(): return lax.ppermute(array, axes, [(i, i ^ k) for i in range(4)])]
  transfers between devices with their start and end apart: 17 -> 17, of which waited for: 10 -> 9; matrix products, arithmetic and copies ran while one was open for 1% -> 1% of each run, Pallas kernels for 6% -> 6%
where the time goes in v8:
time: 147 us; the launch traced here: 146 us
  starting transfers between devices  74.1 us (50%)
  waiting for transfers between devices  40.2 us (27%)
  Pallas kernels  13.4 us (9%)
  blocking collectives  7.92 us (5%)
  local copies, waits for them, and re-layouts  7.48 us (5%)
  between operations  1.64 us (1%)
    ppermute x14, starting transfers between devices, swap(): return lax.ppermute(array, axes, [(i, i ^ k) for i in range(4)])  37.2 us
    all_to_all x2, starting transfers between devices, spread(): lax.all_to_all(blocks.reshape(-1, 16, BLOCK), SPREAD_AXES, 0, 0, axis_ind...  32.9 us
    ppermute x14, waiting for transfers between devices, swap(): return lax.ppermute(array, axes, [(i, i ^ k) for i in range(4)])  19 us
    all_to_all x2, waiting for transfers between devices, spread(): lax.all_to_all(blocks.reshape(-1, 16, BLOCK), SPREAD_AXES, 0, 0, axis_ind...  16.3 us
    all_to_all x1, blocking collectives, local(): lax.all_to_all(attend(counts.reshape(1), parts), 'x', 0, 0, tiled=True)  7.92 us
    unnamed x28, local copies, waits for them, and re-layouts  5.83 us
    all_to_all x1, waiting for transfers between devices, local(): parts = lax.all_to_all(sums, 'x', 0, 0, tiled=True)  4.88 us
    all_to_all x1, starting transfers between devices, local(): parts = lax.all_to_all(sums, 'x', 0, 0, tiled=True)  4.01 us
  transfers between devices with their start and end apart: 17, of which 9 were waited for; matrix products, arithmetic and copies ran while one was open for 1% of the time, Pallas kernels for 6%

profile of v8, /device:TPU:33, one launch (start us, length us, event | category | flops | bytes accessed | tf_op | source)
XLA Modules:
  0.0 145.8 jit_solution(6924700314663001619)
XLA Ops:
  0.6 1.6 %broadcast_in_dim.4 = bf16[16,2,16,256]{3,2,1,0:T(8,128)(2,1)} broadcast(bf16[16,16,256]{2,1,0:T(8,128)(2,1)} %param.6), dimensions={0,2,3} | broadcast | bytes 393216 | tf_op jit(solution)/shard_map/broadcast_in_dim | solution.py:300
  2.3 17.2 %all-to-all-start = ((bf16[32,16,256]{2,1,0:T(8,128)(2,1)}), bf16[32,16,256]{2,1,0:T(8,128)(2,1)S(1)}, u32[]{:S(2)}, u32[]{:S(2)}) async-start(bf16[32,16,256]{2,1,0:T(8,128)(2,1)} %bitcast.7), calls=%async_computation | async-start | bytes 524288 | tf_op jit(solution)/shard_map/all_to_all | solution.py:34
  19.5 0.0 copy-start.11
  19.5 0.0 copy-start.12
  19.5 3.8 %shard_map.78 = (bf16[128,2048]{1,0:T(8,128)(2,1)}, bf16[128,2048]{1,0:T(8,128)(2,1)}, bf16[128,2048]{1,0:T(8,128)(2,1)}) custom-call(bf16[64,128]{1,0:T(8,128)(2,1)} %bitcast.24, bf16[64,128]{1,0:T(8,128)(2,1)} %bitcast.26, bf16[2,4,4,256,128]{4,3,2,1,0:T(8,128)(2,1)} %bitcast.15, bf16[2,4,4,256,128]{4,3,2,1,0:T(8,128)(2,1)} %bitcast.18), custom_call_target="tpu_custom_call" | custom-call | flops 201326592 | bytes 6291456 | tf_op jit(solution)/shard_map/pallas_call | solution.py:109
  23.3 3.1 %collective-permute-start = (bf16[128,2048]{1,0:T(8,128)(2,1)}, bf16[128,2048]{1,0:T(8,128)(2,1)S(1)}, u32[]{:S(2)}, u32[]{:S(2)}) collective-permute-start(bf16[128,2048]{1,0:T(8,128)(2,1)} %get-tuple-element.29), channel_id=1, source_target_pairs={{0,1},{1,0},{2,3},{3,2},{4,5},{5,4},{6,7},{7,6},{8,9},{9,8},{10,11... | collective-permute-start | bytes 1572872 | tf_op jit(solution)/shard_map/ppermute | solution.py:41
  26.4 4.4 %collective-permute-start.1 = (bf16[128,2048]{1,0:T(8,128)(2,1)}, bf16[128,2048]{1,0:T(8,128)(2,1)S(1)}, u32[]{:S(2)}, u32[]{:S(2)}) collective-permute-start(bf16[128,2048]{1,0:T(8,128)(2,1)} %get-tuple-element.30), channel_id=1, source_target_pairs={{0,2},{1,3},{2,0},{3,1},{4,6},{5,7},{6,4},{7,5},{8,10},{9,11},{10,... | collective-permute-start | bytes 1572872 | tf_op jit(solution)/shard_map/ppermute | solution.py:41
  30.8 2.1 %collective-permute-start.2 = (bf16[128,2048]{1,0:T(8,128)(2,1)}, bf16[128,2048]{1,0:T(8,128)(2,1)S(1)}, u32[]{:S(2)}, u32[]{:S(2)}) collective-permute-start(bf16[128,2048]{1,0:T(8,128)(2,1)} %get-tuple-element.31), channel_id=1, source_target_pairs={{0,3},{1,2},{2,1},{3,0},{4,7},{5,6},{6,5},{7,4},{8,11},{9,10},{10,... | collective-permute-start | bytes 1572872 | tf_op jit(solution)/shard_map/ppermute | solution.py:41
  32.9 8.6 %all-to-all-done = bf16[32,16,256]{2,1,0:T(8,128)(2,1)S(1)} async-done(((bf16[32,16,256]{2,1,0:T(8,128)(2,1)}), bf16[32,16,256]{2,1,0:T(8,128)(2,1)S(1)}, u32[]{:S(2)}, u32[]{:S(2)}) %all-to-all-start) | async-done | bytes 262176 | tf_op jit(solution)/shard_map/all_to_all | solution.py:34
  41.5 2.6 %collective-permute-start.4 = (bf16[8,2,16,256]{3,2,1,0:T(8,128)(2,1)S(1)}, bf16[8,2,16,256]{3,2,1,0:T(8,128)(2,1)S(1)}, u32[]{:S(2)}, u32[]{:S(2)}) collective-permute-start(bf16[8,2,16,256]{3,2,1,0:T(8,128)(2,1)S(1)} %bitcast.29), channel_id=1, source_target_pairs={{0,12},{4,8},{8,4},{12,0},{1,13},{5,9},{9,5},{13,1},{2,14},{6,10},... | collective-permute-start | bytes 393224 | tf_op jit(solution)/shard_map/ppermute | solution.py:41
  44.1 2.7 %collective-permute-start.6 = (bf16[8,2,16,256]{3,2,1,0:T(8,128)(2,1)S(1)}, bf16[8,2,16,256]{3,2,1,0:T(8,128)(2,1)S(1)}, u32[]{:S(2)}, u32[]{:S(2)}) collective-permute-start(bf16[8,2,16,256]{3,2,1,0:T(8,128)(2,1)S(1)} %bitcast.28), channel_id=1, source_target_pairs={{0,12},{4,8},{8,4},{12,0},{1,13},{5,9},{9,5},{13,1},{2,14},{6,10},... | collective-permute-start | bytes 393224 | tf_op jit(solution)/shard_map/ppermute | solution.py:41
  46.8 0.0 collective-permute-done.a1
  46.8 2.6 %collective-permute-start.3 = (bf16[16,2,16,256]{3,2,1,0:T(8,128)(2,1)S(1)}, bf16[16,2,16,256]{3,2,1,0:T(8,128)(2,1)S(1)}, u32[]{:S(2)}, u32[]{:S(2)}) collective-permute-start(bf16[16,2,16,256]{3,2,1,0:T(8,128)(2,1)S(1)} %bitcast.20), channel_id=1, source_target_pairs={{0,4},{4,0},{8,12},{12,8},{1,5},{5,1},{9,13},{13,9},{2,6},{6,2},{1... | collective-permute-start | bytes 786440 | tf_op jit(solution)/shard_map/ppermute | solution.py:41
  49.4 4.4 %collective-permute-done.4.refs_4_ = bf16[8,2,16,256]{3,2,1,0:T(8,128)(2,1)S(1)} collective-permute-done((bf16[8,2,16,256]{3,2,1,0:T(8,128)(2,1)S(1)}, bf16[8,2,16,256]{3,2,1,0:T(8,128)(2,1)S(1)}, u32[]{:S(2)}, u32[]{:S(2)}) %collective-permute-start.4) | collective-permute-done | bytes 131104 | tf_op jit(solution)/shard_map/ppermute | solution.py:41
  53.8 1.9 %collective-permute-start.5 = (bf16[8,2,16,256]{3,2,1,0:T(8,128)(2,1)S(1)}, bf16[8,2,16,256]{3,2,1,0:T(8,128)(2,1)S(1)}, u32[]{:S(2)}, u32[]{:S(2)}) collective-permute-start(bf16[8,2,16,256]{3,2,1,0:T(8,128)(2,1)S(1)} %collective-permute-done.4.refs_4_), channel_id=1, source_target_pairs={{0,4},{4,0},{8,12},{12,8},{1,5},{5,1},{9,13},{13,9},{2,6},{6,2},{1... | collective-permute-start | bytes 393224 | tf_op jit(solution)/shard_map/ppermute | solution.py:41
  55.7 1.0 collective-permute-done.6.refs_5_
  56.7 2.4 %collective-permute-start.7 = (bf16[8,2,16,256]{3,2,1,0:T(8,128)(2,1)S(1)}, bf16[8,2,16,256]{3,2,1,0:T(8,128)(2,1)S(1)}, u32[]{:S(2)}, u32[]{:S(2)}) collective-permute-start(bf16[8,2,16,256]{3,2,1,0:T(8,128)(2,1)S(1)} %collective-permute-done.6.refs_5_), channel_id=1, source_target_pairs={{0,4},{4,0},{8,12},{12,8},{1,5},{5,1},{9,13},{13,9},{2,6},{6,2},{1... | collective-permute-start | bytes 393224 | tf_op jit(solution)/shard_map/ppermute | solution.py:41
  59.1 0.1 pad_add_fusion.s_ref
  59.2 0.0 copy-done.11
  59.2 0.0 copy-done.12
  59.2 1.6 %copy-done = bf16[1,8192,128]{2,1,0:T(8,128)(2,1)S(1)} copy-done((bf16[1,8192,128]{2,1,0:T(8,128)(2,1)S(1)}, bf16[1,8192,128]{2,1,0:T(8,128)(2,1)}, u32[]{:S(2)}) %copy-start) | copy-done | bytes 2097176
  60.8 1.6 %copy-done.2 = bf16[1,8192,128]{2,1,0:T(8,128)(2,1)S(1)} copy-done((bf16[1,8192,128]{2,1,0:T(8,128)(2,1)S(1)}, bf16[1,8192,128]{2,1,0:T(8,128)(2,1)}, u32[]{:S(2)}) %copy-start.2) | copy-done | bytes 2097176
  62.4 1.2 shard_map.77.a0
  63.6 0.0 collective-permute-done.1.a2
  63.6 0.0 copy-start.3
  63.6 0.0 collective-permute-done.2.a3
  63.7 0.0 collective-permute-done.5.refs_2_
  63.7 0.0 collective-permute-done.7.refs_3_
  63.7 0.0 collective-permute-done.3.refs_1_
  63.7 2.5 %shard_map.79 = bf16[4,128,256]{2,1,0:T(8,128)(2,1)} custom-call(s32[2]{0:T(128)S(1)} %pad_add_fusion.s_ref, bf16[128,2048]{1,0:T(8,128)(2,1)S(1)} %shard_map.77.a0, bf16[128,2048]{1,0:T(8,128)(2,1)S(1)} %collective-permute-done.a1, bf16[128,2048]{1,0:T(8,128)(2,1)S(1)} %collective-permute-done.1.a2, bf16[128,2048]{1,0:T(8,128)(2,1)S(1)} %collective-permute-done.2.a3, ...), custom_call_target="tpu_custom_call" | custom-call | flops 536870912 | bytes 4194304 | tf_op jit(solution)/shard_map/pallas_call | solution.py:182
  66.2 4.0 %all-to-all-start.1 = ((bf16[4,128,256]{2,1,0:T(8,128)(2,1)}), bf16[4,128,256]{2,1,0:T(8,128)(2,1)S(1)}, u32[]{:S(2)}, u32[]{:S(2)}) async-start(bf16[4,128,256]{2,1,0:T(8,128)(2,1)} %shard_map.79), calls=%async_computation.1 | async-start | bytes 524288 | tf_op jit(solution)/shard_map/all_to_all | solution.py:309
  70.9 4.9 %all-to-all-done.1.s_ref = bf16[4,128,256]{2,1,0:T(8,128)(2,1)S(1)} async-done(((bf16[4,128,256]{2,1,0:T(8,128)(2,1)}), bf16[4,128,256]{2,1,0:T(8,128)(2,1)S(1)}, u32[]{:S(2)}, u32[]{:S(2)}) %all-to-all-start.1) | async-done | bytes 262176 | tf_op jit(solution)/shard_map/all_to_all | solution.py:309
  75.7 0.3 shard_map.80
  76.0 7.9 %all_to_all.20.g_ref = bf16[4,256,128]{2,1,0:T(8,128)(2,1)S(1)} all-to-all(bf16[4,256,128]{2,1,0:T(8,128)(2,1)S(1)} %shard_map.80), channel_id=1, replica_groups=mesh['zh'=2,'y'=4,'c'=2,'za'=2,'zb'=2,'z2'=2,'x'=4] {'x'}, dimensions={0} | all-to-all | bytes 524288 | tf_op jit(solution)/shard_map/all_to_all | solution.py:310
  84.0 0.0 copy-done.3
  84.0 1.2 shard_map.81
  85.1 0.0 copy-start.4
  85.1 0.0 copy-start.6
  85.1 3.3 %collective-permute-start.8 = (bf16[16,2,16,256]{3,2,1,0:T(8,128)(2,1)S(1)}, bf16[16,2,16,256]{3,2,1,0:T(8,128)(2,1)S(1)}, u32[]{:S(2)}, u32[]{:S(2)}) collective-permute-start(bf16[16,2,16,256]{3,2,1,0:T(8,128)(2,1)S(1)} %get-tuple-element.33), channel_id=1, source_target_pairs={{0,4},{4,0},{8,12},{12,8},{1,5},{5,1},{9,13},{13,9},{2,6},{6,2},{1... | collective-permute-start | bytes 786440 | tf_op jit(solution)/shard_map/ppermute | solution.py:41
  88.4 2.1 %collective-permute-start.9 = (bf16[16,2,16,256]{3,2,1,0:T(8,128)(2,1)S(1)}, bf16[16,2,16,256]{3,2,1,0:T(8,128)(2,1)S(1)}, u32[]{:S(2)}, u32[]{:S(2)}) collective-permute-start(bf16[16,2,16,256]{3,2,1,0:T(8,128)(2,1)S(1)} %get-tuple-element.39), channel_id=1, source_target_pairs={{0,4},{4,0},{8,12},{12,8},{1,5},{5,1},{9,13},{13,9},{2,6},{6,2},{1... | collective-permute-start | bytes 786440 | tf_op jit(solution)/shard_map/ppermute | solution.py:41
  90.6 1.1 shard_map.82
  91.7 0.0 copy-start.7
  91.7 0.7 collective-permute-done.8
  92.4 0.1 add_convert_fusion.1
  92.5 0.0 copy-start.1
  92.5 2.9 %collective-permute-start.10 = (bf16[16,2,16,256]{3,2,1,0:T(8,128)(2,1)S(1)}, bf16[16,2,16,256]{3,2,1,0:T(8,128)(2,1)S(1)}, u32[]{:S(2)}, u32[]{:S(2)}) collective-permute-start(bf16[16,2,16,256]{3,2,1,0:T(8,128)(2,1)S(1)} %add_convert_fusion.1), channel_id=1, source_target_pairs={{0,12},{4,8},{8,4},{12,0},{1,13},{5,9},{9,5},{13,1},{2,14},{6,10},... | collective-permute-start | bytes 786440 | tf_op jit(solution)/shard_map/ppermute | solution.py:41
  95.4 2.2 %collective-permute-start.11 = (bf16[64,2048]{1,0:T(8,128)(2,1)S(1)}, bf16[64,2048]{1,0:T(8,128)(2,1)S(1)}, u32[]{:S(2)}, u32[]{:S(2)}) collective-permute-start(bf16[64,2048]{1,0:T(8,128)(2,1)S(1)} %get-tuple-element.42), channel_id=1, source_target_pairs={{0,1},{1,0},{2,3},{3,2},{4,5},{5,4},{6,7},{7,6},{8,9},{9,8},{10,11... | collective-permute-start | bytes 786440 | tf_op jit(solution)/shard_map/ppermute | solution.py:41
  97.6 2.5 %collective-permute-start.12 = (bf16[64,2048]{1,0:T(8,128)(2,1)S(1)}, bf16[64,2048]{1,0:T(8,128)(2,1)S(1)}, u32[]{:S(2)}, u32[]{:S(2)}) collective-permute-start(bf16[64,2048]{1,0:T(8,128)(2,1)S(1)} %get-tuple-element.43), channel_id=1, source_target_pairs={{0,3},{1,2},{2,1},{3,0},{4,7},{5,6},{6,5},{7,4},{8,11},{9,10},{10,... | collective-permute-start | bytes 786440 | tf_op jit(solution)/shard_map/ppermute | solution.py:41
  100.1 0.8 shard_map.83
  100.9 0.0 collective-permute-done.9
  101.0 0.0 collective-permute-done.10
  101.0 0.8 add_convert_fusion
  101.8 0.0 copy-done.7
  101.8 1.0 collective-permute-done.11.x1
  102.8 3.1 %collective-permute-done.12.x3 = bf16[64,2048]{1,0:T(8,128)(2,1)S(1)} collective-permute-done((bf16[64,2048]{1,0:T(8,128)(2,1)S(1)}, bf16[64,2048]{1,0:T(8,128)(2,1)S(1)}, u32[]{:S(2)}, u32[]{:S(2)}) %collective-permute-start.12) | collective-permute-done | bytes 262176 | tf_op jit(solution)/shard_map/ppermute | solution.py:41
  105.9 0.7 copy-done.9
  106.6 15.7 %all-to-all-start.3 = ((bf16[32,16,256]{2,1,0:T(8,128)(2,1)}), bf16[32,16,256]{2,1,0:T(8,128)(2,1)S(1)}, u32[]{:S(2)}, u32[]{:S(2)}) async-start(bf16[32,16,256]{2,1,0:T(8,128)(2,1)} %bitcast.12), calls=%async_computation.3 | async-start | bytes 524288 | tf_op jit(solution)/shard_map/all_to_all | solution.py:34
  122.3 2.5 %collective-permute-start.13 = (bf16[64,2048]{1,0:T(8,128)(2,1)}, bf16[64,2048]{1,0:T(8,128)(2,1)S(1)}, u32[]{:S(2)}, u32[]{:S(2)}) collective-permute-start(bf16[64,2048]{1,0:T(8,128)(2,1)} %copy-done.13), channel_id=1, source_target_pairs={{0,2},{1,3},{2,0},{3,1},{4,6},{5,7},{6,4},{7,5},{8,10},{9,11},{10,... | collective-permute-start | bytes 786440 | tf_op jit(solution)/shard_map/ppermute | solution.py:41
  124.8 8.8 %collective-permute-done.13.x2 = bf16[64,2048]{1,0:T(8,128)(2,1)S(1)} collective-permute-done((bf16[64,2048]{1,0:T(8,128)(2,1)}, bf16[64,2048]{1,0:T(8,128)(2,1)S(1)}, u32[]{:S(2)}, u32[]{:S(2)}) %collective-permute-start.13) | collective-permute-done | bytes 262176 | tf_op jit(solution)/shard_map/ppermute | solution.py:41
  133.6 0.9 copy-done.8
  134.5 0.9 copy-done.10
  135.5 1.8 %shard_map.84 = bf16[64,128]{1,0:T(8,128)(2,1)} custom-call(s32[2]{0:T(128)S(1)} %pad_add_fusion.s_ref, bf16[64,2048]{1,0:T(8,128)(2,1)S(1)} %copy-done.8, bf16[64,2048]{1,0:T(8,128)(2,1)S(1)} %collective-permute-done.11.x1, bf16[64,2048]{1,0:T(8,128)(2,1)S(1)} %collective-permute-done.13.x2, bf16[64,2048]{1,0:T(8,128)(2,1)S(1)} %copy-done.10, ...), custom_call_target="tpu_custom_call" | custom-call | flops 134217728 | bytes 3145728 | tf_op jit(solution)/shard_map/pallas_call | solution.py:261
  137.3 7.8 %all-to-all-done.3 = bf16[32,16,256]{2,1,0:T(8,128)(2,1)S(1)} async-done(((bf16[32,16,256]{2,1,0:T(8,128)(2,1)}), bf16[32,16,256]{2,1,0:T(8,128)(2,1)S(1)}, u32[]{:S(2)}, u32[]{:S(2)}) %all-to-all-start.3) | async-done | bytes 262176 | tf_op jit(solution)/shard_map/all_to_all | solution.py:34
  145.1 0.7 shard_map.85
  (13 shorter events, 0.0 us)
Async XLA Ops:
  2.3 39.2 %all-to-all-start = ((bf16[32,16,256]{2,1,0:T(8,128)(2,1)}), bf16[32,16,256]{2,1,0:T(8,128)(2,1)S(1)}, u32[]{:S(2)}, u32[]{:S(2)}) async-start(bf16[32,16,256]{2,1,0:T(8,128)(2,1)} %bitcast.7), calls=%async_computation | async-start | bytes 524288 | tf_op jit(solution)/shard_map/all_to_all | solution.py:34
  19.5 39.7 %copy-start.11 = (bf16[1,64,128]{2,1,0:T(8,128)(2,1)S(1)}, bf16[1,64,128]{2,1,0:T(8,128)(2,1)}, u32[]{:S(2)}) copy-start(bf16[1,64,128]{2,1,0:T(8,128)(2,1)} %param.9) | copy-start | bytes 49156
  19.5 39.7 %copy-start.12 = (bf16[1,64,128]{2,1,0:T(8,128)(2,1)S(1)}, bf16[1,64,128]{2,1,0:T(8,128)(2,1)}, u32[]{:S(2)}) copy-start(bf16[1,64,128]{2,1,0:T(8,128)(2,1)} %param.10) | copy-start | bytes 49156
  23.3 23.5 %collective-permute-start = (bf16[128,2048]{1,0:T(8,128)(2,1)}, bf16[128,2048]{1,0:T(8,128)(2,1)S(1)}, u32[]{:S(2)}, u32[]{:S(2)}) collective-permute-start(bf16[128,2048]{1,0:T(8,128)(2,1)} %get-tuple-element.29), channel_id=1, source_target_pairs={{0,1},{1,0},{2,3},{3,2},{4,5},{5,4},{6,7},{7,6},{8,9},{9,8},{10,11... | collective-permute-start | bytes 1572872 | tf_op jit(solution)/shard_map/ppermute | solution.py:41
  26.4 37.2 %collective-permute-start.1 = (bf16[128,2048]{1,0:T(8,128)(2,1)}, bf16[128,2048]{1,0:T(8,128)(2,1)S(1)}, u32[]{:S(2)}, u32[]{:S(2)}) collective-permute-start(bf16[128,2048]{1,0:T(8,128)(2,1)} %get-tuple-element.30), channel_id=1, source_target_pairs={{0,2},{1,3},{2,0},{3,1},{4,6},{5,7},{6,4},{7,5},{8,10},{9,11},{10,... | collective-permute-start | bytes 1572872 | tf_op jit(solution)/shard_map/ppermute | solution.py:41
  30.8 32.9 %collective-permute-start.2 = (bf16[128,2048]{1,0:T(8,128)(2,1)}, bf16[128,2048]{1,0:T(8,128)(2,1)S(1)}, u32[]{:S(2)}, u32[]{:S(2)}) collective-permute-start(bf16[128,2048]{1,0:T(8,128)(2,1)} %get-tuple-element.31), channel_id=1, source_target_pairs={{0,3},{1,2},{2,1},{3,0},{4,7},{5,6},{6,5},{7,4},{8,11},{9,10},{10,... | collective-permute-start | bytes 1572872 | tf_op jit(solution)/shard_map/ppermute | solution.py:41
  41.5 12.4 %collective-permute-start.4 = (bf16[8,2,16,256]{3,2,1,0:T(8,128)(2,1)S(1)}, bf16[8,2,16,256]{3,2,1,0:T(8,128)(2,1)S(1)}, u32[]{:S(2)}, u32[]{:S(2)}) collective-permute-start(bf16[8,2,16,256]{3,2,1,0:T(8,128)(2,1)S(1)} %bitcast.29), channel_id=1, source_target_pairs={{0,12},{4,8},{8,4},{12,0},{1,13},{5,9},{9,5},{13,1},{2,14},{6,10},... | collective-permute-start | bytes 393224 | tf_op jit(solution)/shard_map/ppermute | solution.py:41
  44.1 12.6 %collective-permute-start.6 = (bf16[8,2,16,256]{3,2,1,0:T(8,128)(2,1)S(1)}, bf16[8,2,16,256]{3,2,1,0:T(8,128)(2,1)S(1)}, u32[]{:S(2)}, u32[]{:S(2)}) collective-permute-start(bf16[8,2,16,256]{3,2,1,0:T(8,128)(2,1)S(1)} %bitcast.28), channel_id=1, source_target_pairs={{0,12},{4,8},{8,4},{12,0},{1,13},{5,9},{9,5},{13,1},{2,14},{6,10},... | collective-permute-start | bytes 393224 | tf_op jit(solution)/shard_map/ppermute | solution.py:41
  46.8 16.9 %collective-permute-start.3 = (bf16[16,2,16,256]{3,2,1,0:T(8,128)(2,1)S(1)}, bf16[16,2,16,256]{3,2,1,0:T(8,128)(2,1)S(1)}, u32[]{:S(2)}, u32[]{:S(2)}) collective-permute-start(bf16[16,2,16,256]{3,2,1,0:T(8,128)(2,1)S(1)} %bitcast.20), channel_id=1, source_target_pairs={{0,4},{4,0},{8,12},{12,8},{1,5},{5,1},{9,13},{13,9},{2,6},{6,2},{1... | collective-permute-start | bytes 786440 | tf_op jit(solution)/shard_map/ppermute | solution.py:41
  53.8 9.9 %collective-permute-start.5 = (bf16[8,2,16,256]{3,2,1,0:T(8,128)(2,1)S(1)}, bf16[8,2,16,256]{3,2,1,0:T(8,128)(2,1)S(1)}, u32[]{:S(2)}, u32[]{:S(2)}) collective-permute-start(bf16[8,2,16,256]{3,2,1,0:T(8,128)(2,1)S(1)} %collective-permute-done.4.refs_4_), channel_id=1, source_target_pairs={{0,4},{4,0},{8,12},{12,8},{1,5},{5,1},{9,13},{13,9},{2,6},{6,2},{1... | collective-permute-start | bytes 393224 | tf_op jit(solution)/shard_map/ppermute | solution.py:41
  56.7 7.0 %collective-permute-start.7 = (bf16[8,2,16,256]{3,2,1,0:T(8,128)(2,1)S(1)}, bf16[8,2,16,256]{3,2,1,0:T(8,128)(2,1)S(1)}, u32[]{:S(2)}, u32[]{:S(2)}) collective-permute-start(bf16[8,2,16,256]{3,2,1,0:T(8,128)(2,1)S(1)} %collective-permute-done.6.refs_5_), channel_id=1, source_target_pairs={{0,4},{4,0},{8,12},{12,8},{1,5},{5,1},{9,13},{13,9},{2,6},{6,2},{1... | collective-permute-start | bytes 393224 | tf_op jit(solution)/shard_map/ppermute | solution.py:41
  59.2 1.6 %copy-start = (bf16[1,8192,128]{2,1,0:T(8,128)(2,1)S(1)}, bf16[1,8192,128]{2,1,0:T(8,128)(2,1)}, u32[]{:S(2)}) copy-start(bf16[1,8192,128]{2,1,0:T(8,128)(2,1)} %param.7) | copy-start | bytes 6291460
  60.8 1.6 %copy-start.2 = (bf16[1,8192,128]{2,1,0:T(8,128)(2,1)S(1)}, bf16[1,8192,128]{2,1,0:T(8,128)(2,1)}, u32[]{:S(2)}) copy-start(bf16[1,8192,128]{2,1,0:T(8,128)(2,1)} %param.8) | copy-start | bytes 6291460
  63.6 20.3 %copy-start.3 = (bf16[128,2048]{1,0:T(8,128)(2,1)}, bf16[128,2048]{1,0:T(8,128)(2,1)S(1)}, u32[]{:S(2)}) copy-start(bf16[128,2048]{1,0:T(8,128)(2,1)S(1)} %collective-permute-done.1.a2) | copy-start | bytes 1572868
  63.7 20.3 %copy-start.5 = (bf16[128,2048]{1,0:T(8,128)(2,1)}, bf16[128,2048]{1,0:T(8,128)(2,1)S(1)}, u32[]{:S(2)}) copy-start(bf16[128,2048]{1,0:T(8,128)(2,1)S(1)} %collective-permute-done.2.a3) | copy-start | bytes 1572868
  66.2 9.5 %all-to-all-start.1 = ((bf16[4,128,256]{2,1,0:T(8,128)(2,1)}), bf16[4,128,256]{2,1,0:T(8,128)(2,1)S(1)}, u32[]{:S(2)}, u32[]{:S(2)}) async-start(bf16[4,128,256]{2,1,0:T(8,128)(2,1)} %shard_map.79), calls=%async_computation.1 | async-start | bytes 524288 | tf_op jit(solution)/shard_map/all_to_all | solution.py:309
  85.1 15.0 %copy-start.4 = (bf16[128,2048]{1,0:T(8,128)(2,1)S(1)}, bf16[128,2048]{1,0:T(8,128)(2,1)}, u32[]{:S(2)}) copy-start(bf16[128,2048]{1,0:T(8,128)(2,1)} %copy-done.3) | copy-start | bytes 1572868
  85.1 15.0 %copy-start.6 = (bf16[128,2048]{1,0:T(8,128)(2,1)S(1)}, bf16[128,2048]{1,0:T(8,128)(2,1)}, u32[]{:S(2)}) copy-start(bf16[128,2048]{1,0:T(8,128)(2,1)} %copy-done.5) | copy-start | bytes 1572868
  85.1 7.2 %collective-permute-start.8 = (bf16[16,2,16,256]{3,2,1,0:T(8,128)(2,1)S(1)}, bf16[16,2,16,256]{3,2,1,0:T(8,128)(2,1)S(1)}, u32[]{:S(2)}, u32[]{:S(2)}) collective-permute-start(bf16[16,2,16,256]{3,2,1,0:T(8,128)(2,1)S(1)} %get-tuple-element.33), channel_id=1, source_target_pairs={{0,4},{4,0},{8,12},{12,8},{1,5},{5,1},{9,13},{13,9},{2,6},{6,2},{1... | collective-permute-start | bytes 786440 | tf_op jit(solution)/shard_map/ppermute | solution.py:41
  88.4 12.5 %collective-permute-start.9 = (bf16[16,2,16,256]{3,2,1,0:T(8,128)(2,1)S(1)}, bf16[16,2,16,256]{3,2,1,0:T(8,128)(2,1)S(1)}, u32[]{:S(2)}, u32[]{:S(2)}) collective-permute-start(bf16[16,2,16,256]{3,2,1,0:T(8,128)(2,1)S(1)} %get-tuple-element.39), channel_id=1, source_target_pairs={{0,4},{4,0},{8,12},{12,8},{1,5},{5,1},{9,13},{13,9},{2,6},{6,2},{1... | collective-permute-start | bytes 786440 | tf_op jit(solution)/shard_map/ppermute | solution.py:41
  91.7 10.1 %copy-start.7 = (bf16[64,2048]{1,0:T(8,128)(2,1)}, bf16[64,2048]{1,0:T(8,128)(2,1)S(1)}, u32[]{:S(2)}) copy-start(bf16[64,2048]{1,0:T(8,128)(2,1)S(1)} %get-tuple-element.38.x0) | copy-start | bytes 786436
  91.7 10.1 %copy-start.13 = (bf16[64,2048]{1,0:T(8,128)(2,1)}, bf16[64,2048]{1,0:T(8,128)(2,1)S(1)}, u32[]{:S(2)}) copy-start(bf16[64,2048]{1,0:T(8,128)(2,1)S(1)} %get-tuple-element.45) | copy-start | bytes 786436
  92.5 41.1 %copy-start.1 = (bf16[1,8192,128]{2,1,0:T(8,128)(2,1)S(1)}, bf16[1,8192,128]{2,1,0:T(8,128)(2,1)}, u32[]{:S(2)}) copy-start(bf16[1,8192,128]{2,1,0:T(8,128)(2,1)} %param.7) | copy-start | bytes 6291460
  92.5 8.5 %collective-permute-start.10 = (bf16[16,2,16,256]{3,2,1,0:T(8,128)(2,1)S(1)}, bf16[16,2,16,256]{3,2,1,0:T(8,128)(2,1)S(1)}, u32[]{:S(2)}, u32[]{:S(2)}) collective-permute-start(bf16[16,2,16,256]{3,2,1,0:T(8,128)(2,1)S(1)} %add_convert_fusion.1), channel_id=1, source_target_pairs={{0,12},{4,8},{8,4},{12,0},{1,13},{5,9},{9,5},{13,1},{2,14},{6,10},... | collective-permute-start | bytes 786440 | tf_op jit(solution)/shard_map/ppermute | solution.py:41
  95.4 7.4 %collective-permute-start.11 = (bf16[64,2048]{1,0:T(8,128)(2,1)S(1)}, bf16[64,2048]{1,0:T(8,128)(2,1)S(1)}, u32[]{:S(2)}, u32[]{:S(2)}) collective-permute-start(bf16[64,2048]{1,0:T(8,128)(2,1)S(1)} %get-tuple-element.42), channel_id=1, source_target_pairs={{0,1},{1,0},{2,3},{3,2},{4,5},{5,4},{6,7},{7,6},{8,9},{9,8},{10,11... | collective-permute-start | bytes 786440 | tf_op jit(solution)/shard_map/ppermute | solution.py:41
  97.6 8.3 %collective-permute-start.12 = (bf16[64,2048]{1,0:T(8,128)(2,1)S(1)}, bf16[64,2048]{1,0:T(8,128)(2,1)S(1)}, u32[]{:S(2)}, u32[]{:S(2)}) collective-permute-start(bf16[64,2048]{1,0:T(8,128)(2,1)S(1)} %get-tuple-element.43), channel_id=1, source_target_pairs={{0,3},{1,2},{2,1},{3,0},{4,7},{5,6},{6,5},{7,4},{8,11},{9,10},{10,... | collective-permute-start | bytes 786440 | tf_op jit(solution)/shard_map/ppermute | solution.py:41
  105.9 0.7 copy-start.9
  106.6 38.5 %all-to-all-start.3 = ((bf16[32,16,256]{2,1,0:T(8,128)(2,1)}), bf16[32,16,256]{2,1,0:T(8,128)(2,1)S(1)}, u32[]{:S(2)}, u32[]{:S(2)}) async-start(bf16[32,16,256]{2,1,0:T(8,128)(2,1)} %bitcast.12), calls=%async_computation.3 | async-start | bytes 524288 | tf_op jit(solution)/shard_map/all_to_all | solution.py:34
  122.3 11.3 %collective-permute-start.13 = (bf16[64,2048]{1,0:T(8,128)(2,1)}, bf16[64,2048]{1,0:T(8,128)(2,1)S(1)}, u32[]{:S(2)}, u32[]{:S(2)}) collective-permute-start(bf16[64,2048]{1,0:T(8,128)(2,1)} %copy-done.13), channel_id=1, source_target_pairs={{0,2},{1,3},{2,0},{3,1},{4,6},{5,7},{6,4},{7,5},{8,10},{9,11},{10,... | collective-permute-start | bytes 786440 | tf_op jit(solution)/shard_map/ppermute | solution.py:41
  133.6 1.0 copy-start.8
  134.5 0.9 copy-start.10
